TPU v7x, 32 devices: a whole 2x2x4 slice. The times are simulated.
32 devices in a mesh: ctx: 16 (over z, x, core), dp: 2 (over y).
Axes of the slice: x: 2, y: 2, z: 4, core: 2. Of those that a mesh axis runs over, the one named last changes fastest.
Arguments:
- proj: bfloat16 [2, 2048, 1536], P('dp', 'ctx'), may hold values from -6 to 6
- short_filter: float32 [3, 1536], replicated, may hold values from -2.5 to 2.5
- long_filter: float32 [512, 2048], P('ctx'), may hold values from -1 to 1
- w_out: bfloat16 [512, 2048], P('ctx'), may hold values from -0.25 to 0.25
- dout: bfloat16 [2, 2048, 2048], P('dp', 'ctx'), may hold values from -6 to 6
- lengths: int32 [2], replicated, may hold values from 1024 to 2048, as said below
- counts: int32 [2], replicated, may hold values from 256 to 2048
Outputs:
- output: bfloat16 [2, 2048, 2048], P('dp', 'ctx')
- d_proj: bfloat16 [2, 2048, 1536], P('dp', 'ctx')
- d_wout: float32 [512, 2048], P('ctx')
- d_filter: float32 [512, 2048], P('ctx')
Inputs may be any that keep to these rules, and one draw needn't show every extreme that they name: `lengths`: at least one sequence has the full length 2048.
All inputs are finite; a program needn't handle non-finite values.
Results may differ from a plain program's by a relative error of at most 0.0075.
Values may be sent and summed in bfloat16 or wider, within the bound.
No kernel may reach another device: no remote copies, remote signals or barrier semaphores. Data moves between devices by JAX's collectives and lax.ppermute only.
A program may use at most 64 MiB of HBM per device.

v0:
```python
import functools
import math

import jax
import jax.numpy as jnp
import ml_dtypes
import numpy as np
from jax import lax
from jax.experimental import pallas as pl
from jax.experimental.pallas import tpu as pltpu
from jax.sharding import Mesh
from jax.sharding import PartitionSpec as P

F32 = jnp.float32
BF16 = jnp.bfloat16
LANES = 128
VMEM = pl.BlockSpec(memory_space=pltpu.VMEM)
SMEM = pl.BlockSpec(memory_space=pltpu.SMEM)


def split_bf16(values):
    high = values.astype(ml_dtypes.bfloat16)
    low = (values - high.astype(np.float64)).astype(ml_dtypes.bfloat16)
    return high, low


def fft_tables(blocks):
    size = 2 * blocks * LANES
    k1 = np.arange(blocks + 1)[:, None]
    lane = np.arange(LANES)
    angle = -2.0 * np.pi * (k1 * lane[None, :] % size) / size
    twist = np.stack([np.cos(angle), np.sin(angle)]).astype(np.float32)
    inner = -2.0 * np.pi * (lane[:, None] * lane[None, :] % LANES) / LANES
    cos, sin = np.cos(inner), np.sin(inner)
    matrix = np.block([[cos, sin], [-sin, cos]])
    high, low = split_bf16(matrix)
    return jnp.asarray(twist), jnp.asarray(high), jnp.asarray(low)


def real_fft(values):
    half = len(values)
    if half == 1:
        return [(values[0], None), (values[0], None)]
    even, odd = real_fft(values[0::2]), real_fft(values[1::2])
    out = [None] * (half + 1)
    out[0] = (even[0][0] + odd[0][0], None)
    out[half] = (even[0][0] - odd[0][0], None)
    out[half // 2] = (even[half // 2][0], -odd[half // 2][0])
    for k in range(1, half // 2):
        cos, sin = math.cos(math.pi * k / half), -math.sin(math.pi * k / half)
        (e_re, e_im), (o_re, o_im) = even[k], odd[k]
        t_re = o_re * cos - o_im * sin
        t_im = o_re * sin + o_im * cos
        out[k] = (e_re + t_re, e_im + t_im)
        out[half - k] = (e_re - t_re, t_im - e_im)
    return out


def real_ifft(spectrum):
    half = len(spectrum) - 1
    if half == 1:
        return [spectrum[0][0] + spectrum[1][0]]
    even = [None] * (half // 2 + 1)
    odd = [None] * (half // 2 + 1)
    even[0] = (spectrum[0][0] + spectrum[half][0], None)
    odd[0] = (spectrum[0][0] - spectrum[half][0], None)
    even[half // 2] = (2.0 * spectrum[half // 2][0], None)
    odd[half // 2] = (-2.0 * spectrum[half // 2][1], None)
    for k in range(1, half // 2):
        cos, sin = math.cos(math.pi * k / half), math.sin(math.pi * k / half)
        (a_re, a_im), (b_re, b_im) = spectrum[k], spectrum[half - k]
        even[k] = (a_re + b_re, a_im - b_im)
        d_re, d_im = a_re - b_re, a_im + b_im
        odd[k] = (d_re * cos - d_im * sin, d_re * sin + d_im * cos)
    out = [None] * half
    out[0::2] = real_ifft(even)
    out[1::2] = real_ifft(odd)
    return out


def split_dot(left, high, low, transposed):
    dims = (((1,), (1 if transposed else 0,)), ((), ()))
    dot = functools.partial(lax.dot_general, dimension_numbers=dims, preferred_element_type=F32)
    left_high = left.astype(BF16)
    left_low = (left - left_high.astype(F32)).astype(BF16)
    return dot(left_high, high) + (dot(left_low, high) + dot(left_high, low))


def to_spectrum(load, blocks, chans, twist, high, low, work):
    for first in range(0, chans, 8):
        rows = slice(first, first + 8)
        freqs = real_fft([load(n1, rows) for n1 in range(blocks)])
        for k1, (re, im) in enumerate(freqs):
            at = slice(k1 * chans + first, k1 * chans + first + 8)
            if k1 == 0:
                work[at, :LANES] = re
                work[at, LANES:] = jnp.zeros_like(re)
                continue
            cos, sin = twist[0, k1 : k1 + 1, :], twist[1, k1 : k1 + 1, :]
            if im is None:
                work[at, :LANES] = re * cos
                work[at, LANES:] = re * sin
            else:
                work[at, :LANES] = re * cos - im * sin
                work[at, LANES:] = re * sin + im * cos
    return split_dot(work[...], high[...], low[...], False)


def from_spectrum(spectrum, blocks, chans, twist, high, low, work, store):
    scale = 1.0 / (2 * blocks * LANES)
    work[...] = split_dot(spectrum, high[...], low[...], True)
    for first in range(0, chans, 8):
        rows = slice(first, first + 8)
        freqs = []
        for k1 in range(blocks + 1):
            at = slice(k1 * chans + first, k1 * chans + first + 8)
            re, im = work[at, :LANES] * scale, work[at, LANES:] * scale
            cos, sin = twist[0, k1 : k1 + 1, :], twist[1, k1 : k1 + 1, :]
            if k1 == 0:
                freqs.append((re, None))
            elif k1 == blocks:
                freqs.append((re * cos + im * sin, None))
            else:
                freqs.append((re * cos + im * sin, im * cos - re * sin))
        for n1, value in enumerate(real_ifft(freqs)):
            store(n1, rows, value)


def times(a, b):
    a_re, a_im, b_re, b_im = a[:, :LANES], a[:, LANES:], b[:, :LANES], b[:, LANES:]
    return jnp.concatenate([a_re * b_re - a_im * b_im, a_re * b_im + a_im * b_re], axis=1)


def conj_times(a, b):
    a_re, a_im, b_re, b_im = a[:, :LANES], a[:, LANES:], b[:, :LANES], b[:, LANES:]
    return jnp.concatenate([a_re * b_re + a_im * b_im, a_re * b_im - a_im * b_re], axis=1)


def filter_kernel(filt, twist, high, low, spec, work, *, blocks, chans):
    def load(n1, rows):
        return filt[rows, n1 * LANES : (n1 + 1) * LANES]

    spec[...] = to_spectrum(load, blocks, chans, twist, high, low, work)


def forward_kernel(
    gated, filt_spec, twist, high, low, long_out, gated_spec, work, signal, *, blocks, chans
):
    for n1 in range(blocks):
        signal[n1] = gated[n1].astype(F32)

    def load(n1, rows):
        return signal[n1, rows, :]

    spec = to_spectrum(load, blocks, chans, twist, high, low, work)
    gated_spec[...] = spec

    def store(n1, rows, value):
        signal[n1, rows, :] = value

    from_spectrum(times(spec, filt_spec[...]), blocks, chans, twist, high, low, work, store)
    for n1 in range(blocks):
        long_out[n1] = signal[n1].astype(BF16)


def backward_kernel(
    d_long,
    filt_spec,
    gated_spec,
    twist,
    high,
    low,
    d_gated,
    d_filter,
    work,
    signal,
    held,
    *,
    blocks,
    chans,
    scale,
):
    for n1 in range(blocks):
        signal[n1] = d_long[n1].astype(F32)

    def load(n1, rows):
        return signal[n1, rows, :]

    held[...] = to_spectrum(load, blocks, chans, twist, high, low, work)

    def store(n1, rows, value):
        signal[n1, rows, :] = value

    spec = conj_times(filt_spec[...], held[...])
    from_spectrum(spec, blocks, chans, twist, high, low, work, store)
    for n1 in range(blocks):
        d_gated[n1] = signal[n1].astype(BF16)
    spec = conj_times(gated_spec[...], held[...])
    from_spectrum(spec, blocks, chans, twist, high, low, work, store)
    for n1 in range(blocks):
        d_filter[:, n1 * LANES : (n1 + 1) * LANES] = (signal[n1] * scale).astype(BF16)


def prep_kernel(ints, proj, earlier, taps, gated_t, query_t, key_t, value_t, *, width):
    rows = proj.shape[0]
    start, length = ints[2], ints[3]
    position = start + lax.broadcasted_iota(jnp.int32, (rows, 1), 0)
    keep = position < length
    row = lax.broadcasted_iota(jnp.int32, (rows, 1), 0)
    streams = []
    for stream in range(3):
        cols = slice(stream * width, (stream + 1) * width)
        masked = jnp.where(keep, proj[:, cols].astype(F32), 0.0)
        past = earlier[:, cols].astype(F32)
        mixed = taps[0:1, cols] * masked
        for tap in range(1, 3):
            shifted = pltpu.roll(masked, tap, 0)
            for r in range(tap):
                shifted = jnp.where(row == r, past[2 - tap + r : 3 - tap + r, :], shifted)
            mixed = mixed + taps[tap : tap + 1, cols] * shifted
        streams.append(mixed)
    gated_t[...] = (streams[1] * streams[2]).T.astype(BF16)
    query_t[...] = streams[0].T
    key_t[...] = streams[1].T
    value_t[...] = streams[2].T


def natural_row(ints, rel_h, rel_c, line, shape):
    h = (ints[0] + rel_h) % 2
    c = (ints[1] + rel_c) % 2
    lines, chans, line_first = shape
    place = (line * 2 + h) * 2 + c if line_first else (h * lines + line) * 2 + c
    return pl.multiple_of(place * chans, chans)


PIECES = ((0, 0), (1, 0), (0, 1), (1, 1))


def piece_rows(refs, piece):
    near, over, across = refs
    if piece == 0:
        return near[...]
    if piece == 1:
        return over[...]
    return across[piece - 2]


def d_long_kernel(
    ints, floats, dout, near, over, across, query_t, cot, d_product_t, d_long_t, *, shape
):
    lines, chans, _ = shape
    rows = dout.shape[0]
    position = ints[2] + lax.broadcasted_iota(jnp.int32, (rows, 1), 0)
    mask = jnp.where(position < ints[3], 1.0, 0.0)
    cot[...] = (dout[...].astype(F32) * mask * floats[0]).astype(BF16)
    for piece, (rel_h, rel_c) in enumerate(PIECES):
        got = lax.dot_general(
            piece_rows((near, over, across), piece),
            cot[...],
            (((1,), (1,)), ((), ())),
            preferred_element_type=F32,
        )
        for line in range(lines):
            at = natural_row(ints, rel_h, rel_c, line, shape)
            d_product_t[pl.ds(at, chans), :] = got[line * chans : (line + 1) * chans]
    d_long_t[...] = (d_product_t[...] * query_t[...]).astype(BF16)


def partial_kernel(
    ints, long_t, query_t, cot, product, send, stay, product_t, *, shape, scale, tile
):
    lines, chans, _ = shape
    product_t[...] = query_t[...] * long_t[...].astype(F32)
    for piece, (rel_h, rel_c) in enumerate(PIECES):
        left = jnp.concatenate(
            [
                product_t[pl.ds(natural_row(ints, rel_h, rel_c, line, shape), chans), :]
                for line in range(lines)
            ],
            axis=0,
        )
        product[piece] = left.T.astype(BF16)
        left = left.astype(BF16)
        for first in range(0, cot.shape[1], tile):
            cols = slice(first, first + tile)
            got = jnp.dot(left, cot[:, cols], preferred_element_type=F32) * scale
            if rel_c:
                send[rel_h, :, cols] = got.astype(BF16)
            else:
                stay[rel_h, :, cols] = got


def output_kernel(product, near, over, across, out, *, tile):
    for first in range(0, out.shape[1], tile):
        cols = slice(first, first + tile)
        total = jnp.dot(product[0], near[:, cols], preferred_element_type=F32)
        total += jnp.dot(product[1], over[:, cols], preferred_element_type=F32)
        total += jnp.dot(product[2], across[0, :, cols], preferred_element_type=F32)
        total += jnp.dot(product[3], across[1, :, cols], preferred_element_type=F32)
        out[:, cols] = total.astype(BF16)


def mixed_grad_kernel(d_product_t, long_t, d_gated_t, key_t, value_t, d_mixed, *, width):
    d_gated = d_gated_t[...].astype(F32)
    d_mixed[:, :width] = (d_product_t[...] * long_t[...].astype(F32)).T
    d_mixed[:, width : 2 * width] = (d_gated * value_t[...]).T
    d_mixed[:, 2 * width :] = (d_gated * key_t[...]).T


def proj_grad_kernel(ints, d_mixed, later, taps, d_proj):
    rows = d_mixed.shape[0]
    row = lax.broadcasted_iota(jnp.int32, (rows, 1), 0)
    keep = ints[2] + row < ints[3]
    total = taps[0:1, :] * d_mixed[...]
    for tap in range(1, 3):
        shifted = pltpu.roll(d_mixed[...], rows - tap, 0)
        for r in range(tap):
            shifted = jnp.where(row == rows - tap + r, later[r : r + 1, :], shifted)
        total = total + taps[tap : tap + 1, :] * shifted
    d_proj[...] = jnp.where(keep, total, 0.0).astype(BF16)


def call(kernel, outs, specs, scratch=(), flops=0, moved=1 << 20):
    return pl.pallas_call(
        kernel,
        out_shape=[jax.ShapeDtypeStruct(s, d) for s, d in outs],
        in_specs=specs,
        out_specs=[VMEM] * len(outs),
        scratch_shapes=list(scratch),
        compiler_params=pltpu.CompilerParams(vmem_limit_bytes=40 << 20),
        cost_estimate=pl.CostEstimate(flops=flops, bytes_accessed=moved, transcendentals=0),
    )


CTX = None
SWAP = ((0, 1), (1, 0))


def swap(block, axis):
    return lax.ppermute(block, axis, SWAP)


def dp_sum(block):
    if lax.axis_size("dp") == 2:
        return block.astype(F32) + swap(block, "dp").astype(F32)
    return lax.psum(block, "dp").astype(F32)


def per_device(axes, proj, short_filter, long_filter, w_out, dout, lengths, counts):
    rows, width = proj.shape[1], proj.shape[2] // 3
    chans, seq_len = long_filter.shape
    features = w_out.shape[1]
    batch = lengths.shape[0]
    ctx_size = seq_len // rows
    lines = lax.axis_size("l")
    shape = (lines, chans, axes[0] == "l")
    grad_scale = 1.0 / math.sqrt(batch * seq_len)
    here = lax.axis_index(axes)
    samples = batch // lax.axis_size("dp")
    assert samples == 1
    picked = jnp.arange(batch, dtype=jnp.int32) == lax.axis_index("dp")
    length_here = jnp.sum(jnp.where(picked, lengths, 0))
    count_float = counts.astype(F32)
    weight_here = jnp.sum(jnp.where(picked, count_float, 0.0)) * batch / jnp.sum(count_float)
    ints = jnp.stack(
        [lax.axis_index("h"), lax.axis_index("c"), here * rows, length_here]
    ).astype(jnp.int32)
    floats = weight_here.reshape(1)

    near = lax.all_to_all(
        jnp.broadcast_to(w_out[None], (lines,) + w_out.shape), "l", 0, 0, tiled=True
    ).reshape(lines * chans, features)
    over = swap(near, "h")
    across = swap(jnp.stack([near, over]), "c")

    tail = proj[0, rows - 2 :]
    tail_at = here * rows + rows - 2 + jnp.arange(2, dtype=jnp.int32)
    tail = jnp.where((tail_at < length_here)[:, None], tail, jnp.zeros_like(tail))
    route = [(i, i + 1) for i in range(ctx_size - 1)]
    earlier = lax.ppermute(tail, axes, route)
    flat = (width, rows)
    gated_t, query_t, key_t, value_t = call(
        functools.partial(prep_kernel, width=width),
        [(flat, BF16), (flat, F32), (flat, F32), (flat, F32)],
        [SMEM] + [VMEM] * 3,
        flops=1 << 20,
    )(ints, proj[0], earlier, short_filter)

    def exchange(block):
        return lax.all_to_all(block, axes, 0, 0, tiled=True)

    blocked = (ctx_size, chans, rows)
    tables = fft_tables(ctx_size)
    spec_shape = ((ctx_size + 1) * chans, 2 * LANES)
    sizes = {"blocks": ctx_size, "chans": chans}
    work = pltpu.VMEM(spec_shape, F32)
    signal = pltpu.VMEM(blocked, F32)
    fft_flops = 6 * spec_shape[0] * 2 * LANES * 2 * LANES
    (filt_spec,) = call(
        functools.partial(filter_kernel, **sizes),
        [(spec_shape, F32)],
        [VMEM] * 4,
        [work],
        flops=fft_flops,
    )(long_filter, *tables)
    gated_cols = exchange(gated_t.reshape(blocked))
    long_cols, gated_spec = call(
        functools.partial(forward_kernel, **sizes),
        [(blocked, BF16), (spec_shape, F32)],
        [VMEM] * 5,
        [work, signal],
        flops=2 * fft_flops,
    )(gated_cols, filt_spec, *tables)
    long_t = exchange(long_cols).reshape(flat)

    cot, d_product_t, d_long_t = call(
        functools.partial(d_long_kernel, shape=shape),
        [((rows, features), BF16), (flat, F32), (flat, BF16)],
        [SMEM, SMEM] + [VMEM] * 5,
        flops=2 * rows * width * features,
        moved=4 << 20,
    )(ints, floats, dout[0], near, over, across, query_t)
    d_long_cols = exchange(d_long_t.reshape(blocked))
    d_gated_cols, filter_part = call(
        functools.partial(backward_kernel, scale=grad_scale, **sizes),
        [(blocked, BF16), ((chans, seq_len), BF16)],
        [VMEM] * 6,
        [work, signal, work],
        flops=3 * fft_flops,
    )(d_long_cols, filt_spec, gated_spec, *tables)
    d_gated_t = exchange(d_gated_cols).reshape(flat)
    d_filter = dp_sum(filter_part)

    part = (2, lines * chans, features)
    product, send, stay = call(
        functools.partial(partial_kernel, shape=shape, scale=grad_scale, tile=512),
        [((4, rows, lines * chans), BF16), (part, BF16), (part, F32)],
        [SMEM] + [VMEM] * 3,
        [pltpu.VMEM(flat, F32)],
        flops=2 * rows * width * features,
        moved=4 << 20,
    )(ints, long_t, query_t, cot)
    pair = stay + swap(send, "c").astype(F32)
    quad = pair[0] + swap(pair[1].astype(BF16), "h").astype(F32)
    row_sums = jnp.sum(
        lax.all_to_all(
            quad.astype(BF16).reshape(lines, chans, features), "l", 0, 0, tiled=True
        ).astype(F32),
        axis=0,
    )
    d_wout = dp_sum(row_sums.astype(BF16))

    (output,) = call(
        functools.partial(output_kernel, tile=512),
        [((rows, features), BF16)],
        [VMEM] * 4,
        flops=2 * rows * width * features,
        moved=4 << 20,
    )(product, near, over, across.reshape(2, lines * chans, features))

    (d_mixed,) = call(
        functools.partial(mixed_grad_kernel, width=width),
        [((rows, 3 * width), F32)],
        [VMEM] * 5,
        flops=1 << 20,
    )(d_product_t, long_t, d_gated_t, key_t, value_t)
    later = lax.ppermute(d_mixed[:2], axes, [(j, i) for i, j in route])
    (d_proj,) = call(
        proj_grad_kernel,
        [((rows, 3 * width), BF16)],
        [SMEM] + [VMEM] * 3,
        flops=1 << 20,
    )(ints, d_mixed, later, short_filter)
    return output[None], d_proj[None], d_wout, d_filter


def solution(mesh):
    ctx, dp = mesh.shape["ctx"], mesh.shape["dp"]
    if ctx == 16:
        axes, dims = ("l", "h", "c"), (4, 2, 2)
    else:
        axes, dims = ("h", "l", "c"), (2, ctx // 4, 2)
    fine = Mesh(mesh.devices.reshape(dims + (dp,)), axes + ("dp",))
    placed = (
        P("dp", axes, None),
        P(),
        P(axes, None),
        P(axes, None),
        P("dp", axes, None),
        P(),
        P(),
    )
    return jax.shard_map(
        functools.partial(per_device, axes),
        mesh=fine,
        in_specs=placed,
        out_specs=(P("dp", axes, None), P("dp", axes, None), P(axes, None), P(axes, None)),
        check_vma=False,
    )
```

profile of v0, /device:TPU:0, one launch (start us, length us, event | category | flops | bytes accessed | tf_op | source)
XLA Modules:
  0.0 135.1 jit_solution(16410982219392577066)
XLA Ops:
  0.7 1.0 broadcast_in_dim.36
  1.7 0.0 copy-start.12
  1.7 0.0 copy-start.20
  1.7 20.7 %all_to_all.30 = bf16[4,32,2048]{2,1,0:T(8,128)(2,1)S(1)} all-to-all(bf16[4,32,2048]{2,1,0:T(8,128)(2,1)S(1)} %broadcast_in_dim.36), channel_id=1, replica_groups=mesh['l'=4,'h'=2,'c'=2,'dp'=2] {'l'}, dimensions={0} | all-to-all | bytes 1048576 | tf_op jit(solution)/shard_map/all_to_all | solution.py:370
  22.4 1.5 %collective-permute-start.1 = (bf16[128,2048]{1,0:T(8,128)(2,1)S(1)}, bf16[128,2048]{1,0:T(8,128)(2,1)S(1)}, u32[]{:S(2)}, u32[]{:S(2)}) collective-permute-start(bf16[128,2048]{1,0:T(8,128)(2,1)S(1)} %bitcast.27), channel_id=1, source_target_pairs={{0,4},{4,0},{1,5},{5,1},{2,6},{6,2},{3,7},{7,3},{8,12},{12,8},{9,1... | collective-permute-start | bytes 1572872 | tf_op jit(solution)/shard_map/ppermute | solution.py:340
  23.9 1.3 fusion.3
  25.2 0.7 add_compare_fusion
  25.9 9.1 %collective-permute-done.1.over = bf16[128,2048]{1,0:T(8,128)(2,1)S(1)} collective-permute-done((bf16[128,2048]{1,0:T(8,128)(2,1)S(1)}, bf16[128,2048]{1,0:T(8,128)(2,1)S(1)}, u32[]{:S(2)}, u32[]{:S(2)}) %collective-permute-start.1) | collective-permute-done | bytes 524320 | tf_op jit(solution)/shard_map/ppermute | solution.py:340
  35.0 1.1 pad_maximum_fusion
  36.0 0.0 collective-permute-start.2
  36.0 0.1 broadcast_select_fusion
  36.1 2.4 %collective-permute-start = (bf16[2,1536]{1,0:T(2,128)(2,1)S(1)}, bf16[2,1536]{1,0:T(2,128)(2,1)S(1)}, u32[]{:S(2)}, u32[]{:S(2)}) collective-permute-start(bf16[2,1536]{1,0:T(2,128)(2,1)S(1)} %broadcast_select_fusion), channel_id=1, source_target_pairs={{0,2},{2,4},{4,6},{6,8},{8,10},{10,12},{12,14},{14,16},{16,18},{18... | collective-permute-start | bytes 18440 | tf_op jit(solution)/shard_map/ppermute | solution.py:380
  38.5 0.7 pad_add_fusion.ints
  39.2 0.1 collective-permute-done.earlier
  39.3 1.1 shard_map.129
  40.4 0.0 copy-start.2
  40.4 0.7 copy-done.2
  41.1 0.7 copy-done.9
  41.8 0.7 copy-done.18
  42.5 0.7 copy-done.4
  43.2 6.3 %all-to-all-start = ((bf16[16,32,128]{2,1,0:T(8,128)(2,1)}), bf16[16,32,128]{2,1,0:T(8,128)(2,1)}, u32[]{:S(2)}, u32[]{:S(2)}) async-start(bf16[16,32,128]{2,1,0:T(8,128)(2,1)} %bitcast.38), calls=%async_computation | async-start | bytes 262144 | tf_op jit(solution)/shard_map/all_to_all | solution.py:390
  49.6 0.0 copy-start.8
  49.6 0.9 copy-done.8
  50.5 0.9 copy-done.13
  51.4 0.5 shard_map.130.filt_spec
  51.9 5.6 %all-to-all-done.gated = bf16[16,32,128]{2,1,0:T(8,128)(2,1)} async-done(((bf16[16,32,128]{2,1,0:T(8,128)(2,1)}), bf16[16,32,128]{2,1,0:T(8,128)(2,1)}, u32[]{:S(2)}, u32[]{:S(2)}) %all-to-all-start) | async-done | bytes 131104 | tf_op jit(solution)/shard_map/all_to_all | solution.py:390
  57.5 2.1 %shard_map.131 = (bf16[16,32,128]{2,1,0:T(8,128)(2,1)S(1)}, f32[544,256]{1,0:T(8,128)S(1)}) custom-call(bf16[16,32,128]{2,1,0:T(8,128)(2,1)} %all-to-all-done.gated, f32[544,256]{1,0:T(8,128)S(1)} %shard_map.130.filt_spec, f32[2,17,128]{2,1,0:T(8,128)S(1)} %copy-done.20, bf16[256,256]{1,0:T(8,128)(2,1)S(1)} %copy-done.13, bf16[256,256]{1,0:T(8,128)(2,1)S(1)} %copy-done.12), custom_call_target="tpu_custom_call" | custom-call | flops 427819008 | bytes 1048576 | tf_op jit(solution)/shard_map/pallas_call | solution.py:407
  59.6 0.6 copy-done.17
  60.3 0.8 copy-done.23
  61.1 3.5 %all-to-all-start.1 = ((bf16[16,32,128]{2,1,0:T(8,128)(2,1)}), bf16[16,32,128]{2,1,0:T(8,128)(2,1)S(1)}, u32[]{:S(2)}, u32[]{:S(2)}) async-start(bf16[16,32,128]{2,1,0:T(8,128)(2,1)} %copy-done.17), calls=%async_computation.1 | async-start | bytes 262144 | tf_op jit(solution)/shard_map/all_to_all | solution.py:390
  64.6 0.6 convert_reduce_fusion
  66.6 0.0 copy-start.10
  66.6 0.9 copy-done.10
  67.5 1.3 shard_map.132
  68.8 0.0 copy-start.6
  68.9 0.7 copy-done.6
  69.5 0.7 copy-done.15
  70.2 0.8 copy-done.21
  71.0 1.5 %all-to-all-done.1 = bf16[16,32,128]{2,1,0:T(8,128)(2,1)S(1)} async-done(((bf16[16,32,128]{2,1,0:T(8,128)(2,1)}), bf16[16,32,128]{2,1,0:T(8,128)(2,1)S(1)}, u32[]{:S(2)}, u32[]{:S(2)}) %all-to-all-start.1) | async-done | bytes 131104 | tf_op jit(solution)/shard_map/all_to_all | solution.py:390
  72.5 0.9 copy-done.11
  73.5 1.0 copy-done.22
  74.5 1.3 shard_map.133
  75.8 0.1 collective-permute-start.4
  75.8 2.6 %collective-permute-done.4 = bf16[2,128,2048]{2,1,0:T(8,128)(2,1)S(1)} collective-permute-done((bf16[2,128,2048]{2,1,0:T(8,128)(2,1)S(1)}, bf16[2,128,2048]{2,1,0:T(8,128)(2,1)S(1)}, u32[]{:S(2)}, u32[]{:S(2)}) %collective-permute-start.4) | collective-permute-done | bytes 1048608 | tf_op jit(solution)/shard_map/ppermute | solution.py:340
  78.5 0.4 convert_add_fusion
  78.9 0.9 fusion.2
  79.8 0.3 collective-permute-start.5
  80.1 15.2 %all_to_all.31.d_long = bf16[16,32,128]{2,1,0:T(8,128)(2,1)S(1)} all-to-all(bf16[16,32,128]{2,1,0:T(8,128)(2,1)S(1)} %bitcast.37), channel_id=1, replica_groups=mesh['l'=4,'h'=2,'c'=2,'dp'=2] {'l','h','c'}, dimensions={0} | all-to-all | bytes 262144 | tf_op jit(solution)/shard_map/all_to_all | solution.py:390
  95.3 1.9 %shard_map.135 = (bf16[16,32,128]{2,1,0:T(8,128)(2,1)}, bf16[32,2048]{1,0:T(8,128)(2,1)S(1)}) custom-call(bf16[16,32,128]{2,1,0:T(8,128)(2,1)S(1)} %all_to_all.31.d_long, f32[544,256]{1,0:T(8,128)S(1)} %shard_map.130.filt_spec, f32[544,256]{1,0:T(8,128)S(1)} %copy-done.24, f32[2,17,128]{2,1,0:T(8,128)S(1)} %copy-done.20, bf16[256,256]{1,0:T(8,128)(2,1)S(1)} %copy-done.14, ...), custom_call_target="tpu_custom_call" | custom-call | flops 641728512 | bytes 1048576 | tf_op jit(solution)/shard_map/pallas_call | solution.py:424
  97.2 4.6 %all-to-all-start.4 = ((bf16[16,32,128]{2,1,0:T(8,128)(2,1)}), bf16[16,32,128]{2,1,0:T(8,128)(2,1)S(1)}, u32[]{:S(2)}, u32[]{:S(2)}) async-start(bf16[16,32,128]{2,1,0:T(8,128)(2,1)} %get-tuple-element.26), calls=%async_computation.4 | async-start | bytes 262144 | tf_op jit(solution)/shard_map/all_to_all | solution.py:390
  101.8 2.3 %fusion.1 = bf16[128,2048]{1,0:T(8,128)(2,1)} fusion(f32[2,128,2048]{2,1,0:T(8,128)} %copy-done.25, bf16[128,2048]{1,0:T(8,128)(2,1)} %collective-permute-done.5), kind=kLoop, calls=%fused_computation.4 | loop fusion | flops 786432 | bytes 2097152 | tf_op jit(solution)/shard_map/convert_element_type | solution.py:447
  104.1 5.6 %all-to-all-done.4 = bf16[16,32,128]{2,1,0:T(8,128)(2,1)S(1)} async-done(((bf16[16,32,128]{2,1,0:T(8,128)(2,1)}), bf16[16,32,128]{2,1,0:T(8,128)(2,1)S(1)}, u32[]{:S(2)}, u32[]{:S(2)}) %all-to-all-start.4) | async-done | bytes 131104 | tf_op jit(solution)/shard_map/all_to_all | solution.py:390
  109.7 4.1 %all-to-all-start.5 = ((bf16[4,32,2048]{2,1,0:T(8,128)(2,1)}), bf16[4,32,2048]{2,1,0:T(8,128)(2,1)}, u32[]{:S(2)}, u32[]{:S(2)}) async-start(bf16[4,32,2048]{2,1,0:T(8,128)(2,1)} %bitcast.39), calls=%async_computation.5 | async-start | bytes 1048576 | tf_op jit(solution)/shard_map/all_to_all | solution.py:446
  113.9 1.6 %collective-permute-start.7 = (bf16[32,2048]{1,0:T(8,128)(2,1)S(1)}, bf16[32,2048]{1,0:T(8,128)(2,1)}, u32[]{:S(2)}, u32[]{:S(2)}) collective-permute-start(bf16[32,2048]{1,0:T(8,128)(2,1)S(1)} %get-tuple-element.31), channel_id=1, source_target_pairs={{0,1},{1,0},{2,3},{3,2},{4,5},{5,4},{6,7},{7,6},{8,9},{9,8},{10,11... | collective-permute-start | bytes 393224 | tf_op jit(solution)/shard_map/ppermute | solution.py:340
  115.4 1.5 %shard_map.134 = bf16[128,2048]{1,0:T(8,128)(2,1)} custom-call(bf16[4,128,128]{2,1,0:T(8,128)(2,1)S(1)} %get-tuple-element.22.product, bf16[128,2048]{1,0:T(8,128)(2,1)S(1)} %bitcast.30, bf16[128,2048]{1,0:T(8,128)(2,1)S(1)} %collective-permute-done.1.over, bf16[2,128,2048]{2,1,0:T(8,128)(2,1)S(1)} %collective-permute-done.2.across), custom_call_target="tpu_custom_call" | custom-call | flops 268435456 | bytes 4194304 | tf_op jit(solution)/shard_map/pallas_call | solution.py:453
  116.9 0.3 shard_map.136.d_mixed
  117.2 1.3 collective-permute-start.3
  118.5 9.7 %all-to-all-done.5 = bf16[4,32,2048]{2,1,0:T(8,128)(2,1)} async-done(((bf16[4,32,2048]{2,1,0:T(8,128)(2,1)}), bf16[4,32,2048]{2,1,0:T(8,128)(2,1)}, u32[]{:S(2)}, u32[]{:S(2)}) %all-to-all-start.5) | async-done | bytes 524320 | tf_op jit(solution)/shard_map/all_to_all | solution.py:446
  128.2 1.1 reduce_sum.42
  129.3 1.6 %collective-permute-start.6 = (bf16[32,2048]{1,0:T(8,128)(2,1)S(1)}, bf16[32,2048]{1,0:T(8,128)(2,1)S(1)}, u32[]{:S(2)}, u32[]{:S(2)}) collective-permute-start(bf16[32,2048]{1,0:T(8,128)(2,1)S(1)} %reduce_sum.42), channel_id=1, source_target_pairs={{0,1},{1,0},{2,3},{3,2},{4,5},{5,4},{6,7},{7,6},{8,9},{9,8},{10,11... | collective-permute-start | bytes 393224 | tf_op jit(solution)/shard_map/ppermute | solution.py:340
  130.9 1.6 %convert_add_fusion.1 = f32[32,2048]{1,0:T(8,128)} fusion(bf16[32,2048]{1,0:T(8,128)(2,1)} %collective-permute-done.7, bf16[32,2048]{1,0:T(8,128)(2,1)S(1)} %get-tuple-element.31), kind=kLoop, calls=%fused_computation.7 | loop fusion | flops 196608 | bytes 524288 | tf_op jit(solution)/shard_map/add | solution.py:345
  132.6 1.6 %shard_map.137 = bf16[128,1536]{1,0:T(8,128)(2,1)} custom-call(s32[4]{0:T(128)S(1)} %pad_add_fusion.ints, f32[128,1536]{1,0:T(8,128)S(1)} %shard_map.136.d_mixed, f32[2,1536]{1,0:T(2,128)S(1)} %collective-permute-done.3.later, f32[3,1536]{1,0:T(4,128)S(1)} %copy-done.19), custom_call_target="tpu_custom_call" | custom-call | flops 1048576 | bytes 1048576 | tf_op jit(solution)/shard_map/pallas_call | solution.py:468
  134.2 0.2 collective-permute-done.6
  134.4 0.7 convert_add_fusion.2
  (39 shorter events, 0.1 us)
Async XLA Ops:
  0.6 35.4 %copy-start.1 = (bf16[1,128,1536]{2,1,0:T(8,128)(2,1)S(1)}, bf16[1,128,1536]{2,1,0:T(8,128)(2,1)}, u32[]{:S(2)}) copy-start(bf16[1,128,1536]{2,1,0:T(8,128)(2,1)} %param.10) | copy-start | bytes 1179652
  0.6 38.7 %copy-start.19 = (f32[3,1536]{1,0:T(4,128)S(1)}, f32[3,1536]{1,0:T(4,128)}, u32[]{:S(2)}) copy-start(f32[3,1536]{1,0:T(4,128)} %taps.3) | copy-start | bytes 55300
  1.7 47.9 %copy-start.12 = (bf16[256,256]{1,0:T(8,128)(2,1)S(1)}, bf16[256,256]{1,0:T(8,128)(2,1)}, u32[]{:S(2)}) copy-start(bf16[256,256]{1,0:T(8,128)(2,1)} %constant.40.clone.low) | copy-start | bytes 393220
  1.7 47.9 %copy-start.20 = (f32[2,17,128]{2,1,0:T(8,128)S(1)}, f32[2,17,128]{2,1,0:T(8,128)}, u32[]{:S(2)}) copy-start(f32[2,17,128]{2,1,0:T(8,128)} %constant.38.clone.twist) | copy-start | bytes 52228
  22.4 12.5 %collective-permute-start.1 = (bf16[128,2048]{1,0:T(8,128)(2,1)S(1)}, bf16[128,2048]{1,0:T(8,128)(2,1)S(1)}, u32[]{:S(2)}, u32[]{:S(2)}) collective-permute-start(bf16[128,2048]{1,0:T(8,128)(2,1)S(1)} %bitcast.27), channel_id=1, source_target_pairs={{0,4},{4,0},{1,5},{5,1},{2,6},{6,2},{3,7},{7,3},{8,12},{12,8},{9,1... | collective-permute-start | bytes 1572872 | tf_op jit(solution)/shard_map/ppermute | solution.py:340
  36.0 28.6 %copy-start.26 = (s32[2]{0:T(128)S(1)}, s32[2]{0:T(128)}, u32[]{:S(2)}) copy-start(s32[2]{0:T(128)} %param.16) | copy-start | bytes 28
  36.0 30.6 %copy-start = (bf16[1,128,2048]{2,1,0:T(8,128)(2,1)S(1)}, bf16[1,128,2048]{2,1,0:T(8,128)(2,1)}, u32[]{:S(2)}) copy-start(bf16[1,128,2048]{2,1,0:T(8,128)(2,1)} %param.14) | copy-start | bytes 1572868
  36.0 30.5 %collective-permute-start.2 = (bf16[2,128,2048]{2,1,0:T(8,128)(2,1)}, bf16[2,128,2048]{2,1,0:T(8,128)(2,1)S(1)}, u32[]{:S(2)}, u32[]{:S(2)}) collective-permute-start(bf16[2,128,2048]{2,1,0:T(8,128)(2,1)} %pad_maximum_fusion), channel_id=1, source_target_pairs={{0,2},{2,0},{1,3},{3,1},{4,6},{6,4},{5,7},{7,5},{8,10},{10,8},{9,1... | collective-permute-start | bytes 3145736 | tf_op jit(solution)/shard_map/ppermute | solution.py:340
  36.1 3.2 %collective-permute-start = (bf16[2,1536]{1,0:T(2,128)(2,1)S(1)}, bf16[2,1536]{1,0:T(2,128)(2,1)S(1)}, u32[]{:S(2)}, u32[]{:S(2)}) collective-permute-start(bf16[2,1536]{1,0:T(2,128)(2,1)S(1)} %broadcast_select_fusion), channel_id=1, source_target_pairs={{0,2},{2,4},{4,6},{6,8},{8,10},{10,12},{12,14},{14,16},{16,18},{18... | collective-permute-start | bytes 18440 | tf_op jit(solution)/shard_map/ppermute | solution.py:380
  40.4 0.7 copy-start.2
  41.1 0.7 copy-start.9
  41.8 0.7 copy-start.18
  42.5 0.7 copy-start.4
  43.2 14.3 %all-to-all-start = ((bf16[16,32,128]{2,1,0:T(8,128)(2,1)}), bf16[16,32,128]{2,1,0:T(8,128)(2,1)}, u32[]{:S(2)}, u32[]{:S(2)}) async-start(bf16[16,32,128]{2,1,0:T(8,128)(2,1)} %bitcast.38), calls=%async_computation | async-start | bytes 262144 | tf_op jit(solution)/shard_map/all_to_all | solution.py:390
  49.6 1.0 copy-start.8
  50.5 0.9 copy-start.13
  59.6 0.6 copy-start.17
  60.3 0.8 copy-start.23
  61.1 11.4 %all-to-all-start.1 = ((bf16[16,32,128]{2,1,0:T(8,128)(2,1)}), bf16[16,32,128]{2,1,0:T(8,128)(2,1)S(1)}, u32[]{:S(2)}, u32[]{:S(2)}) async-start(bf16[16,32,128]{2,1,0:T(8,128)(2,1)} %copy-done.17), calls=%async_computation.1 | async-start | bytes 262144 | tf_op jit(solution)/shard_map/all_to_all | solution.py:390
  66.6 1.0 copy-start.10
  68.8 0.7 copy-start.6
  69.5 0.7 copy-start.15
  70.2 0.8 copy-start.21
  72.5 1.0 copy-start.11
  73.5 1.0 copy-start.22
  75.8 2.7 %collective-permute-start.4 = (bf16[2,128,2048]{2,1,0:T(8,128)(2,1)S(1)}, bf16[2,128,2048]{2,1,0:T(8,128)(2,1)S(1)}, u32[]{:S(2)}, u32[]{:S(2)}) collective-permute-start(bf16[2,128,2048]{2,1,0:T(8,128)(2,1)S(1)} %get-tuple-element.30), channel_id=1, source_target_pairs={{0,2},{2,0},{1,3},{3,1},{4,6},{6,4},{5,7},{7,5},{8,10},{10,8},{9,1... | collective-permute-start | bytes 3145736 | tf_op jit(solution)/shard_map/ppermute | solution.py:340
  78.5 1.6 %copy-start.16 = (bf16[512,128]{1,0:T(8,128)(2,1)S(1)}, bf16[512,128]{1,0:T(8,128)(2,1)}, u32[]{:S(2)}) copy-start(bf16[512,128]{1,0:T(8,128)(2,1)} %copy-done.15) | copy-start | bytes 393220
  78.5 16.8 %copy-start.14 = (bf16[256,256]{1,0:T(8,128)(2,1)S(1)}, bf16[256,256]{1,0:T(8,128)(2,1)}, u32[]{:S(2)}) copy-start(bf16[256,256]{1,0:T(8,128)(2,1)} %constant.39.clone.high) | copy-start | bytes 393220
  78.5 16.8 %copy-start.24 = (f32[544,256]{1,0:T(8,128)S(1)}, f32[544,256]{1,0:T(8,128)}, u32[]{:S(2)}) copy-start(f32[544,256]{1,0:T(8,128)} %copy-done.23) | copy-start | bytes 1671172
  78.9 18.4 %copy-start.25 = (f32[2,128,2048]{2,1,0:T(8,128)}, f32[2,128,2048]{2,1,0:T(8,128)S(1)}, u32[]{:S(2)}) copy-start(f32[2,128,2048]{2,1,0:T(8,128)S(1)} %convert_add_fusion) | copy-start | bytes 6291460
  79.8 22.0 %collective-permute-start.5 = (bf16[128,2048]{1,0:T(8,128)(2,1)}, bf16[128,2048]{1,0:T(8,128)(2,1)}, u32[]{:S(2)}, u32[]{:S(2)}) collective-permute-start(bf16[128,2048]{1,0:T(8,128)(2,1)} %fusion.2), channel_id=1, source_target_pairs={{0,4},{4,0},{1,5},{5,1},{2,6},{6,2},{3,7},{7,3},{8,12},{12,8},{9,1... | collective-permute-start | bytes 1572872 | tf_op jit(solution)/shard_map/ppermute | solution.py:340
  97.2 12.5 %all-to-all-start.4 = ((bf16[16,32,128]{2,1,0:T(8,128)(2,1)}), bf16[16,32,128]{2,1,0:T(8,128)(2,1)S(1)}, u32[]{:S(2)}, u32[]{:S(2)}) async-start(bf16[16,32,128]{2,1,0:T(8,128)(2,1)} %get-tuple-element.26), calls=%async_computation.4 | async-start | bytes 262144 | tf_op jit(solution)/shard_map/all_to_all | solution.py:390
  104.1 12.9 %copy-start.3 = (f32[512,128]{1,0:T(8,128)S(1)}, f32[512,128]{1,0:T(8,128)}, u32[]{:S(2)}) copy-start(f32[512,128]{1,0:T(8,128)} %copy-done.2) | copy-start | bytes 786436
  104.1 12.9 %copy-start.5 = (f32[512,128]{1,0:T(8,128)S(1)}, f32[512,128]{1,0:T(8,128)}, u32[]{:S(2)}) copy-start(f32[512,128]{1,0:T(8,128)} %copy-done.4) | copy-start | bytes 786436
  104.1 12.9 %copy-start.7 = (f32[512,128]{1,0:T(8,128)S(1)}, f32[512,128]{1,0:T(8,128)}, u32[]{:S(2)}) copy-start(f32[512,128]{1,0:T(8,128)} %copy-done.6) | copy-start | bytes 786436
  109.7 18.5 %all-to-all-start.5 = ((bf16[4,32,2048]{2,1,0:T(8,128)(2,1)}), bf16[4,32,2048]{2,1,0:T(8,128)(2,1)}, u32[]{:S(2)}, u32[]{:S(2)}) async-start(bf16[4,32,2048]{2,1,0:T(8,128)(2,1)} %bitcast.39), calls=%async_computation.5 | async-start | bytes 1048576 | tf_op jit(solution)/shard_map/all_to_all | solution.py:446
  113.9 17.1 %collective-permute-start.7 = (bf16[32,2048]{1,0:T(8,128)(2,1)S(1)}, bf16[32,2048]{1,0:T(8,128)(2,1)}, u32[]{:S(2)}, u32[]{:S(2)}) collective-permute-start(bf16[32,2048]{1,0:T(8,128)(2,1)S(1)} %get-tuple-element.31), channel_id=1, source_target_pairs={{0,1},{1,0},{2,3},{3,2},{4,5},{5,4},{6,7},{7,6},{8,9},{9,8},{10,11... | collective-permute-start | bytes 393224 | tf_op jit(solution)/shard_map/ppermute | solution.py:340
  117.2 15.3 %collective-permute-start.3 = (f32[2,1536]{1,0:T(2,128)S(1)}, f32[2,1536]{1,0:T(2,128)S(1)}, u32[]{:S(2)}, u32[]{:S(2)}) collective-permute-start(f32[2,1536]{1,0:T(2,128)S(1)} %slice.17), channel_id=1, source_target_pairs={{2,0},{4,2},{6,4},{8,6},{10,8},{12,10},{14,12},{16,14},{18,16},{20... | collective-permute-start | bytes 36872 | tf_op jit(solution)/shard_map/ppermute | solution.py:467
  129.3 5.0 %collective-permute-start.6 = (bf16[32,2048]{1,0:T(8,128)(2,1)S(1)}, bf16[32,2048]{1,0:T(8,128)(2,1)S(1)}, u32[]{:S(2)}, u32[]{:S(2)}) collective-permute-start(bf16[32,2048]{1,0:T(8,128)(2,1)S(1)} %reduce_sum.42), channel_id=1, source_target_pairs={{0,1},{1,0},{2,3},{3,2},{4,5},{5,4},{6,7},{7,6},{8,9},{9,8},{10,11... | collective-permute-start | bytes 393224 | tf_op jit(solution)/shard_map/ppermute | solution.py:340
where the time goes:
time: 136 us; the launch traced here: 135 us
  blocking collectives  35.9 us (26%)
  waiting for transfers between devices  34.4 us (25%)
  starting transfers between devices  27.3 us (20%)
  local copies, waits for them, and re-layouts  13.1 us (10%)
  Pallas kernels  11.5 us (8%)
  other arithmetic  10.5 us (8%)
  between operations  2.26 us (2%)
    all_to_all x1, blocking collectives, per_device(): lax.all_to_all(jnp.broadcast_to(w_out[None], (lines,) + w_out.shape), 'l'...  20.7 us
    all_to_all x1, blocking collectives, exchange(): return lax.all_to_all(block, axes, 0, 0, tiled=True)  15.2 us
    all_to_all x3, starting transfers between devices, exchange(): return lax.all_to_all(block, axes, 0, 0, tiled=True)  14.4 us
    all_to_all x3, waiting for transfers between devices, exchange(): return lax.all_to_all(block, axes, 0, 0, tiled=True)  12.8 us
    ppermute x6, waiting for transfers between devices, swap(): return lax.ppermute(block, axis, SWAP)  11.9 us
    unnamed x54, local copies, waits for them, and re-layouts  11.2 us
    all_to_all x1, waiting for transfers between devices, per_device(): lax.all_to_all(quad.astype(BF16).reshape(lines, chans, features), 'l', 0,...  9.65 us
    ppermute x6, starting transfers between devices, swap(): return lax.ppermute(block, axis, SWAP)  5.04 us
  transfers between devices with their start and end apart: 12, of which 8 were waited for; matrix products, arithmetic and copies ran while one was open for 6% of the time, Pallas kernels for 8%

commit v1 on v0

v1 whole, which is shorter than its diff:
```python
import functools
import math
import typing

import jax
import jax.numpy as jnp
import ml_dtypes
import numpy as np
from jax import lax
from jax.experimental import pallas as pl
from jax.experimental.pallas import tpu as pltpu
from jax.sharding import Mesh
from jax.sharding import PartitionSpec as P

F32 = jnp.float32
BF16 = jnp.bfloat16
LANES = 128
VMEM_LIMIT = 20 << 20
SMEM = pl.BlockSpec(memory_space=pltpu.SMEM)
HBM = pl.BlockSpec(memory_space=pltpu.HBM)


def split_bf16(values):
    high = values.astype(ml_dtypes.bfloat16)
    low = (values - high.astype(np.float64)).astype(ml_dtypes.bfloat16)
    return high, low


def fft_tables(blocks):
    size = 2 * blocks * LANES
    k1 = np.arange(blocks + 1)[:, None]
    lane = np.arange(LANES)
    angle = -2.0 * np.pi * (k1 * lane[None, :] % size) / size
    twist = np.stack([np.cos(angle), np.sin(angle)]).astype(np.float32)
    inner = -2.0 * np.pi * (lane[:, None] * lane[None, :] % LANES) / LANES
    cos, sin = np.cos(inner), np.sin(inner)
    matrix = np.block([[cos, sin], [-sin, cos]])
    high, low = split_bf16(matrix)
    return jnp.asarray(twist), jnp.asarray(np.stack([high, low]))


def real_fft(values):
    half = len(values)
    if half == 1:
        return [(values[0], None), (values[0], None)]
    even, odd = real_fft(values[0::2]), real_fft(values[1::2])
    out = [None] * (half + 1)
    out[0] = (even[0][0] + odd[0][0], None)
    out[half] = (even[0][0] - odd[0][0], None)
    out[half // 2] = (even[half // 2][0], -odd[half // 2][0])
    for k in range(1, half // 2):
        cos, sin = math.cos(math.pi * k / half), -math.sin(math.pi * k / half)
        (e_re, e_im), (o_re, o_im) = even[k], odd[k]
        t_re = o_re * cos - o_im * sin
        t_im = o_re * sin + o_im * cos
        out[k] = (e_re + t_re, e_im + t_im)
        out[half - k] = (e_re - t_re, t_im - e_im)
    return out


def real_ifft(spectrum):
    half = len(spectrum) - 1
    if half == 1:
        return [spectrum[0][0] + spectrum[1][0]]
    even = [None] * (half // 2 + 1)
    odd = [None] * (half // 2 + 1)
    even[0] = (spectrum[0][0] + spectrum[half][0], None)
    odd[0] = (spectrum[0][0] - spectrum[half][0], None)
    even[half // 2] = (2.0 * spectrum[half // 2][0], None)
    odd[half // 2] = (-2.0 * spectrum[half // 2][1], None)
    for k in range(1, half // 2):
        cos, sin = math.cos(math.pi * k / half), math.sin(math.pi * k / half)
        (a_re, a_im), (b_re, b_im) = spectrum[k], spectrum[half - k]
        even[k] = (a_re + b_re, a_im - b_im)
        d_re, d_im = a_re - b_re, a_im + b_im
        odd[k] = (d_re * cos - d_im * sin, d_re * sin + d_im * cos)
    out = [None] * half
    out[0::2] = real_ifft(even)
    out[1::2] = real_ifft(odd)
    return out


def split_dot(left, high, low, transposed):
    dims = (((1,), (1 if transposed else 0,)), ((), ()))
    dot = functools.partial(lax.dot_general, dimension_numbers=dims, preferred_element_type=F32)
    left_high = left.astype(BF16)
    left_low = (left - left_high.astype(F32)).astype(BF16)
    return dot(left_high, high) + (dot(left_low, high) + dot(left_high, low))


def to_spectrum(load, blocks, chans, twist, matrix, work):
    for first in range(0, chans, 8):
        rows = slice(first, first + 8)
        freqs = real_fft([load(n1, rows) for n1 in range(blocks)])
        for k1, (re, im) in enumerate(freqs):
            at = slice(k1 * chans + first, k1 * chans + first + 8)
            if k1 == 0:
                work[at, :LANES] = re
                work[at, LANES:] = jnp.zeros_like(re)
                continue
            cos, sin = twist[0, k1 : k1 + 1, :], twist[1, k1 : k1 + 1, :]
            if im is None:
                work[at, :LANES] = re * cos
                work[at, LANES:] = re * sin
            else:
                work[at, :LANES] = re * cos - im * sin
                work[at, LANES:] = re * sin + im * cos
    return split_dot(work[...], matrix[0], matrix[1], False)


def from_spectrum(spectrum, blocks, chans, twist, matrix, work, store):
    scale = 1.0 / (2 * blocks * LANES)
    work[...] = split_dot(spectrum, matrix[0], matrix[1], True)
    for first in range(0, chans, 8):
        rows = slice(first, first + 8)
        freqs = []
        for k1 in range(blocks + 1):
            at = slice(k1 * chans + first, k1 * chans + first + 8)
            re, im = work[at, :LANES] * scale, work[at, LANES:] * scale
            cos, sin = twist[0, k1 : k1 + 1, :], twist[1, k1 : k1 + 1, :]
            if k1 == 0:
                freqs.append((re, None))
            elif k1 == blocks:
                freqs.append((re * cos + im * sin, None))
            else:
                freqs.append((re * cos + im * sin, im * cos - re * sin))
        for n1, value in enumerate(real_ifft(freqs)):
            store(n1, rows, value)


def times(a, b):
    a_re, a_im, b_re, b_im = a[:, :LANES], a[:, LANES:], b[:, :LANES], b[:, LANES:]
    return jnp.concatenate([a_re * b_re - a_im * b_im, a_re * b_im + a_im * b_re], axis=1)


def conj_times(a, b):
    a_re, a_im, b_re, b_im = a[:, :LANES], a[:, LANES:], b[:, :LANES], b[:, LANES:]
    return jnp.concatenate([a_re * b_re + a_im * b_im, a_re * b_im - a_im * b_re], axis=1)


def filter_kernel(filt, twist, matrix, spec, work, *, blocks, chans):
    def load(n1, rows):
        return filt[rows, n1 * LANES : (n1 + 1) * LANES]

    spec[...] = to_spectrum(load, blocks, chans, twist, matrix, work)


def forward_kernel(
    gated, filt_spec, twist, matrix, long_out, gated_spec, work, signal, *, blocks, chans
):
    for n1 in range(blocks):
        signal[n1] = gated[n1].astype(F32)

    def load(n1, rows):
        return signal[n1, rows, :]

    spec = to_spectrum(load, blocks, chans, twist, matrix, work)
    gated_spec[...] = spec

    def store(n1, rows, value):
        signal[n1, rows, :] = value

    from_spectrum(times(spec, filt_spec[...]), blocks, chans, twist, matrix, work, store)
    for n1 in range(blocks):
        long_out[n1] = signal[n1].astype(BF16)


def backward_kernel(
    d_long,
    filt_spec,
    gated_spec,
    twist,
    matrix,
    d_gated,
    d_filter,
    work,
    signal,
    held,
    *,
    blocks,
    chans,
    scale,
):
    for n1 in range(blocks):
        signal[n1] = d_long[n1].astype(F32)

    def load(n1, rows):
        return signal[n1, rows, :]

    held[...] = to_spectrum(load, blocks, chans, twist, matrix, work)

    def store(n1, rows, value):
        signal[n1, rows, :] = value

    spec = conj_times(filt_spec[...], held[...])
    from_spectrum(spec, blocks, chans, twist, matrix, work, store)
    for n1 in range(blocks):
        d_gated[n1] = signal[n1].astype(BF16)
    spec = conj_times(gated_spec[...], held[...])
    from_spectrum(spec, blocks, chans, twist, matrix, work, store)
    for n1 in range(blocks):
        d_filter[:, n1 * LANES : (n1 + 1) * LANES] = (signal[n1] * scale).astype(BF16)


class Split(typing.NamedTuple):
    samples: int
    lines: int
    chans: int
    line_first: bool


def mixed_stream(stream, proj, earlier, taps, room, width):
    rows = proj.shape[0]
    row = lax.broadcasted_iota(jnp.int32, (rows, 1), 0)
    past_row = lax.broadcasted_iota(jnp.int32, (2, 1), 0)
    cols = slice(stream * width, (stream + 1) * width)
    masked = jnp.where(row < room, proj[:, cols].astype(F32), 0.0)
    past = jnp.where(past_row < room + 2, earlier[:, cols].astype(F32), 0.0)
    mixed = taps[0:1, cols] * masked
    for tap in range(1, 3):
        shifted = pltpu.roll(masked, tap, 0)
        for r in range(tap):
            shifted = jnp.where(row == r, past[2 - tap + r : 3 - tap + r, :], shifted)
        mixed = mixed + taps[tap : tap + 1, cols] * shifted
    return mixed


def prep_kernel(
    scalars, proj_far, earlier, taps_far, gated_t, query_t, proj, taps, done, *, width, split
):
    copies = [
        pltpu.make_async_copy(proj_far, proj, done.at[0]),
        pltpu.make_async_copy(taps_far, taps, done.at[1]),
    ]
    for copy in copies:
        copy.start()
    for copy in copies:
        copy.wait()
    room = room_left(scalars, split, proj.shape[0])
    query, key, value = (
        mixed_stream(stream, proj, earlier, taps, room, width) for stream in range(3)
    )
    gated_t[...] = (key * value).T.astype(BF16)
    query_t[...] = query.T


def room_left(scalars, split, rows):
    group, sample = scalars[0] // split.samples, scalars[0] % split.samples
    length = scalars[1]
    for other in range(1, split.samples):
        length = jnp.where(sample == other, scalars[1 + other], length)
    return length - group * rows


def loss_weight(scalars, split):
    sample = scalars[0] % split.samples
    total, mine = jnp.float32(0), jnp.float32(0)
    for other in range(split.samples):
        count = scalars[1 + split.samples + other].astype(F32)
        total = total + count
        mine = jnp.where(sample == other, count, mine)
    return jnp.full((1, LANES), mine * split.samples) / jnp.full((1, LANES), total)


def natural_row(scalars, rel_h, rel_c, step, split):
    group = scalars[0] // split.samples
    lines, chans = split.lines, split.chans
    c = (group % 2 + rel_c) % 2
    if split.line_first:
        h, line = group // 2 % 2, group // 4
    else:
        h, line = group // (2 * lines), group // 2 % lines
    h, line = (h + rel_h) % 2, (line + lines - step) % lines
    at = (line * 2 + h) * 2 + c if split.line_first else (h * lines + line) * 2 + c
    return pl.multiple_of(at * chans, chans)


PIECES = ((0, 0), (1, 0), (0, 1), (1, 1))
CHUNKS = 1


def cotangent_kernel(scalars, dout, cot, *, split):
    rows = dout.shape[0]
    row = lax.broadcasted_iota(jnp.int32, (rows, 1), 0)
    mask = jnp.where(row < room_left(scalars, split, rows), 1.0, 0.0)
    weight = loss_weight(scalars, split)[:, :1]
    cot[...] = (dout[...].astype(F32) * mask * weight).astype(BF16)


def d_long_kernel(scalars, cot, query_t, *refs, split):
    *weights, d_product_t, d_long_t = refs
    lines, chans = split.lines, split.chans
    part = cot.shape[1] // CHUNKS
    for piece, (rel_h, rel_c) in enumerate(PIECES):
        got = sum(
            lax.dot_general(
                weights[piece * CHUNKS + chunk][...],
                cot[:, chunk * part : (chunk + 1) * part],
                (((1,), (1,)), ((), ())),
                preferred_element_type=F32,
            )
            for chunk in range(CHUNKS)
        )
        for line in range(lines):
            at = natural_row(scalars, rel_h, rel_c, line, split)
            d_product_t[pl.ds(at, chans), :] = got[line * chans : (line + 1) * chans]
    d_long_t[...] = (d_product_t[...] * query_t[...]).astype(BF16)


def partial_kernel(
    scalars, long_t, query_t, cot, product, *refs, split, scale, tile
):
    *parts, product_t = refs
    lines, chans = split.lines, split.chans
    part = cot.shape[1] // CHUNKS
    product_t[...] = query_t[...] * long_t[...].astype(F32)
    for piece, (rel_h, rel_c) in enumerate(PIECES):
        left = jnp.concatenate(
            [
                product_t[pl.ds(natural_row(scalars, rel_h, rel_c, line, split), chans), :]
                for line in range(lines)
            ],
            axis=0,
        )
        product[piece] = left.T.astype(BF16)
        left = left.astype(BF16)
        for first in range(0, cot.shape[1], tile):
            cols = slice(first, first + tile)
            got = jnp.dot(left, cot[:, cols], preferred_element_type=F32) * scale
            out = parts[(2 * rel_c + rel_h) * CHUNKS + first // part]
            out[:, first % part : first % part + tile] = got.astype(BF16)


def output_kernel(product, *refs, tile):
    *weights, out = refs
    part = out.shape[1] // CHUNKS
    for first in range(0, out.shape[1], tile):
        chunk, cols = first // part, slice(first % part, first % part + tile)
        total = sum(
            jnp.dot(
                product[piece], weights[piece * CHUNKS + chunk][:, cols], preferred_element_type=F32
            )
            for piece in range(4)
        )
        out[:, first : first + tile] = total.astype(BF16)


def mixed_grads(d_product_t, long_t, d_gated_t, key, value, rows):
    d_query = (d_product_t[...] * long_t[...].astype(F32)).T[:rows]
    d_gated = d_gated_t[...].astype(F32).T[:rows]
    return d_query, d_gated * value[:rows], d_gated * key[:rows]


def head_kernel(
    scalars, proj, earlier, taps, d_product_t, long_t, d_gated_t, head, *, width, split
):
    room = room_left(scalars, split, proj.shape[0])
    key, value = (mixed_stream(i, proj, earlier, taps, room, width) for i in (1, 2))
    grads = mixed_grads(d_product_t, long_t, d_gated_t, key, value, 8)
    for stream, grad in enumerate(grads):
        head[:, stream * width : (stream + 1) * width] = grad


def proj_grad_kernel(
    scalars,
    proj,
    earlier,
    taps,
    d_product_t,
    long_t,
    d_gated_t,
    later,
    d_proj,
    *,
    width,
    split,
):
    rows = proj.shape[0]
    row = lax.broadcasted_iota(jnp.int32, (rows, 1), 0)
    room = room_left(scalars, split, rows)
    key, value = (mixed_stream(i, proj, earlier, taps, room, width) for i in (1, 2))
    grads = mixed_grads(d_product_t, long_t, d_gated_t, key, value, rows)
    for stream, grad in enumerate(grads):
        cols = slice(stream * width, (stream + 1) * width)
        total = taps[0:1, cols] * grad
        for tap in range(1, 3):
            shifted = pltpu.roll(grad, rows - tap, 0)
            for r in range(tap):
                shifted = jnp.where(row == rows - tap + r, later[r : r + 1, cols], shifted)
            total = total + taps[tap : tap + 1, cols] * shifted
        d_proj[:, cols] = jnp.where(row < room, total, 0.0).astype(BF16)


def call(kernel, outs, args, scalars=0, scratch=(), flops=0, far=()):
    def full(value):
        return pl.BlockSpec(value.shape, lambda i, n=len(value.shape): (0,) * n)

    out_shape = [jax.ShapeDtypeStruct(shape, dtype) for shape, dtype in outs]
    return pl.pallas_call(
        kernel,
        grid=(1,),
        out_shape=out_shape,
        in_specs=[
            SMEM if i < scalars else HBM if i in far else full(v) for i, v in enumerate(args)
        ],
        out_specs=[full(v) for v in out_shape],
        scratch_shapes=list(scratch),
        compiler_params=pltpu.CompilerParams(vmem_limit_bytes=VMEM_LIMIT),
        cost_estimate=pl.CostEstimate(flops=flops, bytes_accessed=1024, transcendentals=0),
    )(*args)


SWAP = ((0, 1), (1, 0))


def after(value, *others):
    return lax.optimization_barrier((value,) + others)[0]


def swap(block, axis):
    return lax.ppermute(block, axis, SWAP)


def dp_sum(block):
    if lax.axis_size("dp") == 2:
        return block.astype(F32) + swap(block, "dp").astype(F32)
    return lax.psum(block, "dp").astype(F32)


def line_route(lines, step):
    return [(i, (i + step) % lines) for i in range(lines)]


def along_line(block, lines):
    return [block] + [
        lax.ppermute(block, "l", line_route(lines, step)) for step in range(1, lines)
    ]


def per_device(axes, proj, short_filter, long_filter, w_out, dout, lengths, counts):
    rows, width = proj.shape[1], proj.shape[2] // 3
    chans, seq_len = long_filter.shape
    features = w_out.shape[1]
    batch = lengths.shape[0]
    ctx_size = seq_len // rows
    lines = lax.axis_size("l")
    split = Split(batch, lines, chans, axes[0] == "l")
    grad_scale = 1.0 / math.sqrt(batch * seq_len)
    assert batch == lax.axis_size("dp") and rows == LANES
    place = lax.axis_index(axes + ("dp",)).astype(jnp.int32).reshape(1)
    scalars = jnp.concatenate([place, lengths, counts])

    route = [(i, i + 1) for i in range(ctx_size - 1)]
    earlier = lax.ppermute(proj[0, rows - 2 :], axes, route)


    flat = (width, rows)
    width_of = features // CHUNKS
    parts = [
        along_line(after(w_out[:, i * width_of : (i + 1) * width_of], earlier), lines)
        for i in range(CHUNKS)
    ]
    inputs = (scalars, proj[0], earlier, short_filter)
    gated_t, query_t = call(
        functools.partial(prep_kernel, width=width, split=split),
        [(flat, BF16), (flat, F32)],
        inputs,
        1,
        far=(1, 3),
        scratch=[
            pltpu.VMEM((rows, 3 * width), BF16),
            pltpu.VMEM(short_filter.shape, F32),
            pltpu.SemaphoreType.DMA((2,)),
        ],
        flops=1 << 20,
    )

    (cot,) = call(
        functools.partial(cotangent_kernel, split=split),
        [((rows, features), BF16)],
        (scalars, after(dout[0], gated_t)),
        1,
        flops=1 << 20,
    )

    def exchange(block):
        return lax.all_to_all(block, axes, 0, 0, tiled=True)

    blocked = (ctx_size, chans, rows)
    tables = fft_tables(ctx_size)
    spec_shape = ((ctx_size + 1) * chans, 2 * LANES)
    sizes = {"blocks": ctx_size, "chans": chans}
    work = pltpu.VMEM(spec_shape, F32)
    signal = pltpu.VMEM(blocked, F32)
    fft_flops = 6 * spec_shape[0] * 2 * LANES * 2 * LANES
    (filt_spec,) = call(
        functools.partial(filter_kernel, **sizes),
        [(spec_shape, F32)],
        (after(long_filter, gated_t), *tables),
        scratch=[work],
        flops=fft_flops,
    )
    near = [
        jnp.concatenate(part[:1] + [after(p, filt_spec) for p in part[1:]]) for part in parts
    ]
    over = [swap(part, "h") for part in near]
    long_cols, gated_spec = call(
        functools.partial(forward_kernel, **sizes),
        [(blocked, BF16), (spec_shape, F32)],
        (exchange(gated_t.reshape(blocked)), filt_spec, *tables),
        scratch=[work, signal],
        flops=30 << 30,
    )
    long_t = exchange(long_cols).reshape(flat)
    over = [after(part, long_t) for part in over]
    weights = near + over + [swap(part, "c") for part in near + over]

    d_product_t, d_long_t = call(
        functools.partial(d_long_kernel, split=split),
        [(flat, F32), (flat, BF16)],
        (scalars, cot, query_t, *weights),
        1,
        flops=2 * rows * width * features,
    )
    d_long_cols = exchange(d_long_t.reshape(blocked))

    part = (lines * chans, width_of)
    product, *sums = call(
        functools.partial(partial_kernel, split=split, scale=grad_scale, tile=512),
        [((4, rows, lines * chans), BF16)] + [(part, BF16)] * (4 * CHUNKS),
        (scalars, long_t, query_t, after(cot, *weights)),
        1,
        scratch=[pltpu.VMEM(flat, F32)],
        flops=1024,
    )
    d_gated_cols, filter_part = call(
        functools.partial(backward_kernel, scale=grad_scale, **sizes),
        [(blocked, BF16), ((chans, seq_len), BF16)],
        (d_long_cols, filt_spec, gated_spec, *tables),
        scratch=[work, signal, work],
        flops=3 * fft_flops,
    )
    d_gated_t = exchange(d_gated_cols).reshape(flat)
    d_filter = dp_sum(filter_part)

    d_wout = []
    for chunk in range(CHUNKS):
        near_sum, over_sum, near_send, over_send = sums[chunk::CHUNKS]
        over_core, near_core = swap(over_send, "c"), swap(near_send, "c")
        over_sum = over_sum.astype(F32) + over_core.astype(F32)
        got = swap(over_sum.astype(BF16), "h")
        total = [
            near_sum[at].astype(F32) + near_core[at].astype(F32) + got[at].astype(F32)
            for at in (slice(i * chans, (i + 1) * chans) for i in range(lines))
        ]
        total_here = total[0]
        for step in range(1, lines):
            sent = total[lines - step].astype(BF16)
            total_here += lax.ppermute(sent, "l", line_route(lines, step)).astype(F32)
        d_wout.append(dp_sum(total_here.astype(BF16)))
    d_wout = jnp.concatenate(d_wout, axis=1)

    (output,) = call(
        functools.partial(output_kernel, tile=512),
        [((rows, features), BF16)],
        (product, *weights),
        flops=2 * rows * width * features,
    )

    (head,) = call(
        functools.partial(head_kernel, width=width, split=split),
        [((8, 3 * width), F32)],
        inputs + (d_product_t, long_t, d_gated_t),
        1,
        flops=1 << 20,
    )
    later = lax.ppermute(head[:2], axes, [(j, i) for i, j in route])
    (d_proj,) = call(
        functools.partial(proj_grad_kernel, width=width, split=split),
        [((rows, 3 * width), BF16)],
        inputs + (d_product_t, long_t, d_gated_t, later),
        1,
        flops=1 << 20,
    )
    return output[None], d_proj[None], d_wout, d_filter


def solution(mesh):
    ctx, dp = mesh.shape["ctx"], mesh.shape["dp"]
    if ctx == 16:
        axes, dims = ("l", "h", "c"), (4, 2, 2)
    else:
        axes, dims = ("h", "l", "c"), (2, ctx // 4, 2)
    fine = Mesh(mesh.devices.reshape(dims + (dp,)), axes + ("dp",))
    placed = (
        P("dp", axes, None),
        P(),
        P(axes, None),
        P(axes, None),
        P("dp", axes, None),
        P(),
        P(),
    )
    return jax.shard_map(
        functools.partial(per_device, axes),
        mesh=fine,
        in_specs=placed,
        out_specs=(P("dp", axes, None), P("dp", axes, None), P(axes, None), P(axes, None)),
        check_vma=False,
    )
```

time: 136 us -> 96.7 us (0.71)
  blocking collectives: 35.9 us -> 14.2 us
  waiting for transfers between devices: 34.4 us -> 22.6 us
  local copies, waits for them, and re-layouts: 13.1 us -> 4.53 us
  starting transfers between devices: 27.3 us -> 33 us
  other arithmetic: 10.5 us -> 6.72 us
  Pallas kernels: 11.5 us -> 14 us
    all_to_all x1 -> x0, blocking collectives: 20.7 us -> none  [per_device(): lax.all_to_all(jnp.broadcast_to(w_out[None], (lines,) + w_out.shape), 'l'...]
    ppermute x2 -> x8, starting transfers between devices: 3.69 us -> 17.2 us  [the longest x3 8.74 us: along_line(): lax.ppermute(block, 'l', line_route(lines, step))]
    all_to_all x1 -> x0, waiting for transfers between devices: 9.65 us -> none  [per_device(): lax.all_to_all(quad.astype(BF16).reshape(lines, chans, features), 'l', 0,...]
    ppermute x6 -> x8, waiting for transfers between devices: 11.9 us -> 3.01 us  [swap(): return lax.ppermute(block, axis, SWAP)]
    ppermute x2 -> x8, waiting for transfers between devices: 0.09 us -> 7.72 us  [the longest x3 5.78 us: per_device(): total_here += lax.ppermute(sent, 'l', line_route(lines, step)).astype(F32)]
    unnamed x54 -> x41, local copies, waits for them, and re-layouts: 11.2 us -> 3.76 us
    all_to_all x1 -> x0, starting transfers between devices: 4.13 us -> none  [per_device(): lax.all_to_all(quad.astype(BF16).reshape(lines, chans, features), 'l', 0,...]
    all_to_all x3, starting transfers between devices: 14.4 us -> 11.3 us  [exchange(): return lax.all_to_all(block, axes, 0, 0, tiled=True)]
  transfers between devices with their start and end apart: 12 -> 19, of which waited for: 8 -> 7; matrix products, arithmetic and copies ran while one was open for 6% -> 6% of each run, Pallas kernels for 8% -> 13%
where the time goes in v1:
time: 96.7 us; the launch traced here: 96 us
  starting transfers between devices  33 us (34%)
  waiting for transfers between devices  22.6 us (23%)
  blocking collectives  14.2 us (15%)
  Pallas kernels  14 us (14%)
  other arithmetic  6.72 us (7%)
  local copies, waits for them, and re-layouts  4.53 us (5%)
    all_to_all x1, blocking collectives, exchange(): return lax.all_to_all(block, axes, 0, 0, tiled=True)  14.2 us
    pallas_call x10, Pallas kernels, call(): pl.pallas_call(kernel, grid=(1,), out_shape=out_shape, in_specs=[SMEM if...  14 us
    all_to_all x3, waiting for transfers between devices, exchange(): return lax.all_to_all(block, axes, 0, 0, tiled=True)  11.9 us
    all_to_all x3, starting transfers between devices, exchange(): return lax.all_to_all(block, axes, 0, 0, tiled=True)  11.3 us
    ppermute x3, starting transfers between devices, along_line(): lax.ppermute(block, 'l', line_route(lines, step))  8.74 us
    ppermute x3, waiting for transfers between devices, per_device(): total_here += lax.ppermute(sent, 'l', line_route(lines, step)).astype(F32)  5.78 us
    ppermute x3, starting transfers between devices, per_device(): total_here += lax.ppermute(sent, 'l', line_route(lines, step)).astype(F32)  4.77 us
    ppermute x8, starting transfers between devices, swap(): return lax.ppermute(block, axis, SWAP)  4.58 us
  transfers between devices with their start and end apart: 19, of which 7 were waited for; matrix products, arithmetic and copies ran while one was open for 6% of the time, Pallas kernels for 13%

profile of v1, /device:TPU:0, one launch (start us, length us, event | category | flops | bytes accessed | tf_op | source)
XLA Modules:
  0.0 96.0 jit_solution(10330544630107064148)
XLA Ops:
  0.6 0.0 copy-start.8
  0.6 0.8 slice_bitcast_fusion
  1.4 2.4 %collective-permute-start = (bf16[2,1536]{1,0:T(2,128)(2,1)S(1)}, bf16[2,1536]{1,0:T(2,128)(2,1)S(1)}, u32[]{:S(2)}, u32[]{:S(2)}) collective-permute-start(bf16[2,1536]{1,0:T(2,128)(2,1)S(1)} %slice_bitcast_fusion), channel_id=1, source_target_pairs={{0,2},{2,4},{4,6},{6,8},{8,10},{10,12},{12,14},{14,16},{16,18},{18... | collective-permute-start | bytes 18440 | tf_op jit(solution)/shard_map/ppermute | solution.py:454
  3.8 0.0 copy-start.17
  3.8 0.0 copy-start.18
  3.8 0.6 copy-done.17
  4.4 0.0 copy-done.18
  4.4 0.1 pad_add_fusion.scalars
  4.5 0.0 collective-permute-done.earlier
  4.6 7.7 %collective-permute-start.3 = (bf16[32,2048]{1,0:T(8,128)(2,1)}, bf16[32,2048]{1,0:T(8,128)(2,1)S(1)}, u32[]{:S(2)}, u32[]{:S(2)}) collective-permute-start(bf16[32,2048]{1,0:T(8,128)(2,1)} %param.12), channel_id=1, source_target_pairs={{0,24},{8,0},{16,8},{24,16},{1,25},{9,1},{17,9},{25,17},{2,26},{10... | collective-permute-start | bytes 393224 | tf_op jit(solution)/shard_map/ppermute | solution.py:436
  12.3 1.0 %collective-permute-start.1 = (bf16[32,2048]{1,0:T(8,128)(2,1)}, bf16[32,2048]{1,0:T(8,128)(2,1)S(1)}, u32[]{:S(2)}, u32[]{:S(2)}) collective-permute-start(bf16[32,2048]{1,0:T(8,128)(2,1)} %param.12), channel_id=1, source_target_pairs={{0,8},{8,16},{16,24},{24,0},{1,9},{9,17},{17,25},{25,1},{2,10},{10... | collective-permute-start | bytes 393224 | tf_op jit(solution)/shard_map/ppermute | solution.py:436
  13.3 1.0 %copy-done = bf16[1,128,1536]{2,1,0:T(8,128)(2,1)S(1)} copy-done((bf16[1,128,1536]{2,1,0:T(8,128)(2,1)S(1)}, bf16[1,128,1536]{2,1,0:T(8,128)(2,1)}, u32[]{:S(2)}) %copy-start) | copy-done | bytes 393240
  14.3 1.8 %shard_map.120 = (bf16[512,128]{1,0:T(8,128)(2,1)}, f32[512,128]{1,0:T(8,128)S(1)}) custom-call(s32[5]{0:T(128)S(1)} %pad_add_fusion.scalars, bf16[128,1536]{1,0:T(8,128)(2,1)S(1)} %bitcast.11, bf16[2,1536]{1,0:T(2,128)(2,1)S(1)} %collective-permute-done.earlier, f32[3,1536]{1,0:T(4,128)S(1)} %copy-done.8), custom_call_target="tpu_custom_call" | custom-call | flops 1048576 | bytes 1024 | tf_op jit(solution)/shard_map/pallas_call | solution.py:399
  16.1 0.0 copy-start.12
  16.1 4.2 %all-to-all-start = ((bf16[16,32,128]{2,1,0:T(8,128)(2,1)}), bf16[16,32,128]{2,1,0:T(8,128)(2,1)S(1)}, u32[]{:S(2)}, u32[]{:S(2)}) async-start(bf16[16,32,128]{2,1,0:T(8,128)(2,1)} %bitcast.3), calls=%async_computation | async-start | bytes 262144 | tf_op jit(solution)/shard_map/all_to_all | solution.py:487
  20.4 0.0 copy-start.16
  20.4 0.5 shard_map.121.filt_spec
  20.9 0.4 copy-done.16
  21.3 1.9 %collective-permute-done.2 = bf16[32,2048]{1,0:T(8,128)(2,1)S(1)} collective-permute-done((bf16[32,2048]{1,0:T(8,128)(2,1)}, bf16[32,2048]{1,0:T(8,128)(2,1)S(1)}, u32[]{:S(2)}, u32[]{:S(2)}) %collective-permute-start.2) | collective-permute-done | bytes 131104 | tf_op jit(solution)/shard_map/ppermute | solution.py:436
  23.2 0.0 collective-permute-done.1
  23.2 0.0 collective-permute-done.3
  23.3 0.8 collective-permute-start.4
  24.0 4.3 %all-to-all-done.gated = bf16[16,32,128]{2,1,0:T(8,128)(2,1)S(1)} async-done(((bf16[16,32,128]{2,1,0:T(8,128)(2,1)}), bf16[16,32,128]{2,1,0:T(8,128)(2,1)S(1)}, u32[]{:S(2)}, u32[]{:S(2)}) %all-to-all-start) | async-done | bytes 131104 | tf_op jit(solution)/shard_map/all_to_all | solution.py:487
  28.3 1.8 %shard_map.122 = (bf16[16,32,128]{2,1,0:T(8,128)(2,1)}, f32[544,256]{1,0:T(8,128)S(1)}) custom-call(bf16[16,32,128]{2,1,0:T(8,128)(2,1)S(1)} %all-to-all-done.gated, f32[544,256]{1,0:T(8,128)S(1)} %shard_map.121.filt_spec, f32[2,17,128]{2,1,0:T(8,128)S(1)} %copy-done.12, bf16[2,256,256]{2,1,0:T(8,128)(2,1)S(1)} %copy-done.6), custom_call_target="tpu_custom_call" | custom-call | flops 32212254720 | bytes 1024 | tf_op jit(solution)/shard_map/pallas_call | solution.py:399
  30.1 0.8 copy-done.14
  31.0 3.5 %all-to-all-start.1 = ((bf16[16,32,128]{2,1,0:T(8,128)(2,1)}), bf16[16,32,128]{2,1,0:T(8,128)(2,1)S(1)}, u32[]{:S(2)}, u32[]{:S(2)}) async-start(bf16[16,32,128]{2,1,0:T(8,128)(2,1)} %get-tuple-element.27), calls=%async_computation.1 | async-start | bytes 262144 | tf_op jit(solution)/shard_map/all_to_all | solution.py:487
  34.5 0.3 collective-permute-start.5
  34.8 7.6 %all-to-all-done.1 = bf16[16,32,128]{2,1,0:T(8,128)(2,1)S(1)} async-done(((bf16[16,32,128]{2,1,0:T(8,128)(2,1)}), bf16[16,32,128]{2,1,0:T(8,128)(2,1)S(1)}, u32[]{:S(2)}, u32[]{:S(2)}) %all-to-all-start.1) | async-done | bytes 131104 | tf_op jit(solution)/shard_map/all_to_all | solution.py:487
  42.4 0.0 collective-permute-done.4.refs_1_
  42.4 0.0 collective-permute-start.6
  42.4 0.7 shard_map.123.cot
  43.1 0.0 collective-permute-done.5.refs_2_
  43.1 1.2 %collective-permute-done.6.refs_3_ = bf16[128,2048]{1,0:T(8,128)(2,1)S(1)} collective-permute-done((bf16[128,2048]{1,0:T(8,128)(2,1)S(1)}, bf16[128,2048]{1,0:T(8,128)(2,1)S(1)}, u32[]{:S(2)}, u32[]{:S(2)}) %collective-permute-start.6) | collective-permute-done | bytes 524320 | tf_op jit(solution)/shard_map/ppermute | solution.py:421
  44.3 1.9 %shard_map.124 = (bf16[4,128,128]{2,1,0:T(8,128)(2,1)S(1)}, bf16[128,2048]{1,0:T(8,128)(2,1)S(1)}, bf16[128,2048]{1,0:T(8,128)(2,1)S(1)}, bf16[128,2048]{1,0:T(8,128)(2,1)}, bf16[128,2048]{1,0:T(8,128)(2,1)S(1)}) custom-call(s32[5]{0:T(128)S(1)} %pad_add_fusion.scalars, bf16[512,128]{1,0:T(8,128)(2,1)S(1)} %bitcast.14, ...), custom_call_target="tpu_custom_call" | custom-call | flops 1024 | bytes 1024 | tf_op jit(solution)/shard_map/pallas_call | solution.py:399
  46.2 0.1 collective-permute-start.9
  46.4 0.4 collective-permute-start.8
  46.7 1.4 %collective-permute-done.9 = bf16[128,2048]{1,0:T(8,128)(2,1)S(1)} collective-permute-done((bf16[128,2048]{1,0:T(8,128)(2,1)S(1)}, bf16[128,2048]{1,0:T(8,128)(2,1)S(1)}, u32[]{:S(2)}, u32[]{:S(2)}) %collective-permute-start.9) | collective-permute-done | bytes 524320 | tf_op jit(solution)/shard_map/ppermute | solution.py:421
  48.1 0.9 add_convert_fusion
  49.1 0.0 copy-start.13
  49.1 1.3 %shard_map.126 = (f32[512,128]{1,0:T(8,128)S(1)}, bf16[512,128]{1,0:T(8,128)(2,1)S(1)}) custom-call(s32[5]{0:T(128)S(1)} %pad_add_fusion.scalars, bf16[128,2048]{1,0:T(8,128)(2,1)S(1)} %shard_map.123.cot, f32[512,128]{1,0:T(8,128)S(1)} %get-tuple-element.28.query_t, bf16[128,2048]{1,0:T(8,128)(2,1)S(1)} %constant_dynamic-update-slice_fusion.refs_0_, ...), custom_call_target="tpu_custom_call" | custom-call | flops 268435456 | bytes 1024 | tf_op jit(solution)/shard_map/pallas_call | solution.py:399
  50.4 0.0 copy-start.7
  50.4 14.2 %all_to_all.20.d_long = bf16[16,32,128]{2,1,0:T(8,128)(2,1)S(1)} all-to-all(bf16[16,32,128]{2,1,0:T(8,128)(2,1)S(1)} %bitcast.20), channel_id=1, replica_groups=mesh['l'=4,'h'=2,'c'=2,'dp'=2] {'l','h','c'}, dimensions={0} | all-to-all | bytes 262144 | tf_op jit(solution)/shard_map/all_to_all | solution.py:487
  64.6 1.9 %shard_map.127 = (bf16[16,32,128]{2,1,0:T(8,128)(2,1)}, bf16[32,2048]{1,0:T(8,128)(2,1)}) custom-call(bf16[16,32,128]{2,1,0:T(8,128)(2,1)S(1)} %all_to_all.20.d_long, f32[544,256]{1,0:T(8,128)S(1)} %copy-done.3, f32[544,256]{1,0:T(8,128)S(1)} %copy-done.15, f32[2,17,128]{2,1,0:T(8,128)S(1)} %copy-done.13, bf16[2,256,256]{2,1,0:T(8,128)(2,1)S(1)} %copy-done.7), custom_call_target="tpu_custom_call" | custom-call | flops 641728512 | bytes 1024 | tf_op jit(solution)/shard_map/pallas_call | solution.py:399
  66.6 3.5 %all-to-all-start.3 = ((bf16[16,32,128]{2,1,0:T(8,128)(2,1)}), bf16[16,32,128]{2,1,0:T(8,128)(2,1)S(1)}, u32[]{:S(2)}, u32[]{:S(2)}) async-start(bf16[16,32,128]{2,1,0:T(8,128)(2,1)} %get-tuple-element.40), calls=%async_computation.3 | async-start | bytes 262144 | tf_op jit(solution)/shard_map/all_to_all | solution.py:487
  70.1 0.0 collective-permute-done.8
  70.1 0.0 collective-permute-done.10
  70.1 0.0 copy-start.11
  70.1 2.1 %add_convert_fusion.4 = (bf16[32,2048]{1,0:T(8,128)(2,1)}, bf16[32,2048]{1,0:T(8,128)(2,1)}, bf16[32,2048]{1,0:T(8,128)(2,1)}) fusion(bf16[128,2048]{1,0:T(8,128)(2,1)} %collective-permute-done.10, bf16[128,2048]{1,0:T(8,128)(2,1)} %collective-permute-done.8, bf16[128,2048]{1,0:T(8,128)(2,1)S(1)} %get-tuple-element.41), kind=kLoop, calls=%fused_computation.6 | loop fusion | flops 1179648 | bytes 1572864 | tf_op jit(solution)/shard_map/convert_element_type | solution.py:558
  72.2 1.8 %collective-permute-start.11 = (bf16[32,2048]{1,0:T(8,128)(2,1)}, bf16[32,2048]{1,0:T(8,128)(2,1)}, u32[]{:S(2)}, u32[]{:S(2)}) collective-permute-start(bf16[32,2048]{1,0:T(8,128)(2,1)} %get-tuple-element.46), channel_id=1, source_target_pairs={{0,8},{8,16},{16,24},{24,0},{1,9},{9,17},{17,25},{25,1},{2,10},{10... | collective-permute-start | bytes 393224 | tf_op jit(solution)/shard_map/ppermute | solution.py:559
  74.0 2.0 %collective-permute-start.13 = (bf16[32,2048]{1,0:T(8,128)(2,1)}, bf16[32,2048]{1,0:T(8,128)(2,1)}, u32[]{:S(2)}, u32[]{:S(2)}) collective-permute-start(bf16[32,2048]{1,0:T(8,128)(2,1)} %get-tuple-element.47), channel_id=1, source_target_pairs={{0,24},{8,0},{16,8},{24,16},{1,25},{9,1},{17,9},{25,17},{2,26},{10... | collective-permute-start | bytes 393224 | tf_op jit(solution)/shard_map/ppermute | solution.py:559
  76.0 1.0 collective-permute-start.12
  77.0 1.5 %shard_map.125 = bf16[128,2048]{1,0:T(8,128)(2,1)} custom-call(bf16[4,128,128]{2,1,0:T(8,128)(2,1)S(1)} %copy-done.11, bf16[128,2048]{1,0:T(8,128)(2,1)S(1)} %constant_dynamic-update-slice_fusion.refs_0_, bf16[128,2048]{1,0:T(8,128)(2,1)S(1)} %collective-permute-done.4.refs_1_, bf16[128,2048]{1,0:T(8,128)(2,1)S(1)} %collective-permute-done.5.refs_2_, ...), custom_call_target="tpu_custom_call" | custom-call | flops 268435456 | bytes 1024 | tf_op jit(solution)/shard_map/pallas_call | solution.py:399
  78.5 1.5 %collective-permute-start.15 = (bf16[32,2048]{1,0:T(8,128)(2,1)}, bf16[32,2048]{1,0:T(8,128)(2,1)S(1)}, u32[]{:S(2)}, u32[]{:S(2)}) collective-permute-start(bf16[32,2048]{1,0:T(8,128)(2,1)} %get-tuple-element.45), channel_id=1, source_target_pairs={{0,1},{1,0},{2,3},{3,2},{4,5},{5,4},{6,7},{7,6},{8,9},{9,8},{10,11... | collective-permute-start | bytes 393224 | tf_op jit(solution)/shard_map/ppermute | solution.py:421
  80.0 0.0 all-to-all-done.3
  80.0 0.7 copy-done.9
  80.7 0.7 shard_map.128
  81.4 1.3 %collective-permute-start.7 = (f32[2,1536]{1,0:T(2,128)S(1)}, f32[2,1536]{1,0:T(2,128)S(1)}, u32[]{:S(2)}, u32[]{:S(2)}) collective-permute-start(f32[2,1536]{1,0:T(2,128)S(1)} %slice.56), channel_id=1, source_target_pairs={{2,0},{4,2},{6,4},{8,6},{10,8},{12,10},{14,12},{16,14},{18,16},{20... | collective-permute-start | bytes 36872 | tf_op jit(solution)/shard_map/ppermute | solution.py:577
  82.7 5.8 %collective-permute-done.12 = bf16[32,2048]{1,0:T(8,128)(2,1)} collective-permute-done((bf16[32,2048]{1,0:T(8,128)(2,1)}, bf16[32,2048]{1,0:T(8,128)(2,1)}, u32[]{:S(2)}, u32[]{:S(2)}) %collective-permute-start.12) | collective-permute-done | bytes 131104 | tf_op jit(solution)/shard_map/ppermute | solution.py:559
  88.5 1.3 %add_convert_fusion.1 = bf16[32,2048]{1,0:T(8,128)(2,1)S(1)} fusion(bf16[32,2048]{1,0:T(8,128)(2,1)} %collective-permute-done.13, bf16[32,2048]{1,0:T(8,128)(2,1)} %collective-permute-done.12, bf16[32,2048]{1,0:T(8,128)(2,1)} %collective-permute-done.11, bf16[128,2048]{1,0:T(8,128)(2,1)} %collective-permute-done.10, ...), kind=kLoop, calls=%fused_computation.3 | loop fusion | flops 786432 | bytes 917504 | tf_op jit(solution)/shard_map/convert_element_type | solution.py:560
  89.8 1.5 %collective-permute-start.14 = (bf16[32,2048]{1,0:T(8,128)(2,1)S(1)}, bf16[32,2048]{1,0:T(8,128)(2,1)S(1)}, u32[]{:S(2)}, u32[]{:S(2)}) collective-permute-start(bf16[32,2048]{1,0:T(8,128)(2,1)S(1)} %add_convert_fusion.1), channel_id=1, source_target_pairs={{0,1},{1,0},{2,3},{3,2},{4,5},{5,4},{6,7},{7,6},{8,9},{9,8},{10,11... | collective-permute-start | bytes 393224 | tf_op jit(solution)/shard_map/ppermute | solution.py:421
  91.3 1.6 %convert_add_fusion = f32[32,2048]{1,0:T(8,128)} fusion(bf16[32,2048]{1,0:T(8,128)(2,1)S(1)} %collective-permute-done.15, bf16[32,2048]{1,0:T(8,128)(2,1)} %get-tuple-element.45), kind=kLoop, calls=%fused_computation.1 | loop fusion | flops 196608 | bytes 524288 | tf_op jit(solution)/shard_map/add | solution.py:426
  92.9 1.9 %shard_map.129 = bf16[128,1536]{1,0:T(8,128)(2,1)} custom-call(s32[5]{0:T(128)S(1)} %pad_add_fusion.scalars, bf16[128,1536]{1,0:T(8,128)(2,1)S(1)} %bitcast.13, bf16[2,1536]{1,0:T(2,128)(2,1)S(1)} %collective-permute-done.earlier, f32[3,1536]{1,0:T(4,128)S(1)} %copy-done.9, f32[512,128]{1,0:T(8,128)S(1)} %get-tuple-element.37.d_product_t, ...), custom_call_target="tpu_custom_call" | custom-call | flops 1048576 | bytes 1024 | tf_op jit(solution)/shard_map/pallas_call | solution.py:399
  94.9 0.4 collective-permute-done.14
  95.3 0.7 convert_add_fusion.1
  (35 shorter events, 0.1 us)
Async XLA Ops:
  0.6 12.7 %copy-start.8 = (f32[3,1536]{1,0:T(4,128)S(1)}, f32[3,1536]{1,0:T(4,128)}, u32[]{:S(2)}) copy-start(f32[3,1536]{1,0:T(4,128)} %taps.3) | copy-start | bytes 55300
  1.4 3.2 %collective-permute-start = (bf16[2,1536]{1,0:T(2,128)(2,1)S(1)}, bf16[2,1536]{1,0:T(2,128)(2,1)S(1)}, u32[]{:S(2)}, u32[]{:S(2)}) collective-permute-start(bf16[2,1536]{1,0:T(2,128)(2,1)S(1)} %slice_bitcast_fusion), channel_id=1, source_target_pairs={{0,2},{2,4},{4,6},{6,8},{8,10},{10,12},{12,14},{14,16},{16,18},{18... | collective-permute-start | bytes 18440 | tf_op jit(solution)/shard_map/ppermute | solution.py:454
  3.8 0.7 copy-start.17
  3.8 0.7 copy-start.18
  4.6 18.7 %collective-permute-start.3 = (bf16[32,2048]{1,0:T(8,128)(2,1)}, bf16[32,2048]{1,0:T(8,128)(2,1)S(1)}, u32[]{:S(2)}, u32[]{:S(2)}) collective-permute-start(bf16[32,2048]{1,0:T(8,128)(2,1)} %param.12), channel_id=1, source_target_pairs={{0,24},{8,0},{16,8},{24,16},{1,25},{9,1},{17,9},{25,17},{2,26},{10... | collective-permute-start | bytes 393224 | tf_op jit(solution)/shard_map/ppermute | solution.py:436
  12.3 10.9 %collective-permute-start.2 = (bf16[32,2048]{1,0:T(8,128)(2,1)}, bf16[32,2048]{1,0:T(8,128)(2,1)S(1)}, u32[]{:S(2)}, u32[]{:S(2)}) collective-permute-start(bf16[32,2048]{1,0:T(8,128)(2,1)} %param.12), channel_id=1, source_target_pairs={{0,16},{8,24},{16,0},{24,8},{1,17},{9,25},{17,1},{25,9},{2,18},{10... | collective-permute-start | bytes 393224 | tf_op jit(solution)/shard_map/ppermute | solution.py:436
  12.3 10.9 %collective-permute-start.1 = (bf16[32,2048]{1,0:T(8,128)(2,1)}, bf16[32,2048]{1,0:T(8,128)(2,1)S(1)}, u32[]{:S(2)}, u32[]{:S(2)}) collective-permute-start(bf16[32,2048]{1,0:T(8,128)(2,1)} %param.12), channel_id=1, source_target_pairs={{0,8},{8,16},{16,24},{24,0},{1,9},{9,17},{17,25},{25,1},{2,10},{10... | collective-permute-start | bytes 393224 | tf_op jit(solution)/shard_map/ppermute | solution.py:436
  13.3 1.0 %copy-start = (bf16[1,128,1536]{2,1,0:T(8,128)(2,1)S(1)}, bf16[1,128,1536]{2,1,0:T(8,128)(2,1)}, u32[]{:S(2)}) copy-start(bf16[1,128,1536]{2,1,0:T(8,128)(2,1)} %param.9) | copy-start | bytes 1179652
  14.3 6.1 %copy-start.5 = (f32[32,2048]{1,0:T(8,128)S(1)}, f32[32,2048]{1,0:T(8,128)}, u32[]{:S(2)}) copy-start(f32[32,2048]{1,0:T(8,128)} %filt) | copy-start | bytes 786436
  14.3 6.1 %copy-start.6 = (bf16[2,256,256]{2,1,0:T(8,128)(2,1)S(1)}, bf16[2,256,256]{2,1,0:T(8,128)(2,1)}, u32[]{:S(2)}) copy-start(bf16[2,256,256]{2,1,0:T(8,128)(2,1)} %constant.25.clone.matrix) | copy-start | bytes 786436
  16.1 4.3 %copy-start.12 = (f32[2,17,128]{2,1,0:T(8,128)S(1)}, f32[2,17,128]{2,1,0:T(8,128)}, u32[]{:S(2)}) copy-start(f32[2,17,128]{2,1,0:T(8,128)} %constant.24.clone.twist) | copy-start | bytes 52228
  16.1 12.2 %all-to-all-start = ((bf16[16,32,128]{2,1,0:T(8,128)(2,1)}), bf16[16,32,128]{2,1,0:T(8,128)(2,1)S(1)}, u32[]{:S(2)}, u32[]{:S(2)}) async-start(bf16[16,32,128]{2,1,0:T(8,128)(2,1)} %bitcast.3), calls=%async_computation | async-start | bytes 262144 | tf_op jit(solution)/shard_map/all_to_all | solution.py:487
  20.4 0.9 copy-start.16
  21.3 8.8 %copy-start.2 = (f32[544,256]{1,0:T(8,128)}, f32[544,256]{1,0:T(8,128)S(1)}, u32[]{:S(2)}) copy-start(f32[544,256]{1,0:T(8,128)S(1)} %shard_map.121.filt_spec) | copy-start | bytes 1671172
  23.3 19.1 %collective-permute-start.4 = (bf16[128,2048]{1,0:T(8,128)(2,1)S(1)}, bf16[128,2048]{1,0:T(8,128)(2,1)S(1)}, u32[]{:S(2)}, u32[]{:S(2)}) collective-permute-start(bf16[128,2048]{1,0:T(8,128)(2,1)S(1)} %constant_dynamic-update-slice_fusion.refs_0_), channel_id=1, source_target_pairs={{0,4},{4,0},{1,5},{5,1},{2,6},{6,2},{3,7},{7,3},{8,12},{12,8},{9,1... | collective-permute-start | bytes 1572872 | tf_op jit(solution)/shard_map/ppermute | solution.py:421
  28.3 14.1 %copy-start.4 = (bf16[1,128,2048]{2,1,0:T(8,128)(2,1)S(1)}, bf16[1,128,2048]{2,1,0:T(8,128)(2,1)}, u32[]{:S(2)}) copy-start(bf16[1,128,2048]{2,1,0:T(8,128)(2,1)} %param.13) | copy-start | bytes 1572868
  30.1 0.8 copy-start.14
  31.0 11.4 %all-to-all-start.1 = ((bf16[16,32,128]{2,1,0:T(8,128)(2,1)}), bf16[16,32,128]{2,1,0:T(8,128)(2,1)S(1)}, u32[]{:S(2)}, u32[]{:S(2)}) async-start(bf16[16,32,128]{2,1,0:T(8,128)(2,1)} %get-tuple-element.27), calls=%async_computation.1 | async-start | bytes 262144 | tf_op jit(solution)/shard_map/all_to_all | solution.py:487
  34.5 8.6 %collective-permute-start.5 = (bf16[128,2048]{1,0:T(8,128)(2,1)S(1)}, bf16[128,2048]{1,0:T(8,128)(2,1)S(1)}, u32[]{:S(2)}, u32[]{:S(2)}) collective-permute-start(bf16[128,2048]{1,0:T(8,128)(2,1)S(1)} %constant_dynamic-update-slice_fusion.refs_0_), channel_id=1, source_target_pairs={{0,2},{2,0},{1,3},{3,1},{4,6},{6,4},{5,7},{7,5},{8,10},{10,8},{9,1... | collective-permute-start | bytes 1572872 | tf_op jit(solution)/shard_map/ppermute | solution.py:421
  42.4 1.9 %collective-permute-start.6 = (bf16[128,2048]{1,0:T(8,128)(2,1)S(1)}, bf16[128,2048]{1,0:T(8,128)(2,1)S(1)}, u32[]{:S(2)}, u32[]{:S(2)}) collective-permute-start(bf16[128,2048]{1,0:T(8,128)(2,1)S(1)} %collective-permute-done.4.refs_1_), channel_id=1, source_target_pairs={{0,2},{2,0},{1,3},{3,1},{4,6},{6,4},{5,7},{7,5},{8,10},{10,8},{9,1... | collective-permute-start | bytes 1572872 | tf_op jit(solution)/shard_map/ppermute | solution.py:421
  46.2 2.8 %copy-start.10 = (bf16[4,128,128]{2,1,0:T(8,128)(2,1)}, bf16[4,128,128]{2,1,0:T(8,128)(2,1)S(1)}, u32[]{:S(2)}) copy-start(bf16[4,128,128]{2,1,0:T(8,128)(2,1)S(1)} %get-tuple-element.36.product) | copy-start | bytes 393220
  46.2 1.9 %collective-permute-start.9 = (bf16[128,2048]{1,0:T(8,128)(2,1)S(1)}, bf16[128,2048]{1,0:T(8,128)(2,1)S(1)}, u32[]{:S(2)}, u32[]{:S(2)}) collective-permute-start(bf16[128,2048]{1,0:T(8,128)(2,1)S(1)} %get-tuple-element.44), channel_id=1, source_target_pairs={{0,2},{2,0},{1,3},{3,1},{4,6},{6,4},{5,7},{7,5},{8,10},{10,8},{9,1... | collective-permute-start | bytes 1572872 | tf_op jit(solution)/shard_map/ppermute | solution.py:421
  46.4 23.7 %collective-permute-start.8 = (bf16[128,2048]{1,0:T(8,128)(2,1)}, bf16[128,2048]{1,0:T(8,128)(2,1)}, u32[]{:S(2)}, u32[]{:S(2)}) collective-permute-start(bf16[128,2048]{1,0:T(8,128)(2,1)} %get-tuple-element.42), channel_id=1, source_target_pairs={{0,2},{2,0},{1,3},{3,1},{4,6},{6,4},{5,7},{7,5},{8,10},{10,8},{9,1... | collective-permute-start | bytes 1572872 | tf_op jit(solution)/shard_map/ppermute | solution.py:421
  49.1 15.5 %copy-start.3 = (f32[544,256]{1,0:T(8,128)S(1)}, f32[544,256]{1,0:T(8,128)}, u32[]{:S(2)}) copy-start(f32[544,256]{1,0:T(8,128)} %copy-done.2) | copy-start | bytes 1671172
  49.1 15.5 %copy-start.15 = (f32[544,256]{1,0:T(8,128)S(1)}, f32[544,256]{1,0:T(8,128)}, u32[]{:S(2)}) copy-start(f32[544,256]{1,0:T(8,128)} %copy-done.14) | copy-start | bytes 1671172
  49.1 21.0 %collective-permute-start.10 = (bf16[128,2048]{1,0:T(8,128)(2,1)}, bf16[128,2048]{1,0:T(8,128)(2,1)}, u32[]{:S(2)}, u32[]{:S(2)}) collective-permute-start(bf16[128,2048]{1,0:T(8,128)(2,1)} %add_convert_fusion), channel_id=1, source_target_pairs={{0,4},{4,0},{1,5},{5,1},{2,6},{6,2},{3,7},{7,3},{8,12},{12,8},{9,1... | collective-permute-start | bytes 1572872 | tf_op jit(solution)/shard_map/ppermute | solution.py:421
  49.1 15.5 %copy-start.13 = (f32[2,17,128]{2,1,0:T(8,128)S(1)}, f32[2,17,128]{2,1,0:T(8,128)}, u32[]{:S(2)}) copy-start(f32[2,17,128]{2,1,0:T(8,128)} %constant.24.clone.twist) | copy-start | bytes 52228
  50.4 14.2 %copy-start.7 = (bf16[2,256,256]{2,1,0:T(8,128)(2,1)S(1)}, bf16[2,256,256]{2,1,0:T(8,128)(2,1)}, u32[]{:S(2)}) copy-start(bf16[2,256,256]{2,1,0:T(8,128)(2,1)} %constant.25.clone.matrix) | copy-start | bytes 786436
  66.6 13.4 %all-to-all-start.3 = ((bf16[16,32,128]{2,1,0:T(8,128)(2,1)}), bf16[16,32,128]{2,1,0:T(8,128)(2,1)S(1)}, u32[]{:S(2)}, u32[]{:S(2)}) async-start(bf16[16,32,128]{2,1,0:T(8,128)(2,1)} %get-tuple-element.40), calls=%async_computation.3 | async-start | bytes 262144 | tf_op jit(solution)/shard_map/all_to_all | solution.py:487
  70.1 6.9 %copy-start.11 = (bf16[4,128,128]{2,1,0:T(8,128)(2,1)S(1)}, bf16[4,128,128]{2,1,0:T(8,128)(2,1)}, u32[]{:S(2)}) copy-start(bf16[4,128,128]{2,1,0:T(8,128)(2,1)} %copy-done.10) | copy-start | bytes 393220
  72.2 10.5 %collective-permute-start.11 = (bf16[32,2048]{1,0:T(8,128)(2,1)}, bf16[32,2048]{1,0:T(8,128)(2,1)}, u32[]{:S(2)}, u32[]{:S(2)}) collective-permute-start(bf16[32,2048]{1,0:T(8,128)(2,1)} %get-tuple-element.46), channel_id=1, source_target_pairs={{0,8},{8,16},{16,24},{24,0},{1,9},{9,17},{17,25},{25,1},{2,10},{10... | collective-permute-start | bytes 393224 | tf_op jit(solution)/shard_map/ppermute | solution.py:559
  74.0 8.7 %collective-permute-start.13 = (bf16[32,2048]{1,0:T(8,128)(2,1)}, bf16[32,2048]{1,0:T(8,128)(2,1)}, u32[]{:S(2)}, u32[]{:S(2)}) collective-permute-start(bf16[32,2048]{1,0:T(8,128)(2,1)} %get-tuple-element.47), channel_id=1, source_target_pairs={{0,24},{8,0},{16,8},{24,16},{1,25},{9,1},{17,9},{25,17},{2,26},{10... | collective-permute-start | bytes 393224 | tf_op jit(solution)/shard_map/ppermute | solution.py:559
  76.0 12.5 %collective-permute-start.12 = (bf16[32,2048]{1,0:T(8,128)(2,1)}, bf16[32,2048]{1,0:T(8,128)(2,1)}, u32[]{:S(2)}, u32[]{:S(2)}) collective-permute-start(bf16[32,2048]{1,0:T(8,128)(2,1)} %get-tuple-element.48), channel_id=1, source_target_pairs={{0,16},{8,24},{16,0},{24,8},{1,17},{9,25},{17,1},{25,9},{2,18},{10... | collective-permute-start | bytes 393224 | tf_op jit(solution)/shard_map/ppermute | solution.py:559
  77.0 3.0 %copy-start.1 = (bf16[1,128,1536]{2,1,0:T(8,128)(2,1)S(1)}, bf16[1,128,1536]{2,1,0:T(8,128)(2,1)}, u32[]{:S(2)}) copy-start(bf16[1,128,1536]{2,1,0:T(8,128)(2,1)} %param.9) | copy-start | bytes 1179652
  78.5 12.8 %collective-permute-start.15 = (bf16[32,2048]{1,0:T(8,128)(2,1)}, bf16[32,2048]{1,0:T(8,128)(2,1)S(1)}, u32[]{:S(2)}, u32[]{:S(2)}) collective-permute-start(bf16[32,2048]{1,0:T(8,128)(2,1)} %get-tuple-element.45), channel_id=1, source_target_pairs={{0,1},{1,0},{2,3},{3,2},{4,5},{5,4},{6,7},{7,6},{8,9},{9,8},{10,11... | collective-permute-start | bytes 393224 | tf_op jit(solution)/shard_map/ppermute | solution.py:421
  80.0 0.7 copy-start.9
  81.4 11.5 %collective-permute-start.7 = (f32[2,1536]{1,0:T(2,128)S(1)}, f32[2,1536]{1,0:T(2,128)S(1)}, u32[]{:S(2)}, u32[]{:S(2)}) collective-permute-start(f32[2,1536]{1,0:T(2,128)S(1)} %slice.56), channel_id=1, source_target_pairs={{2,0},{4,2},{6,4},{8,6},{10,8},{12,10},{14,12},{16,14},{18,16},{20... | collective-permute-start | bytes 36872 | tf_op jit(solution)/shard_map/ppermute | solution.py:577
  89.8 5.5 %collective-permute-start.14 = (bf16[32,2048]{1,0:T(8,128)(2,1)S(1)}, bf16[32,2048]{1,0:T(8,128)(2,1)S(1)}, u32[]{:S(2)}, u32[]{:S(2)}) collective-permute-start(bf16[32,2048]{1,0:T(8,128)(2,1)S(1)} %add_convert_fusion.1), channel_id=1, source_target_pairs={{0,1},{1,0},{2,3},{3,2},{4,5},{5,4},{6,7},{7,6},{8,9},{9,8},{10,11... | collective-permute-start | bytes 393224 | tf_op jit(solution)/shard_map/ppermute | solution.py:421

commit v2 on v1

--- a/solution.py
+++ b/solution.py
@@ -15,7 +15,7 @@
 F32 = jnp.float32
 BF16 = jnp.bfloat16
 LANES = 128
-VMEM_LIMIT = 20 << 20
+VMEM_LIMIT = 8 << 20
 SMEM = pl.BlockSpec(memory_space=pltpu.SMEM)
 HBM = pl.BlockSpec(memory_space=pltpu.HBM)
 
@@ -225,17 +225,7 @@
     return mixed
 
 
-def prep_kernel(
-    scalars, proj_far, earlier, taps_far, gated_t, query_t, proj, taps, done, *, width, split
-):
-    copies = [
-        pltpu.make_async_copy(proj_far, proj, done.at[0]),
-        pltpu.make_async_copy(taps_far, taps, done.at[1]),
-    ]
-    for copy in copies:
-        copy.start()
-    for copy in copies:
-        copy.wait()
+def prep_kernel(scalars, proj, earlier, taps, gated_t, query_t, *, width, split):
     room = room_left(scalars, split, proj.shape[0])
     query, key, value = (
         mixed_stream(stream, proj, earlier, taps, room, width) for stream in range(3)
@@ -466,12 +456,6 @@
         [(flat, BF16), (flat, F32)],
         inputs,
         1,
-        far=(1, 3),
-        scratch=[
-            pltpu.VMEM((rows, 3 * width), BF16),
-            pltpu.VMEM(short_filter.shape, F32),
-            pltpu.SemaphoreType.DMA((2,)),
-        ],
         flops=1 << 20,
     )
 
@@ -528,7 +512,7 @@
     product, *sums = call(
         functools.partial(partial_kernel, split=split, scale=grad_scale, tile=512),
         [((4, rows, lines * chans), BF16)] + [(part, BF16)] * (4 * CHUNKS),
-        (scalars, long_t, query_t, after(cot, *weights)),
+        (scalars, long_t, query_t, after(cot, d_long_t)),
         1,
         scratch=[pltpu.VMEM(flat, F32)],
         flops=1024,
@@ -540,32 +524,30 @@
         scratch=[work, signal, work],
         flops=3 * fft_flops,
     )
-    d_gated_t = exchange(d_gated_cols).reshape(flat)
-    d_filter = dp_sum(filter_part)
-
-    d_wout = []
-    for chunk in range(CHUNKS):
-        near_sum, over_sum, near_send, over_send = sums[chunk::CHUNKS]
-        over_core, near_core = swap(over_send, "c"), swap(near_send, "c")
-        over_sum = over_sum.astype(F32) + over_core.astype(F32)
-        got = swap(over_sum.astype(BF16), "h")
-        total = [
-            near_sum[at].astype(F32) + near_core[at].astype(F32) + got[at].astype(F32)
-            for at in (slice(i * chans, (i + 1) * chans) for i in range(lines))
-        ]
-        total_here = total[0]
-        for step in range(1, lines):
-            sent = total[lines - step].astype(BF16)
-            total_here += lax.ppermute(sent, "l", line_route(lines, step)).astype(F32)
-        d_wout.append(dp_sum(total_here.astype(BF16)))
-    d_wout = jnp.concatenate(d_wout, axis=1)
-
     (output,) = call(
         functools.partial(output_kernel, tile=512),
         [((rows, features), BF16)],
         (product, *weights),
         flops=2 * rows * width * features,
     )
+
+    near_sum, over_sum, near_send, over_send = sums
+    over_core, near_core = swap(over_send, "c"), swap(near_send, "c")
+    over_sum = over_sum.astype(F32) + after(over_core, output).astype(F32)
+    got = after(swap(over_sum.astype(BF16), "h"), filter_part)
+    total = [
+        near_sum[at].astype(F32) + near_core[at].astype(F32) + got[at].astype(F32)
+        for at in (slice(i * chans, (i + 1) * chans) for i in range(lines))
+    ]
+    sent = [total[lines - step].astype(BF16) for step in range(1, lines)]
+    d_filter = dp_sum(filter_part)
+    total_here = total[0]
+    for step, block in enumerate(sent, 1):
+        got = after(lax.ppermute(block, "l", line_route(lines, step)), d_filter)
+        total_here += got.astype(F32)
+    d_wout = dp_sum(total_here.astype(BF16))
+
+    d_gated_t = exchange(after(d_gated_cols, *sent)).reshape(flat)
 
     (head,) = call(
         functools.partial(head_kernel, width=width, split=split),

time: 96.7 us -> 92.8 us (0.960)
  other arithmetic: 6.72 us -> 2.88 us
  starting transfers between devices: 33 us -> 30 us
  waiting for transfers between devices: 22.6 us -> 25.3 us
    convert_element_type x3, other arithmetic: 4.28 us -> 1.35 us  [the longest x1 1.07 us: per_device(): d_wout = dp_sum(total_here.astype(BF16))]
    ppermute x3, starting transfers between devices: 4.77 us -> 2.36 us  [per_device(): got = after(lax.ppermute(block, 'l', line_route(lines, step)), d_filter)]
    ppermute x1, waiting for transfers between devices: 0.01 us -> 1.77 us  [per_device(): later = lax.ppermute(head[:2], axes, [(j, i) for i, j in route])]
    ppermute x3, waiting for transfers between devices: 5.78 us -> 7.53 us  [per_device(): got = after(lax.ppermute(block, 'l', line_route(lines, step)), d_filter)]
    unnamed x41 -> x33, local copies, waits for them, and re-layouts: 3.76 us -> 3.77 us
  transfers between devices with their start and end apart: 19 -> 19, of which waited for: 7 -> 8; matrix products, arithmetic and copies ran while one was open for 6% -> 2% of each run, Pallas kernels for 13% -> 11%
where the time goes in v2:
time: 92.8 us; the launch traced here: 91.8 us
  starting transfers between devices  30 us (32%)
  waiting for transfers between devices  25.3 us (27%)
  blocking collectives  15.1 us (16%)
  Pallas kernels  13.1 us (14%)
  local copies, waits for them, and re-layouts  4.54 us (5%)
  other arithmetic  2.88 us (3%)
    all_to_all x1, blocking collectives, exchange(): return lax.all_to_all(block, axes, 0, 0, tiled=True)  15.1 us
    pallas_call x10, Pallas kernels, call(): pl.pallas_call(kernel, grid=(1,), out_shape=out_shape, in_specs=[SMEM if...  13.1 us
    all_to_all x3, waiting for transfers between devices, exchange(): return lax.all_to_all(block, axes, 0, 0, tiled=True)  11.8 us
    all_to_all x3, starting transfers between devices, exchange(): return lax.all_to_all(block, axes, 0, 0, tiled=True)  11.7 us
    ppermute x3, starting transfers between devices, along_line(): lax.ppermute(block, 'l', line_route(lines, step))  8.74 us
    ppermute x3, waiting for transfers between devices, per_device(): got = after(lax.ppermute(block, 'l', line_route(lines, step)), d_filter)  7.53 us
    unnamed x33, local copies, waits for them, and re-layouts  3.77 us
    ppermute x8, starting transfers between devices, swap(): return lax.ppermute(block, axis, SWAP)  3.62 us
  transfers between devices with their start and end apart: 19, of which 8 were waited for; matrix products, arithmetic and copies ran while one was open for 2% of the time, Pallas kernels for 11%

profile of v2, /device:TPU:0, one launch (start us, length us, event | category | flops | bytes accessed | tf_op | source)
XLA Modules:
  0.0 91.8 jit_solution(2510814385483399389)
XLA Ops:
  0.6 0.8 slice_bitcast_fusion
  1.4 2.4 %collective-permute-start = (bf16[2,1536]{1,0:T(2,128)(2,1)S(1)}, bf16[2,1536]{1,0:T(2,128)(2,1)S(1)}, u32[]{:S(2)}, u32[]{:S(2)}) collective-permute-start(bf16[2,1536]{1,0:T(2,128)(2,1)S(1)} %slice_bitcast_fusion), channel_id=1, source_target_pairs={{0,2},{2,4},{4,6},{6,8},{8,10},{10,12},{12,14},{14,16},{16,18},{18... | collective-permute-start | bytes 18440 | tf_op jit(solution)/shard_map/ppermute | solution.py:444
  3.8 0.0 copy-start.13
  3.8 0.0 copy-start.14
  3.8 0.6 copy-done.13
  4.4 0.0 copy-done.14
  4.4 0.1 pad_add_fusion.scalars
  4.5 0.0 collective-permute-done.earlier
  4.6 7.7 %collective-permute-start.3 = (bf16[32,2048]{1,0:T(8,128)(2,1)}, bf16[32,2048]{1,0:T(8,128)(2,1)S(1)}, u32[]{:S(2)}, u32[]{:S(2)}) collective-permute-start(bf16[32,2048]{1,0:T(8,128)(2,1)} %param.12), channel_id=1, source_target_pairs={{0,24},{8,0},{16,8},{24,16},{1,25},{9,1},{17,9},{25,17},{2,26},{10... | collective-permute-start | bytes 393224 | tf_op jit(solution)/shard_map/ppermute | solution.py:426
  12.3 0.0 collective-permute-start.2
  12.3 1.0 %collective-permute-start.1 = (bf16[32,2048]{1,0:T(8,128)(2,1)}, bf16[32,2048]{1,0:T(8,128)(2,1)S(1)}, u32[]{:S(2)}, u32[]{:S(2)}) collective-permute-start(bf16[32,2048]{1,0:T(8,128)(2,1)} %param.12), channel_id=1, source_target_pairs={{0,8},{8,16},{16,24},{24,0},{1,9},{9,17},{17,25},{25,1},{2,10},{10... | collective-permute-start | bytes 393224 | tf_op jit(solution)/shard_map/ppermute | solution.py:426
  13.3 1.0 %copy-done = bf16[1,128,1536]{2,1,0:T(8,128)(2,1)S(1)} copy-done((bf16[1,128,1536]{2,1,0:T(8,128)(2,1)S(1)}, bf16[1,128,1536]{2,1,0:T(8,128)(2,1)}, u32[]{:S(2)}) %copy-start) | copy-done | bytes 393240
  14.3 1.6 %shard_map.120 = (bf16[512,128]{1,0:T(8,128)(2,1)}, f32[512,128]{1,0:T(8,128)S(1)}) custom-call(s32[5]{0:T(128)S(1)} %pad_add_fusion.scalars, bf16[128,1536]{1,0:T(8,128)(2,1)S(1)} %bitcast.11, bf16[2,1536]{1,0:T(2,128)(2,1)S(1)} %collective-permute-done.earlier, f32[3,1536]{1,0:T(4,128)S(1)} %copy-done.6), custom_call_target="tpu_custom_call" | custom-call | flops 1048576 | bytes 1024 | tf_op jit(solution)/shard_map/pallas_call | solution.py:389
  15.9 4.4 %all-to-all-start = ((bf16[16,32,128]{2,1,0:T(8,128)(2,1)}), bf16[16,32,128]{2,1,0:T(8,128)(2,1)S(1)}, u32[]{:S(2)}, u32[]{:S(2)}) async-start(bf16[16,32,128]{2,1,0:T(8,128)(2,1)} %bitcast.3), calls=%async_computation | async-start | bytes 262144 | tf_op jit(solution)/shard_map/all_to_all | solution.py:471
  20.3 0.0 copy-start.12
  20.3 0.5 shard_map.121.filt_spec
  20.7 0.4 copy-done.12
  21.2 2.0 %collective-permute-done.2 = bf16[32,2048]{1,0:T(8,128)(2,1)S(1)} collective-permute-done((bf16[32,2048]{1,0:T(8,128)(2,1)}, bf16[32,2048]{1,0:T(8,128)(2,1)S(1)}, u32[]{:S(2)}, u32[]{:S(2)}) %collective-permute-start.2) | collective-permute-done | bytes 131104 | tf_op jit(solution)/shard_map/ppermute | solution.py:426
  23.2 0.0 collective-permute-done.1
  23.2 0.0 collective-permute-done.3
  23.3 0.8 collective-permute-start.4
  24.0 4.1 %all-to-all-done.gated = bf16[16,32,128]{2,1,0:T(8,128)(2,1)S(1)} async-done(((bf16[16,32,128]{2,1,0:T(8,128)(2,1)}), bf16[16,32,128]{2,1,0:T(8,128)(2,1)S(1)}, u32[]{:S(2)}, u32[]{:S(2)}) %all-to-all-start) | async-done | bytes 131104 | tf_op jit(solution)/shard_map/all_to_all | solution.py:471
  28.2 1.8 %shard_map.122 = (bf16[16,32,128]{2,1,0:T(8,128)(2,1)}, f32[544,256]{1,0:T(8,128)S(1)}) custom-call(bf16[16,32,128]{2,1,0:T(8,128)(2,1)S(1)} %all-to-all-done.gated, f32[544,256]{1,0:T(8,128)S(1)} %shard_map.121.filt_spec, f32[2,17,128]{2,1,0:T(8,128)S(1)} %copy-done.7, bf16[2,256,256]{2,1,0:T(8,128)(2,1)S(1)} %copy-done.4), custom_call_target="tpu_custom_call" | custom-call | flops 32212254720 | bytes 1024 | tf_op jit(solution)/shard_map/pallas_call | solution.py:389
  30.0 0.8 copy-done.8
  30.8 3.5 %all-to-all-start.1 = ((bf16[16,32,128]{2,1,0:T(8,128)(2,1)}), bf16[16,32,128]{2,1,0:T(8,128)(2,1)S(1)}, u32[]{:S(2)}, u32[]{:S(2)}) async-start(bf16[16,32,128]{2,1,0:T(8,128)(2,1)} %get-tuple-element.33), calls=%async_computation.1 | async-start | bytes 262144 | tf_op jit(solution)/shard_map/all_to_all | solution.py:471
  34.3 0.3 collective-permute-start.5
  34.6 7.6 %all-to-all-done.1 = bf16[16,32,128]{2,1,0:T(8,128)(2,1)S(1)} async-done(((bf16[16,32,128]{2,1,0:T(8,128)(2,1)}), bf16[16,32,128]{2,1,0:T(8,128)(2,1)S(1)}, u32[]{:S(2)}, u32[]{:S(2)}) %all-to-all-start.1) | async-done | bytes 131104 | tf_op jit(solution)/shard_map/all_to_all | solution.py:471
  42.2 0.0 collective-permute-done.4.refs_1_
  42.2 0.0 collective-permute-start.6
  42.3 0.7 shard_map.123.cot
  43.0 1.2 %collective-permute-done.6.refs_3_ = bf16[128,2048]{1,0:T(8,128)(2,1)S(1)} collective-permute-done((bf16[128,2048]{1,0:T(8,128)(2,1)S(1)}, bf16[128,2048]{1,0:T(8,128)(2,1)S(1)}, u32[]{:S(2)}, u32[]{:S(2)}) %collective-permute-start.6) | collective-permute-done | bytes 524320 | tf_op jit(solution)/shard_map/ppermute | solution.py:411
  44.2 1.3 %shard_map.124 = (f32[512,128]{1,0:T(8,128)S(1)}, bf16[512,128]{1,0:T(8,128)(2,1)S(1)}) custom-call(s32[5]{0:T(128)S(1)} %pad_add_fusion.scalars, bf16[128,2048]{1,0:T(8,128)(2,1)S(1)} %shard_map.123.cot, f32[512,128]{1,0:T(8,128)S(1)} %get-tuple-element.34.query_t, bf16[128,2048]{1,0:T(8,128)(2,1)S(1)} %constant_dynamic-update-slice_fusion.refs_0_, ...), custom_call_target="tpu_custom_call" | custom-call | flops 268435456 | bytes 1024 | tf_op jit(solution)/shard_map/pallas_call | solution.py:389
  45.4 1.3 %shard_map.125 = (bf16[4,128,128]{2,1,0:T(8,128)(2,1)S(1)}, bf16[128,2048]{1,0:T(8,128)(2,1)S(1)}, bf16[128,2048]{1,0:T(8,128)(2,1)S(1)}, bf16[128,2048]{1,0:T(8,128)(2,1)S(1)}, bf16[128,2048]{1,0:T(8,128)(2,1)S(1)}) custom-call(s32[5]{0:T(128)S(1)} %pad_add_fusion.scalars, bf16[512,128]{1,0:T(8,128)(2,1)S(1)} %bitcast.14, ...), custom_call_target="tpu_custom_call" | custom-call | flops 1024 | bytes 1024 | tf_op jit(solution)/shard_map/pallas_call | solution.py:389
  46.7 0.2 collective-permute-start.8
  46.9 1.5 %shard_map.126 = bf16[128,2048]{1,0:T(8,128)(2,1)} custom-call(bf16[4,128,128]{2,1,0:T(8,128)(2,1)S(1)} %get-tuple-element.43.product, bf16[128,2048]{1,0:T(8,128)(2,1)S(1)} %constant_dynamic-update-slice_fusion.refs_0_, bf16[128,2048]{1,0:T(8,128)(2,1)S(1)} %collective-permute-done.4.refs_1_, bf16[128,2048]{1,0:T(8,128)(2,1)S(1)} %collective-permute-done.5.refs_2_, ...), custom_call_target="tpu_custom_call" | custom-call | flops 268435456 | bytes 1024 | tf_op jit(solution)/shard_map/pallas_call | solution.py:389
  48.4 0.3 collective-permute-done.8
  48.7 0.1 add_convert_fusion
  48.8 0.0 copy-start.5
  48.8 0.1 collective-permute-start.9
  48.9 0.2 collective-permute-start.7
  49.1 15.1 %all_to_all.20.d_long = bf16[16,32,128]{2,1,0:T(8,128)(2,1)S(1)} all-to-all(bf16[16,32,128]{2,1,0:T(8,128)(2,1)S(1)} %bitcast.20), channel_id=1, replica_groups=mesh['l'=4,'h'=2,'c'=2,'dp'=2] {'l','h','c'}, dimensions={0} | all-to-all | bytes 262144 | tf_op jit(solution)/shard_map/all_to_all | solution.py:471
  64.2 1.9 %shard_map.127 = (bf16[16,32,128]{2,1,0:T(8,128)(2,1)}, bf16[32,2048]{1,0:T(8,128)(2,1)S(1)}) custom-call(bf16[16,32,128]{2,1,0:T(8,128)(2,1)S(1)} %all_to_all.20.d_long, f32[544,256]{1,0:T(8,128)S(1)} %shard_map.121.filt_spec, f32[544,256]{1,0:T(8,128)S(1)} %copy-done.9, f32[2,17,128]{2,1,0:T(8,128)S(1)} %copy-done.7, bf16[2,256,256]{2,1,0:T(8,128)(2,1)S(1)} %copy-done.5), custom_call_target="tpu_custom_call" | custom-call | flops 641728512 | bytes 1024 | tf_op jit(solution)/shard_map/pallas_call | solution.py:389
  66.1 1.5 %collective-permute-start.12 = (bf16[32,2048]{1,0:T(8,128)(2,1)S(1)}, bf16[32,2048]{1,0:T(8,128)(2,1)S(1)}, u32[]{:S(2)}, u32[]{:S(2)}) collective-permute-start(bf16[32,2048]{1,0:T(8,128)(2,1)S(1)} %get-tuple-element.52), channel_id=1, source_target_pairs={{0,1},{1,0},{2,3},{3,2},{4,5},{5,4},{6,7},{7,6},{8,9},{9,8},{10,11... | collective-permute-start | bytes 393224 | tf_op jit(solution)/shard_map/ppermute | solution.py:411
  67.6 0.0 collective-permute-done.7
  67.6 0.1 add_convert_fusion.2
  67.8 0.7 copy-done.10
  68.4 0.1 copy-done.11
  68.6 0.7 collective-permute-start.14
  69.3 0.6 collective-permute-start.13
  69.9 1.0 %collective-permute-start.11 = (bf16[32,2048]{1,0:T(8,128)(2,1)S(1)}, bf16[32,2048]{1,0:T(8,128)(2,1)S(1)}, u32[]{:S(2)}, u32[]{:S(2)}) collective-permute-start(bf16[32,2048]{1,0:T(8,128)(2,1)S(1)} %get-tuple-element.60), channel_id=1, source_target_pairs={{0,8},{8,16},{16,24},{24,0},{1,9},{9,17},{17,25},{25,1},{2,10},{10... | collective-permute-start | bytes 393224 | tf_op jit(solution)/shard_map/ppermute | solution.py:546
  70.9 0.7 collective-permute-done.12
  71.6 0.7 convert_add_fusion.1
  72.3 3.8 %all-to-all-start.3 = ((bf16[16,32,128]{2,1,0:T(8,128)(2,1)}), bf16[16,32,128]{2,1,0:T(8,128)(2,1)S(1)}, u32[]{:S(2)}, u32[]{:S(2)}) async-start(bf16[16,32,128]{2,1,0:T(8,128)(2,1)} %get-tuple-element.54), calls=%async_computation.3 | async-start | bytes 262144 | tf_op jit(solution)/shard_map/all_to_all | solution.py:471
  76.1 0.0 copy-start.1
  76.1 0.0 collective-permute-done.14
  76.2 7.5 %collective-permute-done.13 = bf16[32,2048]{1,0:T(8,128)(2,1)S(1)} collective-permute-done((bf16[32,2048]{1,0:T(8,128)(2,1)S(1)}, bf16[32,2048]{1,0:T(8,128)(2,1)S(1)}, u32[]{:S(2)}, u32[]{:S(2)}) %collective-permute-start.13) | collective-permute-done | bytes 131104 | tf_op jit(solution)/shard_map/ppermute | solution.py:546
  83.7 1.1 %add_convert_fusion.1 = bf16[32,2048]{1,0:T(8,128)(2,1)S(1)} fusion(bf16[32,2048]{1,0:T(8,128)(2,1)S(1)} %collective-permute-done.14, bf16[32,2048]{1,0:T(8,128)(2,1)S(1)} %collective-permute-done.13, bf16[32,2048]{1,0:T(8,128)(2,1)S(1)} %collective-permute-done.11, bf16[128,2048]{1,0:T(8,128)(2,1)} %copy-done.11, bf16[128,2048]{1,0:T(8,128)(2,1)} %copy-done.10, ...), kind=kLoop, calls=%fused_computation.2 | loop fusion | flops 786432 | bytes 917504 | tf_op jit(solution)/shard_map/convert_element_type | solution.py:548
  84.8 0.6 collective-permute-start.15
  85.3 0.0 all-to-all-done.3
  85.3 0.7 shard_map.128
  86.0 1.3 %collective-permute-start.10 = (f32[2,1536]{1,0:T(2,128)S(1)}, f32[2,1536]{1,0:T(2,128)S(1)}, u32[]{:S(2)}, u32[]{:S(2)}) collective-permute-start(f32[2,1536]{1,0:T(2,128)S(1)} %slice.59), channel_id=1, source_target_pairs={{2,0},{4,2},{6,4},{8,6},{10,8},{12,10},{14,12},{16,14},{18,16},{20... | collective-permute-start | bytes 36872 | tf_op jit(solution)/shard_map/ppermute | solution.py:559
  87.3 1.8 %collective-permute-done.10.later = f32[2,1536]{1,0:T(2,128)S(1)} collective-permute-done((f32[2,1536]{1,0:T(2,128)S(1)}, f32[2,1536]{1,0:T(2,128)S(1)}, u32[]{:S(2)}, u32[]{:S(2)}) %collective-permute-start.10) | collective-permute-done | bytes 12320 | tf_op jit(solution)/shard_map/ppermute | solution.py:559
  89.1 1.9 %shard_map.129 = bf16[128,1536]{1,0:T(8,128)(2,1)} custom-call(s32[5]{0:T(128)S(1)} %pad_add_fusion.scalars, bf16[128,1536]{1,0:T(8,128)(2,1)S(1)} %bitcast.13, bf16[2,1536]{1,0:T(2,128)(2,1)S(1)} %collective-permute-done.earlier, f32[3,1536]{1,0:T(4,128)S(1)} %copy-done.6, f32[512,128]{1,0:T(8,128)S(1)} %get-tuple-element.44.d_product_t, ...), custom_call_target="tpu_custom_call" | custom-call | flops 1048576 | bytes 1024 | tf_op jit(solution)/shard_map/pallas_call | solution.py:389
  91.0 0.7 convert_add_fusion
  (27 shorter events, 0.1 us)
Async XLA Ops:
  0.6 12.7 %copy-start.6 = (f32[3,1536]{1,0:T(4,128)S(1)}, f32[3,1536]{1,0:T(4,128)}, u32[]{:S(2)}) copy-start(f32[3,1536]{1,0:T(4,128)} %taps.5) | copy-start | bytes 55300
  1.4 3.2 %collective-permute-start = (bf16[2,1536]{1,0:T(2,128)(2,1)S(1)}, bf16[2,1536]{1,0:T(2,128)(2,1)S(1)}, u32[]{:S(2)}, u32[]{:S(2)}) collective-permute-start(bf16[2,1536]{1,0:T(2,128)(2,1)S(1)} %slice_bitcast_fusion), channel_id=1, source_target_pairs={{0,2},{2,4},{4,6},{6,8},{8,10},{10,12},{12,14},{14,16},{16,18},{18... | collective-permute-start | bytes 18440 | tf_op jit(solution)/shard_map/ppermute | solution.py:444
  3.8 0.7 copy-start.13
  3.8 0.7 copy-start.14
  4.6 18.7 %collective-permute-start.3 = (bf16[32,2048]{1,0:T(8,128)(2,1)}, bf16[32,2048]{1,0:T(8,128)(2,1)S(1)}, u32[]{:S(2)}, u32[]{:S(2)}) collective-permute-start(bf16[32,2048]{1,0:T(8,128)(2,1)} %param.12), channel_id=1, source_target_pairs={{0,24},{8,0},{16,8},{24,16},{1,25},{9,1},{17,9},{25,17},{2,26},{10... | collective-permute-start | bytes 393224 | tf_op jit(solution)/shard_map/ppermute | solution.py:426
  12.3 10.9 %collective-permute-start.2 = (bf16[32,2048]{1,0:T(8,128)(2,1)}, bf16[32,2048]{1,0:T(8,128)(2,1)S(1)}, u32[]{:S(2)}, u32[]{:S(2)}) collective-permute-start(bf16[32,2048]{1,0:T(8,128)(2,1)} %param.12), channel_id=1, source_target_pairs={{0,16},{8,24},{16,0},{24,8},{1,17},{9,25},{17,1},{25,9},{2,18},{10... | collective-permute-start | bytes 393224 | tf_op jit(solution)/shard_map/ppermute | solution.py:426
  12.3 10.9 %collective-permute-start.1 = (bf16[32,2048]{1,0:T(8,128)(2,1)}, bf16[32,2048]{1,0:T(8,128)(2,1)S(1)}, u32[]{:S(2)}, u32[]{:S(2)}) collective-permute-start(bf16[32,2048]{1,0:T(8,128)(2,1)} %param.12), channel_id=1, source_target_pairs={{0,8},{8,16},{16,24},{24,0},{1,9},{9,17},{17,25},{25,1},{2,10},{10... | collective-permute-start | bytes 393224 | tf_op jit(solution)/shard_map/ppermute | solution.py:426
  13.3 1.0 %copy-start = (bf16[1,128,1536]{2,1,0:T(8,128)(2,1)S(1)}, bf16[1,128,1536]{2,1,0:T(8,128)(2,1)}, u32[]{:S(2)}) copy-start(bf16[1,128,1536]{2,1,0:T(8,128)(2,1)} %param.9) | copy-start | bytes 1179652
  14.3 5.9 %copy-start.3 = (f32[32,2048]{1,0:T(8,128)S(1)}, f32[32,2048]{1,0:T(8,128)}, u32[]{:S(2)}) copy-start(f32[32,2048]{1,0:T(8,128)} %filt) | copy-start | bytes 786436
  14.3 5.9 %copy-start.4 = (bf16[2,256,256]{2,1,0:T(8,128)(2,1)S(1)}, bf16[2,256,256]{2,1,0:T(8,128)(2,1)}, u32[]{:S(2)}) copy-start(bf16[2,256,256]{2,1,0:T(8,128)(2,1)} %constant.25.clone.matrix) | copy-start | bytes 786436
  15.9 4.4 %copy-start.7 = (f32[2,17,128]{2,1,0:T(8,128)S(1)}, f32[2,17,128]{2,1,0:T(8,128)}, u32[]{:S(2)}) copy-start(f32[2,17,128]{2,1,0:T(8,128)} %constant.24.clone.twist) | copy-start | bytes 52228
  15.9 12.3 %all-to-all-start = ((bf16[16,32,128]{2,1,0:T(8,128)(2,1)}), bf16[16,32,128]{2,1,0:T(8,128)(2,1)S(1)}, u32[]{:S(2)}, u32[]{:S(2)}) async-start(bf16[16,32,128]{2,1,0:T(8,128)(2,1)} %bitcast.3), calls=%async_computation | async-start | bytes 262144 | tf_op jit(solution)/shard_map/all_to_all | solution.py:471
  20.3 0.9 copy-start.12
  23.3 19.0 %collective-permute-start.4 = (bf16[128,2048]{1,0:T(8,128)(2,1)S(1)}, bf16[128,2048]{1,0:T(8,128)(2,1)S(1)}, u32[]{:S(2)}, u32[]{:S(2)}) collective-permute-start(bf16[128,2048]{1,0:T(8,128)(2,1)S(1)} %constant_dynamic-update-slice_fusion.refs_0_), channel_id=1, source_target_pairs={{0,4},{4,0},{1,5},{5,1},{2,6},{6,2},{3,7},{7,3},{8,12},{12,8},{9,1... | collective-permute-start | bytes 1572872 | tf_op jit(solution)/shard_map/ppermute | solution.py:411
  28.2 14.1 %copy-start.2 = (bf16[1,128,2048]{2,1,0:T(8,128)(2,1)S(1)}, bf16[1,128,2048]{2,1,0:T(8,128)(2,1)}, u32[]{:S(2)}) copy-start(bf16[1,128,2048]{2,1,0:T(8,128)(2,1)} %param.13) | copy-start | bytes 1572868
  30.0 0.8 copy-start.8
  30.8 11.4 %all-to-all-start.1 = ((bf16[16,32,128]{2,1,0:T(8,128)(2,1)}), bf16[16,32,128]{2,1,0:T(8,128)(2,1)S(1)}, u32[]{:S(2)}, u32[]{:S(2)}) async-start(bf16[16,32,128]{2,1,0:T(8,128)(2,1)} %get-tuple-element.33), calls=%async_computation.1 | async-start | bytes 262144 | tf_op jit(solution)/shard_map/all_to_all | solution.py:471
  34.3 8.6 %collective-permute-start.5 = (bf16[128,2048]{1,0:T(8,128)(2,1)S(1)}, bf16[128,2048]{1,0:T(8,128)(2,1)S(1)}, u32[]{:S(2)}, u32[]{:S(2)}) collective-permute-start(bf16[128,2048]{1,0:T(8,128)(2,1)S(1)} %constant_dynamic-update-slice_fusion.refs_0_), channel_id=1, source_target_pairs={{0,2},{2,0},{1,3},{3,1},{4,6},{6,4},{5,7},{7,5},{8,10},{10,8},{9,1... | collective-permute-start | bytes 1572872 | tf_op jit(solution)/shard_map/ppermute | solution.py:411
  42.2 1.9 %collective-permute-start.6 = (bf16[128,2048]{1,0:T(8,128)(2,1)S(1)}, bf16[128,2048]{1,0:T(8,128)(2,1)S(1)}, u32[]{:S(2)}, u32[]{:S(2)}) collective-permute-start(bf16[128,2048]{1,0:T(8,128)(2,1)S(1)} %collective-permute-done.4.refs_1_), channel_id=1, source_target_pairs={{0,2},{2,0},{1,3},{3,1},{4,6},{6,4},{5,7},{7,5},{8,10},{10,8},{9,1... | collective-permute-start | bytes 1572872 | tf_op jit(solution)/shard_map/ppermute | solution.py:411
  46.7 2.0 %collective-permute-start.8 = (bf16[128,2048]{1,0:T(8,128)(2,1)S(1)}, bf16[128,2048]{1,0:T(8,128)(2,1)S(1)}, u32[]{:S(2)}, u32[]{:S(2)}) collective-permute-start(bf16[128,2048]{1,0:T(8,128)(2,1)S(1)} %get-tuple-element.50), channel_id=1, source_target_pairs={{0,2},{2,0},{1,3},{3,1},{4,6},{6,4},{5,7},{7,5},{8,10},{10,8},{9,1... | collective-permute-start | bytes 1572872 | tf_op jit(solution)/shard_map/ppermute | solution.py:411
  48.7 15.5 %copy-start.9 = (f32[544,256]{1,0:T(8,128)S(1)}, f32[544,256]{1,0:T(8,128)}, u32[]{:S(2)}) copy-start(f32[544,256]{1,0:T(8,128)} %copy-done.8) | copy-start | bytes 1671172
  48.8 15.4 %copy-start.5 = (bf16[2,256,256]{2,1,0:T(8,128)(2,1)S(1)}, bf16[2,256,256]{2,1,0:T(8,128)(2,1)}, u32[]{:S(2)}) copy-start(bf16[2,256,256]{2,1,0:T(8,128)(2,1)} %constant.25.clone.matrix) | copy-start | bytes 786436
  48.8 18.7 %collective-permute-start.9 = (bf16[128,2048]{1,0:T(8,128)(2,1)S(1)}, bf16[128,2048]{1,0:T(8,128)(2,1)S(1)}, u32[]{:S(2)}, u32[]{:S(2)}) collective-permute-start(bf16[128,2048]{1,0:T(8,128)(2,1)S(1)} %add_convert_fusion), channel_id=1, source_target_pairs={{0,4},{4,0},{1,5},{5,1},{2,6},{6,2},{3,7},{7,3},{8,12},{12,8},{9,1... | collective-permute-start | bytes 1572872 | tf_op jit(solution)/shard_map/ppermute | solution.py:411
  48.9 18.7 %collective-permute-start.7 = (bf16[128,2048]{1,0:T(8,128)(2,1)S(1)}, bf16[128,2048]{1,0:T(8,128)(2,1)S(1)}, u32[]{:S(2)}, u32[]{:S(2)}) collective-permute-start(bf16[128,2048]{1,0:T(8,128)(2,1)S(1)} %get-tuple-element.48), channel_id=1, source_target_pairs={{0,2},{2,0},{1,3},{3,1},{4,6},{6,4},{5,7},{7,5},{8,10},{10,8},{9,1... | collective-permute-start | bytes 1572872 | tf_op jit(solution)/shard_map/ppermute | solution.py:411
  66.1 5.5 %collective-permute-start.12 = (bf16[32,2048]{1,0:T(8,128)(2,1)S(1)}, bf16[32,2048]{1,0:T(8,128)(2,1)S(1)}, u32[]{:S(2)}, u32[]{:S(2)}) collective-permute-start(bf16[32,2048]{1,0:T(8,128)(2,1)S(1)} %get-tuple-element.52), channel_id=1, source_target_pairs={{0,1},{1,0},{2,3},{3,2},{4,5},{5,4},{6,7},{7,6},{8,9},{9,8},{10,11... | collective-permute-start | bytes 393224 | tf_op jit(solution)/shard_map/ppermute | solution.py:411
  67.6 0.8 copy-start.10
  67.6 1.0 %copy-start.11 = (bf16[128,2048]{1,0:T(8,128)(2,1)}, bf16[128,2048]{1,0:T(8,128)(2,1)S(1)}, u32[]{:S(2)}) copy-start(bf16[128,2048]{1,0:T(8,128)(2,1)S(1)} %collective-permute-done.7) | copy-start | bytes 1572868
  68.6 7.6 %collective-permute-start.14 = (bf16[32,2048]{1,0:T(8,128)(2,1)S(1)}, bf16[32,2048]{1,0:T(8,128)(2,1)S(1)}, u32[]{:S(2)}, u32[]{:S(2)}) collective-permute-start(bf16[32,2048]{1,0:T(8,128)(2,1)S(1)} %get-tuple-element.58), channel_id=1, source_target_pairs={{0,24},{8,0},{16,8},{24,16},{1,25},{9,1},{17,9},{25,17},{2,26},{10... | collective-permute-start | bytes 393224 | tf_op jit(solution)/shard_map/ppermute | solution.py:546
  69.3 14.4 %collective-permute-start.13 = (bf16[32,2048]{1,0:T(8,128)(2,1)S(1)}, bf16[32,2048]{1,0:T(8,128)(2,1)S(1)}, u32[]{:S(2)}, u32[]{:S(2)}) collective-permute-start(bf16[32,2048]{1,0:T(8,128)(2,1)S(1)} %get-tuple-element.59), channel_id=1, source_target_pairs={{0,16},{8,24},{16,0},{24,8},{1,17},{9,25},{17,1},{25,9},{2,18},{10... | collective-permute-start | bytes 393224 | tf_op jit(solution)/shard_map/ppermute | solution.py:546
  69.9 13.7 %collective-permute-start.11 = (bf16[32,2048]{1,0:T(8,128)(2,1)S(1)}, bf16[32,2048]{1,0:T(8,128)(2,1)S(1)}, u32[]{:S(2)}, u32[]{:S(2)}) collective-permute-start(bf16[32,2048]{1,0:T(8,128)(2,1)S(1)} %get-tuple-element.60), channel_id=1, source_target_pairs={{0,8},{8,16},{16,24},{24,0},{1,9},{9,17},{17,25},{25,1},{2,10},{10... | collective-permute-start | bytes 393224 | tf_op jit(solution)/shard_map/ppermute | solution.py:546
  72.3 13.0 %all-to-all-start.3 = ((bf16[16,32,128]{2,1,0:T(8,128)(2,1)}), bf16[16,32,128]{2,1,0:T(8,128)(2,1)S(1)}, u32[]{:S(2)}, u32[]{:S(2)}) async-start(bf16[16,32,128]{2,1,0:T(8,128)(2,1)} %get-tuple-element.54), calls=%async_computation.3 | async-start | bytes 262144 | tf_op jit(solution)/shard_map/all_to_all | solution.py:471
  76.1 9.2 %copy-start.1 = (bf16[1,128,1536]{2,1,0:T(8,128)(2,1)S(1)}, bf16[1,128,1536]{2,1,0:T(8,128)(2,1)}, u32[]{:S(2)}) copy-start(bf16[1,128,1536]{2,1,0:T(8,128)(2,1)} %param.9) | copy-start | bytes 1179652
  84.8 6.3 %collective-permute-start.15 = (bf16[32,2048]{1,0:T(8,128)(2,1)S(1)}, bf16[32,2048]{1,0:T(8,128)(2,1)S(1)}, u32[]{:S(2)}, u32[]{:S(2)}) collective-permute-start(bf16[32,2048]{1,0:T(8,128)(2,1)S(1)} %add_convert_fusion.1), channel_id=1, source_target_pairs={{0,1},{1,0},{2,3},{3,2},{4,5},{5,4},{6,7},{7,6},{8,9},{9,8},{10,11... | collective-permute-start | bytes 393224 | tf_op jit(solution)/shard_map/ppermute | solution.py:411
  86.0 3.1 %collective-permute-start.10 = (f32[2,1536]{1,0:T(2,128)S(1)}, f32[2,1536]{1,0:T(2,128)S(1)}, u32[]{:S(2)}, u32[]{:S(2)}) collective-permute-start(f32[2,1536]{1,0:T(2,128)S(1)} %slice.59), channel_id=1, source_target_pairs={{2,0},{4,2},{6,4},{8,6},{10,8},{12,10},{14,12},{16,14},{18,16},{20... | collective-permute-start | bytes 36872 | tf_op jit(solution)/shard_map/ppermute | solution.py:559

commit v3 on v2

--- a/solution.py
+++ b/solution.py
@@ -146,7 +146,7 @@
 
 
 def forward_kernel(
-    gated, filt_spec, twist, matrix, long_out, gated_spec, work, signal, *, blocks, chans
+    gated, filt_spec, twist, matrix, long_out, work, signal, *, blocks, chans
 ):
     for n1 in range(blocks):
         signal[n1] = gated[n1].astype(F32)
@@ -155,7 +155,6 @@
         return signal[n1, rows, :]
 
     spec = to_spectrum(load, blocks, chans, twist, matrix, work)
-    gated_spec[...] = spec
 
     def store(n1, rows, value):
         signal[n1, rows, :] = value
@@ -168,7 +167,7 @@
 def backward_kernel(
     d_long,
     filt_spec,
-    gated_spec,
+    gated,
     twist,
     matrix,
     d_gated,
@@ -196,7 +195,9 @@
     from_spectrum(spec, blocks, chans, twist, matrix, work, store)
     for n1 in range(blocks):
         d_gated[n1] = signal[n1].astype(BF16)
-    spec = conj_times(gated_spec[...], held[...])
+    for n1 in range(blocks):
+        signal[n1] = gated[n1].astype(F32)
+    spec = conj_times(to_spectrum(load, blocks, chans, twist, matrix, work), held[...])
     from_spectrum(spec, blocks, chans, twist, matrix, work, store)
     for n1 in range(blocks):
         d_filter[:, n1 * LANES : (n1 + 1) * LANES] = (signal[n1] * scale).astype(BF16)
@@ -411,10 +412,14 @@
     return lax.ppermute(block, axis, SWAP)
 
 
-def dp_sum(block):
+def dp_start(block):
+    return swap(block, "dp") if lax.axis_size("dp") == 2 else lax.psum(block, "dp")
+
+
+def dp_finish(block, got):
     if lax.axis_size("dp") == 2:
-        return block.astype(F32) + swap(block, "dp").astype(F32)
-    return lax.psum(block, "dp").astype(F32)
+        return block.astype(F32) + got.astype(F32)
+    return got.astype(F32)
 
 
 def line_route(lines, step):
@@ -441,13 +446,14 @@
     scalars = jnp.concatenate([place, lengths, counts])
 
     route = [(i, i + 1) for i in range(ctx_size - 1)]
-    earlier = lax.ppermute(proj[0, rows - 2 :], axes, route)
+    tail = proj[0, rows - 2 :]
+    earlier = lax.ppermute(tail, axes, route)
 
 
     flat = (width, rows)
     width_of = features // CHUNKS
     parts = [
-        along_line(after(w_out[:, i * width_of : (i + 1) * width_of], earlier), lines)
+        along_line(after(w_out[:, i * width_of : (i + 1) * width_of], tail), lines)
         for i in range(CHUNKS)
     ]
     inputs = (scalars, proj[0], earlier, short_filter)
@@ -485,13 +491,14 @@
         flops=fft_flops,
     )
     near = [
-        jnp.concatenate(part[:1] + [after(p, filt_spec) for p in part[1:]]) for part in parts
+        jnp.concatenate([after(part[0], filt_spec)] + part[1:]) for part in parts
     ]
     over = [swap(part, "h") for part in near]
-    long_cols, gated_spec = call(
+    gated_cols = exchange(gated_t.reshape(blocked))
+    (long_cols,) = call(
         functools.partial(forward_kernel, **sizes),
-        [(blocked, BF16), (spec_shape, F32)],
-        (exchange(gated_t.reshape(blocked)), filt_spec, *tables),
+        [(blocked, BF16)],
+        (gated_cols, filt_spec, *tables),
         scratch=[work, signal],
         flops=30 << 30,
     )
@@ -520,7 +527,7 @@
     d_gated_cols, filter_part = call(
         functools.partial(backward_kernel, scale=grad_scale, **sizes),
         [(blocked, BF16), ((chans, seq_len), BF16)],
-        (d_long_cols, filt_spec, gated_spec, *tables),
+        (d_long_cols, filt_spec, gated_cols, *tables),
         scratch=[work, signal, work],
         flops=3 * fft_flops,
     )
@@ -540,12 +547,12 @@
         for at in (slice(i * chans, (i + 1) * chans) for i in range(lines))
     ]
     sent = [total[lines - step].astype(BF16) for step in range(1, lines)]
-    d_filter = dp_sum(filter_part)
-    total_here = total[0]
+    filter_sum = dp_start(filter_part)
+    total_here = after(total[0], *sent)
     for step, block in enumerate(sent, 1):
-        got = after(lax.ppermute(block, "l", line_route(lines, step)), d_filter)
-        total_here += got.astype(F32)
-    d_wout = dp_sum(total_here.astype(BF16))
+        total_here += lax.ppermute(block, "l", line_route(lines, step)).astype(F32)
+    total_here = total_here.astype(BF16)
+    d_wout = dp_finish(total_here, dp_start(total_here))
 
     d_gated_t = exchange(after(d_gated_cols, *sent)).reshape(flat)
 
@@ -556,6 +563,7 @@
         1,
         flops=1 << 20,
     )
+    d_filter = dp_finish(filter_part, after(filter_sum, head))
     later = lax.ppermute(head[:2], axes, [(j, i) for i, j in route])
     (d_proj,) = call(
         functools.partial(proj_grad_kernel, width=width, split=split),

time: 92.8 us -> 88.7 us (0.956)
  waiting for transfers between devices: 25.3 us -> 22.9 us
  local copies, waits for them, and re-layouts: 4.54 us -> 2.93 us
  other arithmetic: 2.88 us -> 1.95 us
    ppermute x3, starting transfers between devices: 8.74 us -> 5.68 us  [along_line(): lax.ppermute(block, 'l', line_route(lines, step))]
    unnamed x33 -> x25, local copies, waits for them, and re-layouts: 3.77 us -> 2.16 us
    ppermute x8, starting transfers between devices: 3.62 us -> 5.18 us  [swap(): return lax.ppermute(block, axis, SWAP)]
    convert_element_type x2 -> x1, other arithmetic: 1.22 us -> 0.06 us  [per_device(): total_here = total_here.astype(BF16)]
    ppermute x4, starting transfers between devices: 4.71 us -> 5.8 us  [the longest x3 3.45 us: per_device(): total_here += lax.ppermute(block, 'l', line_route(lines, step)).astype(F32)]
    all_to_all x3, starting transfers between devices: 11.7 us -> 12.7 us  [exchange(): return lax.all_to_all(block, axes, 0, 0, tiled=True)]
  transfers between devices with their start and end apart: 19 -> 19, of which waited for: 8 -> 7; matrix products, arithmetic and copies ran while one was open for 2% -> 1% of each run, Pallas kernels for 11% -> 12%
where the time goes in v3:
time: 88.7 us; the launch traced here: 87.5 us
  starting transfers between devices  30.7 us (35%)
  waiting for transfers between devices  22.9 us (26%)
  blocking collectives  15.1 us (17%)
  Pallas kernels  13.2 us (15%)
  local copies, waits for them, and re-layouts  2.93 us (3%)
  other arithmetic  1.95 us (2%)
    all_to_all x1, blocking collectives, exchange(): return lax.all_to_all(block, axes, 0, 0, tiled=True)  15.1 us
    pallas_call x10, Pallas kernels, call(): pl.pallas_call(kernel, grid=(1,), out_shape=out_shape, in_specs=[SMEM if...  13.2 us
    all_to_all x3, starting transfers between devices, exchange(): return lax.all_to_all(block, axes, 0, 0, tiled=True)  12.7 us
    all_to_all x3, waiting for transfers between devices, exchange(): return lax.all_to_all(block, axes, 0, 0, tiled=True)  11 us
    ppermute x3, waiting for transfers between devices, per_device(): total_here += lax.ppermute(block, 'l', line_route(lines, step)).astype(F32)  7.07 us
    ppermute x3, starting transfers between devices, along_line(): lax.ppermute(block, 'l', line_route(lines, step))  5.68 us
    ppermute x8, starting transfers between devices, swap(): return lax.ppermute(block, axis, SWAP)  5.18 us
    ppermute x3, starting transfers between devices, per_device(): total_here += lax.ppermute(block, 'l', line_route(lines, step)).astype(F32)  3.45 us
  transfers between devices with their start and end apart: 19, of which 7 were waited for; matrix products, arithmetic and copies ran while one was open for 1% of the time, Pallas kernels for 12%

profile of v3, /device:TPU:0, one launch (start us, length us, event | category | flops | bytes accessed | tf_op | source)
XLA Modules:
  0.0 87.5 jit_solution(11049126597157874384)
XLA Ops:
  0.6 0.8 slice_bitcast_fusion
  1.4 2.4 %collective-permute-start = (bf16[2,1536]{1,0:T(2,128)(2,1)S(1)}, bf16[2,1536]{1,0:T(2,128)(2,1)S(1)}, u32[]{:S(2)}, u32[]{:S(2)}) collective-permute-start(bf16[2,1536]{1,0:T(2,128)(2,1)S(1)} %slice_bitcast_fusion), channel_id=1, source_target_pairs={{0,2},{2,4},{4,6},{6,8},{8,10},{10,12},{12,14},{14,16},{16,18},{18... | collective-permute-start | bytes 18440 | tf_op jit(solution)/shard_map/ppermute | solution.py:450
  3.8 4.7 %collective-permute-start.3 = (bf16[32,2048]{1,0:T(8,128)(2,1)}, bf16[32,2048]{1,0:T(8,128)(2,1)S(1)}, u32[]{:S(2)}, u32[]{:S(2)}) collective-permute-start(bf16[32,2048]{1,0:T(8,128)(2,1)} %param.12), channel_id=1, source_target_pairs={{0,24},{8,0},{16,8},{24,16},{1,25},{9,1},{17,9},{25,17},{2,26},{10... | collective-permute-start | bytes 393224 | tf_op jit(solution)/shard_map/ppermute | solution.py:431
  8.4 0.0 collective-permute-start.2
  8.4 1.0 %collective-permute-start.1 = (bf16[32,2048]{1,0:T(8,128)(2,1)}, bf16[32,2048]{1,0:T(8,128)(2,1)S(1)}, u32[]{:S(2)}, u32[]{:S(2)}) collective-permute-start(bf16[32,2048]{1,0:T(8,128)(2,1)} %param.12), channel_id=1, source_target_pairs={{0,8},{8,16},{16,24},{24,0},{1,9},{9,17},{17,25},{25,1},{2,10},{10... | collective-permute-start | bytes 393224 | tf_op jit(solution)/shard_map/ppermute | solution.py:431
  9.4 0.7 copy-done.9
  10.1 0.0 copy-done.10
  10.1 0.1 pad_add_fusion.scalars
  10.2 0.0 collective-permute-done.earlier
  10.2 1.0 %copy-done = bf16[1,128,1536]{2,1,0:T(8,128)(2,1)S(1)} copy-done((bf16[1,128,1536]{2,1,0:T(8,128)(2,1)S(1)}, bf16[1,128,1536]{2,1,0:T(8,128)(2,1)}, u32[]{:S(2)}) %copy-start) | copy-done | bytes 393240
  11.2 1.6 %shard_map.120 = (bf16[512,128]{1,0:T(8,128)(2,1)}, f32[512,128]{1,0:T(8,128)S(1)}) custom-call(s32[5]{0:T(128)S(1)} %pad_add_fusion.scalars, bf16[128,1536]{1,0:T(8,128)(2,1)S(1)} %bitcast.11, bf16[2,1536]{1,0:T(2,128)(2,1)S(1)} %collective-permute-done.earlier, f32[3,1536]{1,0:T(4,128)S(1)} %copy-done.6), custom_call_target="tpu_custom_call" | custom-call | flops 1048576 | bytes 1024 | tf_op jit(solution)/shard_map/pallas_call | solution.py:390
  12.8 5.3 %all-to-all-start = ((bf16[16,32,128]{2,1,0:T(8,128)(2,1)}), bf16[16,32,128]{2,1,0:T(8,128)(2,1)S(1)}, u32[]{:S(2)}, u32[]{:S(2)}) async-start(bf16[16,32,128]{2,1,0:T(8,128)(2,1)} %bitcast.3), calls=%async_computation | async-start | bytes 262144 | tf_op jit(solution)/shard_map/all_to_all | solution.py:477
  18.1 0.0 copy-start.8
  18.1 0.5 shard_map.121.filt_spec
  18.5 0.4 copy-done.8
  19.0 0.0 collective-permute-done.1
  19.0 2.2 %collective-permute-done.2 = bf16[32,2048]{1,0:T(8,128)(2,1)S(1)} collective-permute-done((bf16[32,2048]{1,0:T(8,128)(2,1)}, bf16[32,2048]{1,0:T(8,128)(2,1)S(1)}, u32[]{:S(2)}, u32[]{:S(2)}) %collective-permute-start.2) | collective-permute-done | bytes 131104 | tf_op jit(solution)/shard_map/ppermute | solution.py:431
  21.3 0.0 collective-permute-done.3
  21.3 1.2 %collective-permute-start.4 = (bf16[128,2048]{1,0:T(8,128)(2,1)S(1)}, bf16[128,2048]{1,0:T(8,128)(2,1)S(1)}, u32[]{:S(2)}, u32[]{:S(2)}) collective-permute-start(bf16[128,2048]{1,0:T(8,128)(2,1)S(1)} %constant_dynamic-update-slice_fusion.refs_0_), channel_id=1, source_target_pairs={{0,4},{4,0},{1,5},{5,1},{2,6},{6,2},{3,7},{7,3},{8,12},{12,8},{9,1... | collective-permute-start | bytes 1572872 | tf_op jit(solution)/shard_map/ppermute | solution.py:412
  22.4 3.5 %all-to-all-done.gated = bf16[16,32,128]{2,1,0:T(8,128)(2,1)S(1)} async-done(((bf16[16,32,128]{2,1,0:T(8,128)(2,1)}), bf16[16,32,128]{2,1,0:T(8,128)(2,1)S(1)}, u32[]{:S(2)}, u32[]{:S(2)}) %all-to-all-start) | async-done | bytes 131104 | tf_op jit(solution)/shard_map/all_to_all | solution.py:477
  26.0 1.8 %shard_map.122 = bf16[16,32,128]{2,1,0:T(8,128)(2,1)} custom-call(bf16[16,32,128]{2,1,0:T(8,128)(2,1)S(1)} %all-to-all-done.gated, f32[544,256]{1,0:T(8,128)S(1)} %shard_map.121.filt_spec, f32[2,17,128]{2,1,0:T(8,128)S(1)} %copy-done.7, bf16[2,256,256]{2,1,0:T(8,128)(2,1)S(1)} %copy-done.4), custom_call_target="tpu_custom_call" | custom-call | flops 32212254720 | bytes 1024 | tf_op jit(solution)/shard_map/pallas_call | solution.py:390
  27.8 3.9 %all-to-all-start.1 = ((bf16[16,32,128]{2,1,0:T(8,128)(2,1)}), bf16[16,32,128]{2,1,0:T(8,128)(2,1)S(1)}, u32[]{:S(2)}, u32[]{:S(2)}) async-start(bf16[16,32,128]{2,1,0:T(8,128)(2,1)} %shard_map.122), calls=%async_computation.1 | async-start | bytes 262144 | tf_op jit(solution)/shard_map/all_to_all | solution.py:477
  31.8 0.4 collective-permute-start.5
  32.2 7.5 %all-to-all-done.1 = bf16[16,32,128]{2,1,0:T(8,128)(2,1)S(1)} async-done(((bf16[16,32,128]{2,1,0:T(8,128)(2,1)}), bf16[16,32,128]{2,1,0:T(8,128)(2,1)S(1)}, u32[]{:S(2)}, u32[]{:S(2)}) %all-to-all-start.1) | async-done | bytes 131104 | tf_op jit(solution)/shard_map/all_to_all | solution.py:477
  39.7 0.0 collective-permute-done.4.refs_1_
  39.7 0.0 collective-permute-start.6
  39.7 0.0 copy-done.2
  39.7 0.7 shard_map.123.cot
  40.4 0.0 collective-permute-done.5.refs_2_
  40.4 1.2 %collective-permute-done.6.refs_3_ = bf16[128,2048]{1,0:T(8,128)(2,1)S(1)} collective-permute-done((bf16[128,2048]{1,0:T(8,128)(2,1)S(1)}, bf16[128,2048]{1,0:T(8,128)(2,1)S(1)}, u32[]{:S(2)}, u32[]{:S(2)}) %collective-permute-start.6) | collective-permute-done | bytes 524320 | tf_op jit(solution)/shard_map/ppermute | solution.py:412
  41.6 1.3 %shard_map.124 = (f32[512,128]{1,0:T(8,128)S(1)}, bf16[512,128]{1,0:T(8,128)(2,1)S(1)}) custom-call(s32[5]{0:T(128)S(1)} %pad_add_fusion.scalars, bf16[128,2048]{1,0:T(8,128)(2,1)S(1)} %shard_map.123.cot, f32[512,128]{1,0:T(8,128)S(1)} %get-tuple-element.28.query_t, bf16[128,2048]{1,0:T(8,128)(2,1)S(1)} %constant_dynamic-update-slice_fusion.refs_0_, ...), custom_call_target="tpu_custom_call" | custom-call | flops 268435456 | bytes 1024 | tf_op jit(solution)/shard_map/pallas_call | solution.py:390
  42.9 1.3 %shard_map.125 = (bf16[4,128,128]{2,1,0:T(8,128)(2,1)S(1)}, bf16[128,2048]{1,0:T(8,128)(2,1)S(1)}, bf16[128,2048]{1,0:T(8,128)(2,1)S(1)}, bf16[128,2048]{1,0:T(8,128)(2,1)S(1)}, bf16[128,2048]{1,0:T(8,128)(2,1)S(1)}) custom-call(s32[5]{0:T(128)S(1)} %pad_add_fusion.scalars, bf16[512,128]{1,0:T(8,128)(2,1)S(1)} %bitcast.14, ...), custom_call_target="tpu_custom_call" | custom-call | flops 1024 | bytes 1024 | tf_op jit(solution)/shard_map/pallas_call | solution.py:390
  44.2 0.2 collective-permute-start.8
  44.4 1.5 %shard_map.126 = bf16[128,2048]{1,0:T(8,128)(2,1)} custom-call(bf16[4,128,128]{2,1,0:T(8,128)(2,1)S(1)} %get-tuple-element.35.product, bf16[128,2048]{1,0:T(8,128)(2,1)S(1)} %constant_dynamic-update-slice_fusion.refs_0_, bf16[128,2048]{1,0:T(8,128)(2,1)S(1)} %collective-permute-done.4.refs_1_, bf16[128,2048]{1,0:T(8,128)(2,1)S(1)} %collective-permute-done.5.refs_2_, ...), custom_call_target="tpu_custom_call" | custom-call | flops 268435456 | bytes 1024 | tf_op jit(solution)/shard_map/pallas_call | solution.py:390
  45.9 0.3 collective-permute-done.8
  46.1 0.1 add_convert_fusion
  46.3 0.0 copy-start.5
  46.3 0.1 collective-permute-start.9
  46.4 0.2 collective-permute-start.7
  46.6 15.1 %all_to_all.20.d_long = bf16[16,32,128]{2,1,0:T(8,128)(2,1)S(1)} all-to-all(bf16[16,32,128]{2,1,0:T(8,128)(2,1)S(1)} %bitcast.20), channel_id=1, replica_groups=mesh['l'=4,'h'=2,'c'=2,'dp'=2] {'l','h','c'}, dimensions={0} | all-to-all | bytes 262144 | tf_op jit(solution)/shard_map/all_to_all | solution.py:477
  61.6 2.0 %shard_map.127 = (bf16[16,32,128]{2,1,0:T(8,128)(2,1)}, bf16[32,2048]{1,0:T(8,128)(2,1)S(1)}) custom-call(bf16[16,32,128]{2,1,0:T(8,128)(2,1)S(1)} %all_to_all.20.d_long, f32[544,256]{1,0:T(8,128)S(1)} %shard_map.121.filt_spec, bf16[16,32,128]{2,1,0:T(8,128)(2,1)S(1)} %all-to-all-done.gated, f32[2,17,128]{2,1,0:T(8,128)S(1)} %copy-done.7, ...), custom_call_target="tpu_custom_call" | custom-call | flops 641728512 | bytes 1024 | tf_op jit(solution)/shard_map/pallas_call | solution.py:390
  63.6 0.0 collective-permute-done.9
  63.6 0.0 collective-permute-done.7
  63.6 0.2 convert_add_fusion.2
  63.8 0.8 collective-permute-start.13
  64.7 0.7 collective-permute-start.12
  65.3 1.9 %collective-permute-start.11 = (bf16[32,2048]{1,0:T(8,128)(2,1)S(1)}, bf16[32,2048]{1,0:T(8,128)(2,1)S(1)}, u32[]{:S(2)}, u32[]{:S(2)}) collective-permute-start(bf16[32,2048]{1,0:T(8,128)(2,1)S(1)} %get-tuple-element.51), channel_id=1, source_target_pairs={{0,8},{8,16},{16,24},{24,0},{1,9},{9,17},{17,25},{25,1},{2,10},{10... | collective-permute-start | bytes 393224 | tf_op jit(solution)/shard_map/ppermute | solution.py:553
  67.3 1.5 %collective-permute-start.15 = (bf16[32,2048]{1,0:T(8,128)(2,1)S(1)}, bf16[32,2048]{1,0:T(8,128)(2,1)S(1)}, u32[]{:S(2)}, u32[]{:S(2)}) collective-permute-start(bf16[32,2048]{1,0:T(8,128)(2,1)S(1)} %get-tuple-element.43), channel_id=1, source_target_pairs={{0,1},{1,0},{2,3},{3,2},{4,5},{5,4},{6,7},{7,6},{8,9},{9,8},{10,11... | collective-permute-start | bytes 393224 | tf_op jit(solution)/shard_map/ppermute | solution.py:412
  68.8 3.5 %all-to-all-start.3 = ((bf16[16,32,128]{2,1,0:T(8,128)(2,1)}), bf16[16,32,128]{2,1,0:T(8,128)(2,1)S(1)}, u32[]{:S(2)}, u32[]{:S(2)}) async-start(bf16[16,32,128]{2,1,0:T(8,128)(2,1)} %get-tuple-element.45), calls=%async_computation.3 | async-start | bytes 262144 | tf_op jit(solution)/shard_map/all_to_all | solution.py:477
  72.3 0.0 copy-start.1
  72.3 0.0 collective-permute-done.13
  72.4 7.1 %collective-permute-done.12 = bf16[32,2048]{1,0:T(8,128)(2,1)S(1)} collective-permute-done((bf16[32,2048]{1,0:T(8,128)(2,1)S(1)}, bf16[32,2048]{1,0:T(8,128)(2,1)S(1)}, u32[]{:S(2)}, u32[]{:S(2)}) %collective-permute-start.12) | collective-permute-done | bytes 131104 | tf_op jit(solution)/shard_map/ppermute | solution.py:553
  79.4 0.0 collective-permute-done.11
  79.4 0.1 add_convert_fusion.1
  79.5 1.6 %collective-permute-start.14 = (bf16[32,2048]{1,0:T(8,128)(2,1)S(1)}, bf16[32,2048]{1,0:T(8,128)(2,1)S(1)}, u32[]{:S(2)}, u32[]{:S(2)}) collective-permute-start(bf16[32,2048]{1,0:T(8,128)(2,1)S(1)} %add_convert_fusion.1), channel_id=1, source_target_pairs={{0,1},{1,0},{2,3},{3,2},{4,5},{5,4},{6,7},{7,6},{8,9},{9,8},{10,11... | collective-permute-start | bytes 393224 | tf_op jit(solution)/shard_map/ppermute | solution.py:412
  81.1 0.0 all-to-all-done.3
  81.1 0.7 shard_map.128
  81.8 0.0 collective-permute-done.15
  81.8 1.3 %collective-permute-start.10 = (f32[2,1536]{1,0:T(2,128)S(1)}, f32[2,1536]{1,0:T(2,128)S(1)}, u32[]{:S(2)}, u32[]{:S(2)}) collective-permute-start(f32[2,1536]{1,0:T(2,128)S(1)} %slice.59), channel_id=1, source_target_pairs={{2,0},{4,2},{6,4},{8,6},{10,8},{12,10},{14,12},{16,14},{18,16},{20... | collective-permute-start | bytes 36872 | tf_op jit(solution)/shard_map/ppermute | solution.py:567
  83.1 0.7 convert_add_fusion
  83.8 1.0 %collective-permute-done.10.later = f32[2,1536]{1,0:T(2,128)S(1)} collective-permute-done((f32[2,1536]{1,0:T(2,128)S(1)}, f32[2,1536]{1,0:T(2,128)S(1)}, u32[]{:S(2)}, u32[]{:S(2)}) %collective-permute-start.10) | collective-permute-done | bytes 12320 | tf_op jit(solution)/shard_map/ppermute | solution.py:567
  84.9 1.9 %shard_map.129 = bf16[128,1536]{1,0:T(8,128)(2,1)} custom-call(s32[5]{0:T(128)S(1)} %pad_add_fusion.scalars, bf16[128,1536]{1,0:T(8,128)(2,1)S(1)} %bitcast.13, bf16[2,1536]{1,0:T(2,128)(2,1)S(1)} %collective-permute-done.earlier, f32[3,1536]{1,0:T(4,128)S(1)} %copy-done.6, f32[512,128]{1,0:T(8,128)S(1)} %get-tuple-element.36.d_product_t, ...), custom_call_target="tpu_custom_call" | custom-call | flops 1048576 | bytes 1024 | tf_op jit(solution)/shard_map/pallas_call | solution.py:390
  86.8 0.0 collective-permute-done.14
  86.8 0.7 convert_add_fusion.1
  (19 shorter events, 0.1 us)
Async XLA Ops:
  0.6 9.6 %copy-start.6 = (f32[3,1536]{1,0:T(4,128)S(1)}, f32[3,1536]{1,0:T(4,128)}, u32[]{:S(2)}) copy-start(f32[3,1536]{1,0:T(4,128)} %taps.5) | copy-start | bytes 55300
  1.4 8.8 %collective-permute-start = (bf16[2,1536]{1,0:T(2,128)(2,1)S(1)}, bf16[2,1536]{1,0:T(2,128)(2,1)S(1)}, u32[]{:S(2)}, u32[]{:S(2)}) collective-permute-start(bf16[2,1536]{1,0:T(2,128)(2,1)S(1)} %slice_bitcast_fusion), channel_id=1, source_target_pairs={{0,2},{2,4},{4,6},{6,8},{8,10},{10,12},{12,14},{14,16},{16,18},{18... | collective-permute-start | bytes 18440 | tf_op jit(solution)/shard_map/ppermute | solution.py:450
  3.8 17.5 %collective-permute-start.3 = (bf16[32,2048]{1,0:T(8,128)(2,1)}, bf16[32,2048]{1,0:T(8,128)(2,1)S(1)}, u32[]{:S(2)}, u32[]{:S(2)}) collective-permute-start(bf16[32,2048]{1,0:T(8,128)(2,1)} %param.12), channel_id=1, source_target_pairs={{0,24},{8,0},{16,8},{24,16},{1,25},{9,1},{17,9},{25,17},{2,26},{10... | collective-permute-start | bytes 393224 | tf_op jit(solution)/shard_map/ppermute | solution.py:431
  8.4 12.8 %collective-permute-start.2 = (bf16[32,2048]{1,0:T(8,128)(2,1)}, bf16[32,2048]{1,0:T(8,128)(2,1)S(1)}, u32[]{:S(2)}, u32[]{:S(2)}) collective-permute-start(bf16[32,2048]{1,0:T(8,128)(2,1)} %param.12), channel_id=1, source_target_pairs={{0,16},{8,24},{16,0},{24,8},{1,17},{9,25},{17,1},{25,9},{2,18},{10... | collective-permute-start | bytes 393224 | tf_op jit(solution)/shard_map/ppermute | solution.py:431
  8.4 10.5 %collective-permute-start.1 = (bf16[32,2048]{1,0:T(8,128)(2,1)}, bf16[32,2048]{1,0:T(8,128)(2,1)S(1)}, u32[]{:S(2)}, u32[]{:S(2)}) collective-permute-start(bf16[32,2048]{1,0:T(8,128)(2,1)} %param.12), channel_id=1, source_target_pairs={{0,8},{8,16},{16,24},{24,0},{1,9},{9,17},{17,25},{25,1},{2,10},{10... | collective-permute-start | bytes 393224 | tf_op jit(solution)/shard_map/ppermute | solution.py:431
  9.4 0.7 copy-start.9
  9.4 0.7 copy-start.10
  10.2 1.0 %copy-start = (bf16[1,128,1536]{2,1,0:T(8,128)(2,1)S(1)}, bf16[1,128,1536]{2,1,0:T(8,128)(2,1)}, u32[]{:S(2)}) copy-start(bf16[1,128,1536]{2,1,0:T(8,128)(2,1)} %param.9) | copy-start | bytes 1179652
  11.2 6.8 %copy-start.3 = (f32[32,2048]{1,0:T(8,128)S(1)}, f32[32,2048]{1,0:T(8,128)}, u32[]{:S(2)}) copy-start(f32[32,2048]{1,0:T(8,128)} %filt) | copy-start | bytes 786436
  11.2 6.8 %copy-start.4 = (bf16[2,256,256]{2,1,0:T(8,128)(2,1)S(1)}, bf16[2,256,256]{2,1,0:T(8,128)(2,1)}, u32[]{:S(2)}) copy-start(bf16[2,256,256]{2,1,0:T(8,128)(2,1)} %constant.25.clone.matrix) | copy-start | bytes 786436
  12.8 5.3 %copy-start.7 = (f32[2,17,128]{2,1,0:T(8,128)S(1)}, f32[2,17,128]{2,1,0:T(8,128)}, u32[]{:S(2)}) copy-start(f32[2,17,128]{2,1,0:T(8,128)} %constant.24.clone.twist) | copy-start | bytes 52228
  12.8 13.2 %all-to-all-start = ((bf16[16,32,128]{2,1,0:T(8,128)(2,1)}), bf16[16,32,128]{2,1,0:T(8,128)(2,1)S(1)}, u32[]{:S(2)}, u32[]{:S(2)}) async-start(bf16[16,32,128]{2,1,0:T(8,128)(2,1)} %bitcast.3), calls=%async_computation | async-start | bytes 262144 | tf_op jit(solution)/shard_map/all_to_all | solution.py:477
  18.1 0.9 %copy-start.8 = (bf16[32,2048]{1,0:T(8,128)(2,1)S(1)}, bf16[32,2048]{1,0:T(8,128)(2,1)}, u32[]{:S(2)}) copy-start(bf16[32,2048]{1,0:T(8,128)(2,1)} %param.12) | copy-start | bytes 393220
  21.3 18.4 %collective-permute-start.4 = (bf16[128,2048]{1,0:T(8,128)(2,1)S(1)}, bf16[128,2048]{1,0:T(8,128)(2,1)S(1)}, u32[]{:S(2)}, u32[]{:S(2)}) collective-permute-start(bf16[128,2048]{1,0:T(8,128)(2,1)S(1)} %constant_dynamic-update-slice_fusion.refs_0_), channel_id=1, source_target_pairs={{0,4},{4,0},{1,5},{5,1},{2,6},{6,2},{3,7},{7,3},{8,12},{12,8},{9,1... | collective-permute-start | bytes 1572872 | tf_op jit(solution)/shard_map/ppermute | solution.py:412
  26.0 13.7 %copy-start.2 = (bf16[1,128,2048]{2,1,0:T(8,128)(2,1)S(1)}, bf16[1,128,2048]{2,1,0:T(8,128)(2,1)}, u32[]{:S(2)}) copy-start(bf16[1,128,2048]{2,1,0:T(8,128)(2,1)} %param.13) | copy-start | bytes 1572868
  27.8 11.9 %all-to-all-start.1 = ((bf16[16,32,128]{2,1,0:T(8,128)(2,1)}), bf16[16,32,128]{2,1,0:T(8,128)(2,1)S(1)}, u32[]{:S(2)}, u32[]{:S(2)}) async-start(bf16[16,32,128]{2,1,0:T(8,128)(2,1)} %shard_map.122), calls=%async_computation.1 | async-start | bytes 262144 | tf_op jit(solution)/shard_map/all_to_all | solution.py:477
  31.8 8.6 %collective-permute-start.5 = (bf16[128,2048]{1,0:T(8,128)(2,1)S(1)}, bf16[128,2048]{1,0:T(8,128)(2,1)S(1)}, u32[]{:S(2)}, u32[]{:S(2)}) collective-permute-start(bf16[128,2048]{1,0:T(8,128)(2,1)S(1)} %constant_dynamic-update-slice_fusion.refs_0_), channel_id=1, source_target_pairs={{0,2},{2,0},{1,3},{3,1},{4,6},{6,4},{5,7},{7,5},{8,10},{10,8},{9,1... | collective-permute-start | bytes 1572872 | tf_op jit(solution)/shard_map/ppermute | solution.py:412
  39.7 1.9 %collective-permute-start.6 = (bf16[128,2048]{1,0:T(8,128)(2,1)S(1)}, bf16[128,2048]{1,0:T(8,128)(2,1)S(1)}, u32[]{:S(2)}, u32[]{:S(2)}) collective-permute-start(bf16[128,2048]{1,0:T(8,128)(2,1)S(1)} %collective-permute-done.4.refs_1_), channel_id=1, source_target_pairs={{0,2},{2,0},{1,3},{3,1},{4,6},{6,4},{5,7},{7,5},{8,10},{10,8},{9,1... | collective-permute-start | bytes 1572872 | tf_op jit(solution)/shard_map/ppermute | solution.py:412
  44.2 2.0 %collective-permute-start.8 = (bf16[128,2048]{1,0:T(8,128)(2,1)S(1)}, bf16[128,2048]{1,0:T(8,128)(2,1)S(1)}, u32[]{:S(2)}, u32[]{:S(2)}) collective-permute-start(bf16[128,2048]{1,0:T(8,128)(2,1)S(1)} %get-tuple-element.41), channel_id=1, source_target_pairs={{0,2},{2,0},{1,3},{3,1},{4,6},{6,4},{5,7},{7,5},{8,10},{10,8},{9,1... | collective-permute-start | bytes 1572872 | tf_op jit(solution)/shard_map/ppermute | solution.py:412
  46.3 15.4 %copy-start.5 = (bf16[2,256,256]{2,1,0:T(8,128)(2,1)S(1)}, bf16[2,256,256]{2,1,0:T(8,128)(2,1)}, u32[]{:S(2)}) copy-start(bf16[2,256,256]{2,1,0:T(8,128)(2,1)} %constant.25.clone.matrix) | copy-start | bytes 786436
  46.3 17.3 %collective-permute-start.9 = (bf16[128,2048]{1,0:T(8,128)(2,1)S(1)}, bf16[128,2048]{1,0:T(8,128)(2,1)S(1)}, u32[]{:S(2)}, u32[]{:S(2)}) collective-permute-start(bf16[128,2048]{1,0:T(8,128)(2,1)S(1)} %add_convert_fusion), channel_id=1, source_target_pairs={{0,4},{4,0},{1,5},{5,1},{2,6},{6,2},{3,7},{7,3},{8,12},{12,8},{9,1... | collective-permute-start | bytes 1572872 | tf_op jit(solution)/shard_map/ppermute | solution.py:412
  46.4 17.3 %collective-permute-start.7 = (bf16[128,2048]{1,0:T(8,128)(2,1)S(1)}, bf16[128,2048]{1,0:T(8,128)(2,1)S(1)}, u32[]{:S(2)}, u32[]{:S(2)}) collective-permute-start(bf16[128,2048]{1,0:T(8,128)(2,1)S(1)} %get-tuple-element.39), channel_id=1, source_target_pairs={{0,2},{2,0},{1,3},{3,1},{4,6},{6,4},{5,7},{7,5},{8,10},{10,8},{9,1... | collective-permute-start | bytes 1572872 | tf_op jit(solution)/shard_map/ppermute | solution.py:412
  63.8 8.5 %collective-permute-start.13 = (bf16[32,2048]{1,0:T(8,128)(2,1)S(1)}, bf16[32,2048]{1,0:T(8,128)(2,1)S(1)}, u32[]{:S(2)}, u32[]{:S(2)}) collective-permute-start(bf16[32,2048]{1,0:T(8,128)(2,1)S(1)} %get-tuple-element.49), channel_id=1, source_target_pairs={{0,24},{8,0},{16,8},{24,16},{1,25},{9,1},{17,9},{25,17},{2,26},{10... | collective-permute-start | bytes 393224 | tf_op jit(solution)/shard_map/ppermute | solution.py:553
  64.7 14.8 %collective-permute-start.12 = (bf16[32,2048]{1,0:T(8,128)(2,1)S(1)}, bf16[32,2048]{1,0:T(8,128)(2,1)S(1)}, u32[]{:S(2)}, u32[]{:S(2)}) collective-permute-start(bf16[32,2048]{1,0:T(8,128)(2,1)S(1)} %get-tuple-element.50), channel_id=1, source_target_pairs={{0,16},{8,24},{16,0},{24,8},{1,17},{9,25},{17,1},{25,9},{2,18},{10... | collective-permute-start | bytes 393224 | tf_op jit(solution)/shard_map/ppermute | solution.py:553
  65.3 14.1 %collective-permute-start.11 = (bf16[32,2048]{1,0:T(8,128)(2,1)S(1)}, bf16[32,2048]{1,0:T(8,128)(2,1)S(1)}, u32[]{:S(2)}, u32[]{:S(2)}) collective-permute-start(bf16[32,2048]{1,0:T(8,128)(2,1)S(1)} %get-tuple-element.51), channel_id=1, source_target_pairs={{0,8},{8,16},{16,24},{24,0},{1,9},{9,17},{17,25},{25,1},{2,10},{10... | collective-permute-start | bytes 393224 | tf_op jit(solution)/shard_map/ppermute | solution.py:553
  67.3 14.5 %collective-permute-start.15 = (bf16[32,2048]{1,0:T(8,128)(2,1)S(1)}, bf16[32,2048]{1,0:T(8,128)(2,1)S(1)}, u32[]{:S(2)}, u32[]{:S(2)}) collective-permute-start(bf16[32,2048]{1,0:T(8,128)(2,1)S(1)} %get-tuple-element.43), channel_id=1, source_target_pairs={{0,1},{1,0},{2,3},{3,2},{4,5},{5,4},{6,7},{7,6},{8,9},{9,8},{10,11... | collective-permute-start | bytes 393224 | tf_op jit(solution)/shard_map/ppermute | solution.py:412
  68.8 12.3 %all-to-all-start.3 = ((bf16[16,32,128]{2,1,0:T(8,128)(2,1)}), bf16[16,32,128]{2,1,0:T(8,128)(2,1)S(1)}, u32[]{:S(2)}, u32[]{:S(2)}) async-start(bf16[16,32,128]{2,1,0:T(8,128)(2,1)} %get-tuple-element.45), calls=%async_computation.3 | async-start | bytes 262144 | tf_op jit(solution)/shard_map/all_to_all | solution.py:477
  72.3 8.8 %copy-start.1 = (bf16[1,128,1536]{2,1,0:T(8,128)(2,1)S(1)}, bf16[1,128,1536]{2,1,0:T(8,128)(2,1)}, u32[]{:S(2)}) copy-start(bf16[1,128,1536]{2,1,0:T(8,128)(2,1)} %param.9) | copy-start | bytes 1179652
  79.5 7.3 %collective-permute-start.14 = (bf16[32,2048]{1,0:T(8,128)(2,1)S(1)}, bf16[32,2048]{1,0:T(8,128)(2,1)S(1)}, u32[]{:S(2)}, u32[]{:S(2)}) collective-permute-start(bf16[32,2048]{1,0:T(8,128)(2,1)S(1)} %add_convert_fusion.1), channel_id=1, source_target_pairs={{0,1},{1,0},{2,3},{3,2},{4,5},{5,4},{6,7},{7,6},{8,9},{9,8},{10,11... | collective-permute-start | bytes 393224 | tf_op jit(solution)/shard_map/ppermute | solution.py:412
  81.8 3.1 %collective-permute-start.10 = (f32[2,1536]{1,0:T(2,128)S(1)}, f32[2,1536]{1,0:T(2,128)S(1)}, u32[]{:S(2)}, u32[]{:S(2)}) collective-permute-start(f32[2,1536]{1,0:T(2,128)S(1)} %slice.59), channel_id=1, source_target_pairs={{2,0},{4,2},{6,4},{8,6},{10,8},{12,10},{14,12},{16,14},{18,16},{20... | collective-permute-start | bytes 36872 | tf_op jit(solution)/shard_map/ppermute | solution.py:567

commit v4 on v3

--- a/solution.py
+++ b/solution.py
@@ -17,7 +17,6 @@
 LANES = 128
 VMEM_LIMIT = 8 << 20
 SMEM = pl.BlockSpec(memory_space=pltpu.SMEM)
-HBM = pl.BlockSpec(memory_space=pltpu.HBM)
 
 
 def split_bf16(values):
@@ -165,20 +164,7 @@
 
 
 def backward_kernel(
-    d_long,
-    filt_spec,
-    gated,
-    twist,
-    matrix,
-    d_gated,
-    d_filter,
-    work,
-    signal,
-    held,
-    *,
-    blocks,
-    chans,
-    scale,
+    d_long, filt_spec, twist, matrix, d_gated, work, signal, *, blocks, chans
 ):
     for n1 in range(blocks):
         signal[n1] = d_long[n1].astype(F32)
@@ -186,15 +172,27 @@
     def load(n1, rows):
         return signal[n1, rows, :]
 
-    held[...] = to_spectrum(load, blocks, chans, twist, matrix, work)
-
     def store(n1, rows, value):
         signal[n1, rows, :] = value
 
-    spec = conj_times(filt_spec[...], held[...])
+    spec = conj_times(filt_spec[...], to_spectrum(load, blocks, chans, twist, matrix, work))
     from_spectrum(spec, blocks, chans, twist, matrix, work, store)
     for n1 in range(blocks):
         d_gated[n1] = signal[n1].astype(BF16)
+
+
+def filter_grad_kernel(
+    d_long, gated, twist, matrix, d_filter, work, signal, held, *, blocks, chans, scale
+):
+    def load(n1, rows):
+        return signal[n1, rows, :]
+
+    def store(n1, rows, value):
+        signal[n1, rows, :] = value
+
+    for n1 in range(blocks):
+        signal[n1] = d_long[n1].astype(F32)
+    held[...] = to_spectrum(load, blocks, chans, twist, matrix, work)
     for n1 in range(blocks):
         signal[n1] = gated[n1].astype(F32)
     spec = conj_times(to_spectrum(load, blocks, chans, twist, matrix, work), held[...])
@@ -524,12 +522,12 @@
         scratch=[pltpu.VMEM(flat, F32)],
         flops=1024,
     )
-    d_gated_cols, filter_part = call(
-        functools.partial(backward_kernel, scale=grad_scale, **sizes),
-        [(blocked, BF16), ((chans, seq_len), BF16)],
-        (d_long_cols, filt_spec, gated_cols, *tables),
-        scratch=[work, signal, work],
-        flops=3 * fft_flops,
+    (d_gated_cols,) = call(
+        functools.partial(backward_kernel, **sizes),
+        [(blocked, BF16)],
+        (d_long_cols, filt_spec, *tables),
+        scratch=[work, signal],
+        flops=2 * fft_flops,
     )
     (output,) = call(
         functools.partial(output_kernel, tile=512),
@@ -541,12 +539,19 @@
     near_sum, over_sum, near_send, over_send = sums
     over_core, near_core = swap(over_send, "c"), swap(near_send, "c")
     over_sum = over_sum.astype(F32) + after(over_core, output).astype(F32)
-    got = after(swap(over_sum.astype(BF16), "h"), filter_part)
+    got = after(swap(over_sum.astype(BF16), "h"), d_gated_cols)
     total = [
         near_sum[at].astype(F32) + near_core[at].astype(F32) + got[at].astype(F32)
         for at in (slice(i * chans, (i + 1) * chans) for i in range(lines))
     ]
     sent = [total[lines - step].astype(BF16) for step in range(1, lines)]
+    (filter_part,) = call(
+        functools.partial(filter_grad_kernel, scale=grad_scale, **sizes),
+        [((chans, seq_len), BF16)],
+        (after(d_long_cols, *sent), gated_cols, *tables),
+        scratch=[work, signal, work],
+        flops=3 * fft_flops,
+    )
     filter_sum = dp_start(filter_part)
     total_here = after(total[0], *sent)
     for step, block in enumerate(sent, 1):

time: 88.7 us -> 88.4 us (level)
  waiting for transfers between devices: 22.9 us -> 21.3 us
  Pallas kernels: 13.2 us -> 14.5 us
    ppermute x3, waiting for transfers between devices: 7.07 us -> 5.51 us  [per_device(): total_here += lax.ppermute(block, 'l', line_route(lines, step)).astype(F32)]
    pallas_call x10 -> x11, Pallas kernels: 13.2 us -> 14.5 us  [call(): pl.pallas_call(kernel, grid=(1,), out_shape=out_shape, in_specs=[SMEM if...]
  transfers between devices with their start and end apart: 19 -> 19, of which waited for: 7 -> 7; matrix products, arithmetic and copies ran while one was open for 1% -> 1% of each run, Pallas kernels for 12% -> 14%
where the time goes in v4:
time: 88.4 us; the launch traced here: 87.4 us
  starting transfers between devices  30.7 us (35%)
  waiting for transfers between devices  21.3 us (24%)
  blocking collectives  15.1 us (17%)
  Pallas kernels  14.5 us (16%)
  local copies, waits for them, and re-layouts  2.93 us (3%)
  other arithmetic  1.95 us (2%)
    all_to_all x1, blocking collectives, exchange(): return lax.all_to_all(block, axes, 0, 0, tiled=True)  15.1 us
    pallas_call x11, Pallas kernels, call(): pl.pallas_call(kernel, grid=(1,), out_shape=out_shape, in_specs=[SMEM if...  14.5 us
    all_to_all x3, starting transfers between devices, exchange(): return lax.all_to_all(block, axes, 0, 0, tiled=True)  12.7 us
    all_to_all x3, waiting for transfers between devices, exchange(): return lax.all_to_all(block, axes, 0, 0, tiled=True)  11 us
    ppermute x3, starting transfers between devices, along_line(): lax.ppermute(block, 'l', line_route(lines, step))  5.68 us
    ppermute x3, waiting for transfers between devices, per_device(): total_here += lax.ppermute(block, 'l', line_route(lines, step)).astype(F32)  5.51 us
    ppermute x8, starting transfers between devices, swap(): return lax.ppermute(block, axis, SWAP)  5.25 us
    ppermute x3, starting transfers between devices, per_device(): total_here += lax.ppermute(block, 'l', line_route(lines, step)).astype(F32)  3.45 us
  transfers between devices with their start and end apart: 19, of which 7 were waited for; matrix products, arithmetic and copies ran while one was open for 1% of the time, Pallas kernels for 14%

profile of v4, /device:TPU:0, one launch (start us, length us, event | category | flops | bytes accessed | tf_op | source)
XLA Modules:
  0.0 87.4 jit_solution(794689098873196254)
XLA Ops:
  0.6 0.8 slice_bitcast_fusion
  1.4 2.4 %collective-permute-start = (bf16[2,1536]{1,0:T(2,128)(2,1)S(1)}, bf16[2,1536]{1,0:T(2,128)(2,1)S(1)}, u32[]{:S(2)}, u32[]{:S(2)}) collective-permute-start(bf16[2,1536]{1,0:T(2,128)(2,1)S(1)} %slice_bitcast_fusion), channel_id=1, source_target_pairs={{0,2},{2,4},{4,6},{6,8},{8,10},{10,12},{12,14},{14,16},{16,18},{18... | collective-permute-start | bytes 18440 | tf_op jit(solution)/shard_map/ppermute | solution.py:448
  3.8 4.7 %collective-permute-start.3 = (bf16[32,2048]{1,0:T(8,128)(2,1)}, bf16[32,2048]{1,0:T(8,128)(2,1)S(1)}, u32[]{:S(2)}, u32[]{:S(2)}) collective-permute-start(bf16[32,2048]{1,0:T(8,128)(2,1)} %param.12), channel_id=1, source_target_pairs={{0,24},{8,0},{16,8},{24,16},{1,25},{9,1},{17,9},{25,17},{2,26},{10... | collective-permute-start | bytes 393224 | tf_op jit(solution)/shard_map/ppermute | solution.py:429
  8.4 0.0 collective-permute-start.2
  8.4 1.0 %collective-permute-start.1 = (bf16[32,2048]{1,0:T(8,128)(2,1)}, bf16[32,2048]{1,0:T(8,128)(2,1)S(1)}, u32[]{:S(2)}, u32[]{:S(2)}) collective-permute-start(bf16[32,2048]{1,0:T(8,128)(2,1)} %param.12), channel_id=1, source_target_pairs={{0,8},{8,16},{16,24},{24,0},{1,9},{9,17},{17,25},{25,1},{2,10},{10... | collective-permute-start | bytes 393224 | tf_op jit(solution)/shard_map/ppermute | solution.py:429
  9.4 0.7 copy-done.9
  10.1 0.0 copy-done.10
  10.1 0.1 pad_add_fusion.scalars
  10.2 0.0 collective-permute-done.earlier
  10.2 1.0 %copy-done = bf16[1,128,1536]{2,1,0:T(8,128)(2,1)S(1)} copy-done((bf16[1,128,1536]{2,1,0:T(8,128)(2,1)S(1)}, bf16[1,128,1536]{2,1,0:T(8,128)(2,1)}, u32[]{:S(2)}) %copy-start) | copy-done | bytes 393240
  11.2 1.6 %shard_map.120 = (bf16[512,128]{1,0:T(8,128)(2,1)}, f32[512,128]{1,0:T(8,128)S(1)}) custom-call(s32[5]{0:T(128)S(1)} %pad_add_fusion.scalars, bf16[128,1536]{1,0:T(8,128)(2,1)S(1)} %bitcast.11, bf16[2,1536]{1,0:T(2,128)(2,1)S(1)} %collective-permute-done.earlier, f32[3,1536]{1,0:T(4,128)S(1)} %copy-done.6), custom_call_target="tpu_custom_call" | custom-call | flops 1048576 | bytes 1024 | tf_op jit(solution)/shard_map/pallas_call | solution.py:388
  12.8 5.3 %all-to-all-start = ((bf16[16,32,128]{2,1,0:T(8,128)(2,1)}), bf16[16,32,128]{2,1,0:T(8,128)(2,1)S(1)}, u32[]{:S(2)}, u32[]{:S(2)}) async-start(bf16[16,32,128]{2,1,0:T(8,128)(2,1)} %bitcast.3), calls=%async_computation | async-start | bytes 262144 | tf_op jit(solution)/shard_map/all_to_all | solution.py:475
  18.1 0.0 copy-start.8
  18.1 0.5 shard_map.121.filt_spec
  18.5 0.4 copy-done.8
  19.0 0.0 collective-permute-done.1
  19.0 2.2 %collective-permute-done.2 = bf16[32,2048]{1,0:T(8,128)(2,1)S(1)} collective-permute-done((bf16[32,2048]{1,0:T(8,128)(2,1)}, bf16[32,2048]{1,0:T(8,128)(2,1)S(1)}, u32[]{:S(2)}, u32[]{:S(2)}) %collective-permute-start.2) | collective-permute-done | bytes 131104 | tf_op jit(solution)/shard_map/ppermute | solution.py:429
  21.3 0.0 collective-permute-done.3
  21.3 1.2 %collective-permute-start.4 = (bf16[128,2048]{1,0:T(8,128)(2,1)S(1)}, bf16[128,2048]{1,0:T(8,128)(2,1)S(1)}, u32[]{:S(2)}, u32[]{:S(2)}) collective-permute-start(bf16[128,2048]{1,0:T(8,128)(2,1)S(1)} %constant_dynamic-update-slice_fusion.refs_0_), channel_id=1, source_target_pairs={{0,4},{4,0},{1,5},{5,1},{2,6},{6,2},{3,7},{7,3},{8,12},{12,8},{9,1... | collective-permute-start | bytes 1572872 | tf_op jit(solution)/shard_map/ppermute | solution.py:410
  22.4 3.5 %all-to-all-done.gated = bf16[16,32,128]{2,1,0:T(8,128)(2,1)S(1)} async-done(((bf16[16,32,128]{2,1,0:T(8,128)(2,1)}), bf16[16,32,128]{2,1,0:T(8,128)(2,1)S(1)}, u32[]{:S(2)}, u32[]{:S(2)}) %all-to-all-start) | async-done | bytes 131104 | tf_op jit(solution)/shard_map/all_to_all | solution.py:475
  26.0 1.8 %shard_map.122 = bf16[16,32,128]{2,1,0:T(8,128)(2,1)} custom-call(bf16[16,32,128]{2,1,0:T(8,128)(2,1)S(1)} %all-to-all-done.gated, f32[544,256]{1,0:T(8,128)S(1)} %shard_map.121.filt_spec, f32[2,17,128]{2,1,0:T(8,128)S(1)} %copy-done.7, bf16[2,256,256]{2,1,0:T(8,128)(2,1)S(1)} %copy-done.4), custom_call_target="tpu_custom_call" | custom-call | flops 32212254720 | bytes 1024 | tf_op jit(solution)/shard_map/pallas_call | solution.py:388
  27.8 3.9 %all-to-all-start.1 = ((bf16[16,32,128]{2,1,0:T(8,128)(2,1)}), bf16[16,32,128]{2,1,0:T(8,128)(2,1)S(1)}, u32[]{:S(2)}, u32[]{:S(2)}) async-start(bf16[16,32,128]{2,1,0:T(8,128)(2,1)} %shard_map.122), calls=%async_computation.1 | async-start | bytes 262144 | tf_op jit(solution)/shard_map/all_to_all | solution.py:475
  31.8 0.4 collective-permute-start.5
  32.2 7.5 %all-to-all-done.1 = bf16[16,32,128]{2,1,0:T(8,128)(2,1)S(1)} async-done(((bf16[16,32,128]{2,1,0:T(8,128)(2,1)}), bf16[16,32,128]{2,1,0:T(8,128)(2,1)S(1)}, u32[]{:S(2)}, u32[]{:S(2)}) %all-to-all-start.1) | async-done | bytes 131104 | tf_op jit(solution)/shard_map/all_to_all | solution.py:475
  39.7 0.0 collective-permute-done.4.refs_1_
  39.7 0.0 collective-permute-start.6
  39.7 0.7 shard_map.123.cot
  40.4 0.0 collective-permute-done.5.refs_2_
  40.4 1.2 %collective-permute-done.6.refs_3_ = bf16[128,2048]{1,0:T(8,128)(2,1)S(1)} collective-permute-done((bf16[128,2048]{1,0:T(8,128)(2,1)S(1)}, bf16[128,2048]{1,0:T(8,128)(2,1)S(1)}, u32[]{:S(2)}, u32[]{:S(2)}) %collective-permute-start.6) | collective-permute-done | bytes 524320 | tf_op jit(solution)/shard_map/ppermute | solution.py:410
  41.6 1.3 %shard_map.124 = (f32[512,128]{1,0:T(8,128)S(1)}, bf16[512,128]{1,0:T(8,128)(2,1)S(1)}) custom-call(s32[5]{0:T(128)S(1)} %pad_add_fusion.scalars, bf16[128,2048]{1,0:T(8,128)(2,1)S(1)} %shard_map.123.cot, f32[512,128]{1,0:T(8,128)S(1)} %get-tuple-element.27.query_t, bf16[128,2048]{1,0:T(8,128)(2,1)S(1)} %constant_dynamic-update-slice_fusion.refs_0_, ...), custom_call_target="tpu_custom_call" | custom-call | flops 268435456 | bytes 1024 | tf_op jit(solution)/shard_map/pallas_call | solution.py:388
  42.9 1.3 %shard_map.125 = (bf16[4,128,128]{2,1,0:T(8,128)(2,1)S(1)}, bf16[128,2048]{1,0:T(8,128)(2,1)S(1)}, bf16[128,2048]{1,0:T(8,128)(2,1)S(1)}, bf16[128,2048]{1,0:T(8,128)(2,1)S(1)}, bf16[128,2048]{1,0:T(8,128)(2,1)S(1)}) custom-call(s32[5]{0:T(128)S(1)} %pad_add_fusion.scalars, bf16[512,128]{1,0:T(8,128)(2,1)S(1)} %bitcast.14, ...), custom_call_target="tpu_custom_call" | custom-call | flops 1024 | bytes 1024 | tf_op jit(solution)/shard_map/pallas_call | solution.py:388
  44.2 0.2 collective-permute-start.8
  44.4 1.5 %shard_map.126 = bf16[128,2048]{1,0:T(8,128)(2,1)} custom-call(bf16[4,128,128]{2,1,0:T(8,128)(2,1)S(1)} %get-tuple-element.34.product, bf16[128,2048]{1,0:T(8,128)(2,1)S(1)} %constant_dynamic-update-slice_fusion.refs_0_, bf16[128,2048]{1,0:T(8,128)(2,1)S(1)} %collective-permute-done.4.refs_1_, bf16[128,2048]{1,0:T(8,128)(2,1)S(1)} %collective-permute-done.5.refs_2_, ...), custom_call_target="tpu_custom_call" | custom-call | flops 268435456 | bytes 1024 | tf_op jit(solution)/shard_map/pallas_call | solution.py:388
  45.9 0.3 collective-permute-done.8
  46.1 0.1 add_convert_fusion
  46.3 0.0 copy-start.5
  46.3 0.1 collective-permute-start.9
  46.4 0.2 collective-permute-start.7
  46.6 15.1 %all_to_all.20.d_long = bf16[16,32,128]{2,1,0:T(8,128)(2,1)S(1)} all-to-all(bf16[16,32,128]{2,1,0:T(8,128)(2,1)S(1)} %bitcast.20), channel_id=1, replica_groups=mesh['l'=4,'h'=2,'c'=2,'dp'=2] {'l','h','c'}, dimensions={0} | all-to-all | bytes 262144 | tf_op jit(solution)/shard_map/all_to_all | solution.py:475
  61.6 1.8 %shard_map.127 = bf16[16,32,128]{2,1,0:T(8,128)(2,1)} custom-call(bf16[16,32,128]{2,1,0:T(8,128)(2,1)S(1)} %all_to_all.20.d_long, f32[544,256]{1,0:T(8,128)S(1)} %shard_map.121.filt_spec, f32[2,17,128]{2,1,0:T(8,128)S(1)} %copy-done.7, bf16[2,256,256]{2,1,0:T(8,128)(2,1)S(1)} %copy-done.5), custom_call_target="tpu_custom_call" | custom-call | flops 427819008 | bytes 1024 | tf_op jit(solution)/shard_map/pallas_call | solution.py:388
  63.5 0.0 collective-permute-done.9
  63.5 0.0 collective-permute-done.7
  63.5 0.2 convert_add_fusion.2
  63.7 0.8 collective-permute-start.13
  64.5 0.7 collective-permute-start.12
  65.2 1.9 %collective-permute-start.11 = (bf16[32,2048]{1,0:T(8,128)(2,1)S(1)}, bf16[32,2048]{1,0:T(8,128)(2,1)S(1)}, u32[]{:S(2)}, u32[]{:S(2)}) collective-permute-start(bf16[32,2048]{1,0:T(8,128)(2,1)S(1)} %get-tuple-element.49), channel_id=1, source_target_pairs={{0,8},{8,16},{16,24},{24,0},{1,9},{9,17},{17,25},{25,1},{2,10},{10... | collective-permute-start | bytes 393224 | tf_op jit(solution)/shard_map/ppermute | solution.py:558
  67.2 3.5 %all-to-all-start.3 = ((bf16[16,32,128]{2,1,0:T(8,128)(2,1)}), bf16[16,32,128]{2,1,0:T(8,128)(2,1)S(1)}, u32[]{:S(2)}, u32[]{:S(2)}) async-start(bf16[16,32,128]{2,1,0:T(8,128)(2,1)} %shard_map.127), calls=%async_computation.3 | async-start | bytes 262144 | tf_op jit(solution)/shard_map/all_to_all | solution.py:475
  70.7 1.5 %shard_map.130 = bf16[32,2048]{1,0:T(8,128)(2,1)S(1)} custom-call(bf16[16,32,128]{2,1,0:T(8,128)(2,1)S(1)} %all_to_all.20.d_long, bf16[16,32,128]{2,1,0:T(8,128)(2,1)S(1)} %all-to-all-done.gated, f32[2,17,128]{2,1,0:T(8,128)S(1)} %copy-done.7, bf16[2,256,256]{2,1,0:T(8,128)(2,1)S(1)} %copy-done.5), custom_call_target="tpu_custom_call" | custom-call | flops 641728512 | bytes 1024 | tf_op jit(solution)/shard_map/pallas_call | solution.py:388
  72.2 0.0 copy-start.1
  72.2 1.6 %collective-permute-start.15 = (bf16[32,2048]{1,0:T(8,128)(2,1)S(1)}, bf16[32,2048]{1,0:T(8,128)(2,1)S(1)}, u32[]{:S(2)}, u32[]{:S(2)}) collective-permute-start(bf16[32,2048]{1,0:T(8,128)(2,1)S(1)} %shard_map.130), channel_id=1, source_target_pairs={{0,1},{1,0},{2,3},{3,2},{4,5},{5,4},{6,7},{7,6},{8,9},{9,8},{10,11... | collective-permute-start | bytes 393224 | tf_op jit(solution)/shard_map/ppermute | solution.py:410
  73.8 0.0 collective-permute-done.13
  73.8 5.5 %collective-permute-done.12 = bf16[32,2048]{1,0:T(8,128)(2,1)S(1)} collective-permute-done((bf16[32,2048]{1,0:T(8,128)(2,1)S(1)}, bf16[32,2048]{1,0:T(8,128)(2,1)S(1)}, u32[]{:S(2)}, u32[]{:S(2)}) %collective-permute-start.12) | collective-permute-done | bytes 131104 | tf_op jit(solution)/shard_map/ppermute | solution.py:558
  79.3 0.0 collective-permute-done.11
  79.3 0.1 add_convert_fusion.1
  79.4 1.6 %collective-permute-start.14 = (bf16[32,2048]{1,0:T(8,128)(2,1)S(1)}, bf16[32,2048]{1,0:T(8,128)(2,1)S(1)}, u32[]{:S(2)}, u32[]{:S(2)}) collective-permute-start(bf16[32,2048]{1,0:T(8,128)(2,1)S(1)} %add_convert_fusion.1), channel_id=1, source_target_pairs={{0,1},{1,0},{2,3},{3,2},{4,5},{5,4},{6,7},{7,6},{8,9},{9,8},{10,11... | collective-permute-start | bytes 393224 | tf_op jit(solution)/shard_map/ppermute | solution.py:410
  81.0 0.0 all-to-all-done.3
  81.0 0.7 shard_map.128
  81.7 1.3 %collective-permute-start.10 = (f32[2,1536]{1,0:T(2,128)S(1)}, f32[2,1536]{1,0:T(2,128)S(1)}, u32[]{:S(2)}, u32[]{:S(2)}) collective-permute-start(f32[2,1536]{1,0:T(2,128)S(1)} %slice.59), channel_id=1, source_target_pairs={{2,0},{4,2},{6,4},{8,6},{10,8},{12,10},{14,12},{16,14},{18,16},{20... | collective-permute-start | bytes 36872 | tf_op jit(solution)/shard_map/ppermute | solution.py:572
  83.0 0.0 collective-permute-done.15
  83.0 0.7 convert_add_fusion
  83.7 1.0 %collective-permute-done.10.later = f32[2,1536]{1,0:T(2,128)S(1)} collective-permute-done((f32[2,1536]{1,0:T(2,128)S(1)}, f32[2,1536]{1,0:T(2,128)S(1)}, u32[]{:S(2)}, u32[]{:S(2)}) %collective-permute-start.10) | collective-permute-done | bytes 12320 | tf_op jit(solution)/shard_map/ppermute | solution.py:572
  84.7 1.9 %shard_map.129 = bf16[128,1536]{1,0:T(8,128)(2,1)} custom-call(s32[5]{0:T(128)S(1)} %pad_add_fusion.scalars, bf16[128,1536]{1,0:T(8,128)(2,1)S(1)} %bitcast.13, bf16[2,1536]{1,0:T(2,128)(2,1)S(1)} %collective-permute-done.earlier, f32[3,1536]{1,0:T(4,128)S(1)} %copy-done.6, f32[512,128]{1,0:T(8,128)S(1)} %get-tuple-element.35.d_product_t, ...), custom_call_target="tpu_custom_call" | custom-call | flops 1048576 | bytes 1024 | tf_op jit(solution)/shard_map/pallas_call | solution.py:388
  86.7 0.0 collective-permute-done.14
  86.7 0.7 convert_add_fusion.1
  (20 shorter events, 0.1 us)
Async XLA Ops:
  0.6 9.6 %copy-start.6 = (f32[3,1536]{1,0:T(4,128)S(1)}, f32[3,1536]{1,0:T(4,128)}, u32[]{:S(2)}) copy-start(f32[3,1536]{1,0:T(4,128)} %taps.5) | copy-start | bytes 55300
  1.4 8.8 %collective-permute-start = (bf16[2,1536]{1,0:T(2,128)(2,1)S(1)}, bf16[2,1536]{1,0:T(2,128)(2,1)S(1)}, u32[]{:S(2)}, u32[]{:S(2)}) collective-permute-start(bf16[2,1536]{1,0:T(2,128)(2,1)S(1)} %slice_bitcast_fusion), channel_id=1, source_target_pairs={{0,2},{2,4},{4,6},{6,8},{8,10},{10,12},{12,14},{14,16},{16,18},{18... | collective-permute-start | bytes 18440 | tf_op jit(solution)/shard_map/ppermute | solution.py:448
  3.8 17.5 %collective-permute-start.3 = (bf16[32,2048]{1,0:T(8,128)(2,1)}, bf16[32,2048]{1,0:T(8,128)(2,1)S(1)}, u32[]{:S(2)}, u32[]{:S(2)}) collective-permute-start(bf16[32,2048]{1,0:T(8,128)(2,1)} %param.12), channel_id=1, source_target_pairs={{0,24},{8,0},{16,8},{24,16},{1,25},{9,1},{17,9},{25,17},{2,26},{10... | collective-permute-start | bytes 393224 | tf_op jit(solution)/shard_map/ppermute | solution.py:429
  8.4 12.8 %collective-permute-start.2 = (bf16[32,2048]{1,0:T(8,128)(2,1)}, bf16[32,2048]{1,0:T(8,128)(2,1)S(1)}, u32[]{:S(2)}, u32[]{:S(2)}) collective-permute-start(bf16[32,2048]{1,0:T(8,128)(2,1)} %param.12), channel_id=1, source_target_pairs={{0,16},{8,24},{16,0},{24,8},{1,17},{9,25},{17,1},{25,9},{2,18},{10... | collective-permute-start | bytes 393224 | tf_op jit(solution)/shard_map/ppermute | solution.py:429
  8.4 10.5 %collective-permute-start.1 = (bf16[32,2048]{1,0:T(8,128)(2,1)}, bf16[32,2048]{1,0:T(8,128)(2,1)S(1)}, u32[]{:S(2)}, u32[]{:S(2)}) collective-permute-start(bf16[32,2048]{1,0:T(8,128)(2,1)} %param.12), channel_id=1, source_target_pairs={{0,8},{8,16},{16,24},{24,0},{1,9},{9,17},{17,25},{25,1},{2,10},{10... | collective-permute-start | bytes 393224 | tf_op jit(solution)/shard_map/ppermute | solution.py:429
  9.4 0.7 copy-start.9
  9.4 0.7 copy-start.10
  10.2 1.0 %copy-start = (bf16[1,128,1536]{2,1,0:T(8,128)(2,1)S(1)}, bf16[1,128,1536]{2,1,0:T(8,128)(2,1)}, u32[]{:S(2)}) copy-start(bf16[1,128,1536]{2,1,0:T(8,128)(2,1)} %param.9) | copy-start | bytes 1179652
  11.2 6.8 %copy-start.3 = (f32[32,2048]{1,0:T(8,128)S(1)}, f32[32,2048]{1,0:T(8,128)}, u32[]{:S(2)}) copy-start(f32[32,2048]{1,0:T(8,128)} %filt) | copy-start | bytes 786436
  11.2 6.8 %copy-start.4 = (bf16[2,256,256]{2,1,0:T(8,128)(2,1)S(1)}, bf16[2,256,256]{2,1,0:T(8,128)(2,1)}, u32[]{:S(2)}) copy-start(bf16[2,256,256]{2,1,0:T(8,128)(2,1)} %constant.25.clone.matrix) | copy-start | bytes 786436
  12.8 5.3 %copy-start.7 = (f32[2,17,128]{2,1,0:T(8,128)S(1)}, f32[2,17,128]{2,1,0:T(8,128)}, u32[]{:S(2)}) copy-start(f32[2,17,128]{2,1,0:T(8,128)} %constant.24.clone.twist) | copy-start | bytes 52228
  12.8 13.2 %all-to-all-start = ((bf16[16,32,128]{2,1,0:T(8,128)(2,1)}), bf16[16,32,128]{2,1,0:T(8,128)(2,1)S(1)}, u32[]{:S(2)}, u32[]{:S(2)}) async-start(bf16[16,32,128]{2,1,0:T(8,128)(2,1)} %bitcast.3), calls=%async_computation | async-start | bytes 262144 | tf_op jit(solution)/shard_map/all_to_all | solution.py:475
  18.1 0.9 %copy-start.8 = (bf16[32,2048]{1,0:T(8,128)(2,1)S(1)}, bf16[32,2048]{1,0:T(8,128)(2,1)}, u32[]{:S(2)}) copy-start(bf16[32,2048]{1,0:T(8,128)(2,1)} %param.12) | copy-start | bytes 393220
  21.3 18.4 %collective-permute-start.4 = (bf16[128,2048]{1,0:T(8,128)(2,1)S(1)}, bf16[128,2048]{1,0:T(8,128)(2,1)S(1)}, u32[]{:S(2)}, u32[]{:S(2)}) collective-permute-start(bf16[128,2048]{1,0:T(8,128)(2,1)S(1)} %constant_dynamic-update-slice_fusion.refs_0_), channel_id=1, source_target_pairs={{0,4},{4,0},{1,5},{5,1},{2,6},{6,2},{3,7},{7,3},{8,12},{12,8},{9,1... | collective-permute-start | bytes 1572872 | tf_op jit(solution)/shard_map/ppermute | solution.py:410
  26.0 13.7 %copy-start.2 = (bf16[1,128,2048]{2,1,0:T(8,128)(2,1)S(1)}, bf16[1,128,2048]{2,1,0:T(8,128)(2,1)}, u32[]{:S(2)}) copy-start(bf16[1,128,2048]{2,1,0:T(8,128)(2,1)} %param.13) | copy-start | bytes 1572868
  27.8 11.9 %all-to-all-start.1 = ((bf16[16,32,128]{2,1,0:T(8,128)(2,1)}), bf16[16,32,128]{2,1,0:T(8,128)(2,1)S(1)}, u32[]{:S(2)}, u32[]{:S(2)}) async-start(bf16[16,32,128]{2,1,0:T(8,128)(2,1)} %shard_map.122), calls=%async_computation.1 | async-start | bytes 262144 | tf_op jit(solution)/shard_map/all_to_all | solution.py:475
  31.8 8.6 %collective-permute-start.5 = (bf16[128,2048]{1,0:T(8,128)(2,1)S(1)}, bf16[128,2048]{1,0:T(8,128)(2,1)S(1)}, u32[]{:S(2)}, u32[]{:S(2)}) collective-permute-start(bf16[128,2048]{1,0:T(8,128)(2,1)S(1)} %constant_dynamic-update-slice_fusion.refs_0_), channel_id=1, source_target_pairs={{0,2},{2,0},{1,3},{3,1},{4,6},{6,4},{5,7},{7,5},{8,10},{10,8},{9,1... | collective-permute-start | bytes 1572872 | tf_op jit(solution)/shard_map/ppermute | solution.py:410
  39.7 1.9 %collective-permute-start.6 = (bf16[128,2048]{1,0:T(8,128)(2,1)S(1)}, bf16[128,2048]{1,0:T(8,128)(2,1)S(1)}, u32[]{:S(2)}, u32[]{:S(2)}) collective-permute-start(bf16[128,2048]{1,0:T(8,128)(2,1)S(1)} %collective-permute-done.4.refs_1_), channel_id=1, source_target_pairs={{0,2},{2,0},{1,3},{3,1},{4,6},{6,4},{5,7},{7,5},{8,10},{10,8},{9,1... | collective-permute-start | bytes 1572872 | tf_op jit(solution)/shard_map/ppermute | solution.py:410
  44.2 2.0 %collective-permute-start.8 = (bf16[128,2048]{1,0:T(8,128)(2,1)S(1)}, bf16[128,2048]{1,0:T(8,128)(2,1)S(1)}, u32[]{:S(2)}, u32[]{:S(2)}) collective-permute-start(bf16[128,2048]{1,0:T(8,128)(2,1)S(1)} %get-tuple-element.39), channel_id=1, source_target_pairs={{0,2},{2,0},{1,3},{3,1},{4,6},{6,4},{5,7},{7,5},{8,10},{10,8},{9,1... | collective-permute-start | bytes 1572872 | tf_op jit(solution)/shard_map/ppermute | solution.py:410
  46.3 15.4 %copy-start.5 = (bf16[2,256,256]{2,1,0:T(8,128)(2,1)S(1)}, bf16[2,256,256]{2,1,0:T(8,128)(2,1)}, u32[]{:S(2)}) copy-start(bf16[2,256,256]{2,1,0:T(8,128)(2,1)} %constant.25.clone.matrix) | copy-start | bytes 786436
  46.3 17.2 %collective-permute-start.9 = (bf16[128,2048]{1,0:T(8,128)(2,1)S(1)}, bf16[128,2048]{1,0:T(8,128)(2,1)S(1)}, u32[]{:S(2)}, u32[]{:S(2)}) collective-permute-start(bf16[128,2048]{1,0:T(8,128)(2,1)S(1)} %add_convert_fusion), channel_id=1, source_target_pairs={{0,4},{4,0},{1,5},{5,1},{2,6},{6,2},{3,7},{7,3},{8,12},{12,8},{9,1... | collective-permute-start | bytes 1572872 | tf_op jit(solution)/shard_map/ppermute | solution.py:410
  46.4 17.1 %collective-permute-start.7 = (bf16[128,2048]{1,0:T(8,128)(2,1)S(1)}, bf16[128,2048]{1,0:T(8,128)(2,1)S(1)}, u32[]{:S(2)}, u32[]{:S(2)}) collective-permute-start(bf16[128,2048]{1,0:T(8,128)(2,1)S(1)} %get-tuple-element.37), channel_id=1, source_target_pairs={{0,2},{2,0},{1,3},{3,1},{4,6},{6,4},{5,7},{7,5},{8,10},{10,8},{9,1... | collective-permute-start | bytes 1572872 | tf_op jit(solution)/shard_map/ppermute | solution.py:410
  63.7 10.1 %collective-permute-start.13 = (bf16[32,2048]{1,0:T(8,128)(2,1)S(1)}, bf16[32,2048]{1,0:T(8,128)(2,1)S(1)}, u32[]{:S(2)}, u32[]{:S(2)}) collective-permute-start(bf16[32,2048]{1,0:T(8,128)(2,1)S(1)} %get-tuple-element.47), channel_id=1, source_target_pairs={{0,24},{8,0},{16,8},{24,16},{1,25},{9,1},{17,9},{25,17},{2,26},{10... | collective-permute-start | bytes 393224 | tf_op jit(solution)/shard_map/ppermute | solution.py:558
  64.5 14.8 %collective-permute-start.12 = (bf16[32,2048]{1,0:T(8,128)(2,1)S(1)}, bf16[32,2048]{1,0:T(8,128)(2,1)S(1)}, u32[]{:S(2)}, u32[]{:S(2)}) collective-permute-start(bf16[32,2048]{1,0:T(8,128)(2,1)S(1)} %get-tuple-element.48), channel_id=1, source_target_pairs={{0,16},{8,24},{16,0},{24,8},{1,17},{9,25},{17,1},{25,9},{2,18},{10... | collective-permute-start | bytes 393224 | tf_op jit(solution)/shard_map/ppermute | solution.py:558
  65.2 14.1 %collective-permute-start.11 = (bf16[32,2048]{1,0:T(8,128)(2,1)S(1)}, bf16[32,2048]{1,0:T(8,128)(2,1)S(1)}, u32[]{:S(2)}, u32[]{:S(2)}) collective-permute-start(bf16[32,2048]{1,0:T(8,128)(2,1)S(1)} %get-tuple-element.49), channel_id=1, source_target_pairs={{0,8},{8,16},{16,24},{24,0},{1,9},{9,17},{17,25},{25,1},{2,10},{10... | collective-permute-start | bytes 393224 | tf_op jit(solution)/shard_map/ppermute | solution.py:558
  67.2 13.8 %all-to-all-start.3 = ((bf16[16,32,128]{2,1,0:T(8,128)(2,1)}), bf16[16,32,128]{2,1,0:T(8,128)(2,1)S(1)}, u32[]{:S(2)}, u32[]{:S(2)}) async-start(bf16[16,32,128]{2,1,0:T(8,128)(2,1)} %shard_map.127), calls=%async_computation.3 | async-start | bytes 262144 | tf_op jit(solution)/shard_map/all_to_all | solution.py:475
  72.2 8.8 %copy-start.1 = (bf16[1,128,1536]{2,1,0:T(8,128)(2,1)S(1)}, bf16[1,128,1536]{2,1,0:T(8,128)(2,1)}, u32[]{:S(2)}) copy-start(bf16[1,128,1536]{2,1,0:T(8,128)(2,1)} %param.9) | copy-start | bytes 1179652
  72.2 10.8 %collective-permute-start.15 = (bf16[32,2048]{1,0:T(8,128)(2,1)S(1)}, bf16[32,2048]{1,0:T(8,128)(2,1)S(1)}, u32[]{:S(2)}, u32[]{:S(2)}) collective-permute-start(bf16[32,2048]{1,0:T(8,128)(2,1)S(1)} %shard_map.130), channel_id=1, source_target_pairs={{0,1},{1,0},{2,3},{3,2},{4,5},{5,4},{6,7},{7,6},{8,9},{9,8},{10,11... | collective-permute-start | bytes 393224 | tf_op jit(solution)/shard_map/ppermute | solution.py:410
  79.4 7.3 %collective-permute-start.14 = (bf16[32,2048]{1,0:T(8,128)(2,1)S(1)}, bf16[32,2048]{1,0:T(8,128)(2,1)S(1)}, u32[]{:S(2)}, u32[]{:S(2)}) collective-permute-start(bf16[32,2048]{1,0:T(8,128)(2,1)S(1)} %add_convert_fusion.1), channel_id=1, source_target_pairs={{0,1},{1,0},{2,3},{3,2},{4,5},{5,4},{6,7},{7,6},{8,9},{9,8},{10,11... | collective-permute-start | bytes 393224 | tf_op jit(solution)/shard_map/ppermute | solution.py:410
  81.7 3.1 %collective-permute-start.10 = (f32[2,1536]{1,0:T(2,128)S(1)}, f32[2,1536]{1,0:T(2,128)S(1)}, u32[]{:S(2)}, u32[]{:S(2)}) collective-permute-start(f32[2,1536]{1,0:T(2,128)S(1)} %slice.59), channel_id=1, source_target_pairs={{2,0},{4,2},{6,4},{8,6},{10,8},{12,10},{14,12},{16,14},{18,16},{20... | collective-permute-start | bytes 36872 | tf_op jit(solution)/shard_map/ppermute | solution.py:572

commit v5 on v4

--- a/solution.py
+++ b/solution.py
@@ -517,7 +517,7 @@
     product, *sums = call(
         functools.partial(partial_kernel, split=split, scale=grad_scale, tile=512),
         [((4, rows, lines * chans), BF16)] + [(part, BF16)] * (4 * CHUNKS),
-        (scalars, long_t, query_t, after(cot, d_long_t)),
+        (scalars, long_t, query_t, after(cot, *weights)),
         1,
         scratch=[pltpu.VMEM(flat, F32)],
         flops=1024,

time: 88.4 us -> 87.1 us (0.985)
  blocking collectives: 15.1 us -> 13.8 us
    all_to_all x1, blocking collectives: 15.1 us -> 13.8 us  [exchange(): return lax.all_to_all(block, axes, 0, 0, tiled=True)]
  transfers between devices with their start and end apart: 19 -> 19, of which waited for: 7 -> 7; matrix products, arithmetic and copies ran while one was open for 1% -> 1% of each run, Pallas kernels for 14% -> 15%
where the time goes in v5:
time: 87.1 us; the launch traced here: 86.1 us
  starting transfers between devices  30.7 us (35%)
  waiting for transfers between devices  21.3 us (24%)
  Pallas kernels  14.5 us (17%)
  blocking collectives  13.8 us (16%)
  local copies, waits for them, and re-layouts  2.93 us (3%)
  other arithmetic  1.95 us (2%)
  between operations  0.88 us (1%)
    pallas_call x11, Pallas kernels, call(): pl.pallas_call(kernel, grid=(1,), out_shape=out_shape, in_specs=[SMEM if...  14.5 us
    all_to_all x1, blocking collectives, exchange(): return lax.all_to_all(block, axes, 0, 0, tiled=True)  13.8 us
    all_to_all x3, starting transfers between devices, exchange(): return lax.all_to_all(block, axes, 0, 0, tiled=True)  12.7 us
    all_to_all x3, waiting for transfers between devices, exchange(): return lax.all_to_all(block, axes, 0, 0, tiled=True)  11 us
    ppermute x3, starting transfers between devices, along_line(): lax.ppermute(block, 'l', line_route(lines, step))  5.68 us
    ppermute x3, waiting for transfers between devices, per_device(): total_here += lax.ppermute(block, 'l', line_route(lines, step)).astype(F32)  5.51 us
    ppermute x8, starting transfers between devices, swap(): return lax.ppermute(block, axis, SWAP)  5.24 us
    ppermute x3, starting transfers between devices, per_device(): total_here += lax.ppermute(block, 'l', line_route(lines, step)).astype(F32)  3.44 us
  transfers between devices with their start and end apart: 19, of which 7 were waited for; matrix products, arithmetic and copies ran while one was open for 1% of the time, Pallas kernels for 15%

profile of v5, /device:TPU:0, one launch (start us, length us, event | category | flops | bytes accessed | tf_op | source)
XLA Modules:
  0.0 86.1 jit_solution(17817035748099527225)
XLA Ops:
  0.6 0.8 slice_bitcast_fusion
  1.4 2.4 %collective-permute-start = (bf16[2,1536]{1,0:T(2,128)(2,1)S(1)}, bf16[2,1536]{1,0:T(2,128)(2,1)S(1)}, u32[]{:S(2)}, u32[]{:S(2)}) collective-permute-start(bf16[2,1536]{1,0:T(2,128)(2,1)S(1)} %slice_bitcast_fusion), channel_id=1, source_target_pairs={{0,2},{2,4},{4,6},{6,8},{8,10},{10,12},{12,14},{14,16},{16,18},{18... | collective-permute-start | bytes 18440 | tf_op jit(solution)/shard_map/ppermute | solution.py:448
  3.8 4.7 %collective-permute-start.3 = (bf16[32,2048]{1,0:T(8,128)(2,1)}, bf16[32,2048]{1,0:T(8,128)(2,1)S(1)}, u32[]{:S(2)}, u32[]{:S(2)}) collective-permute-start(bf16[32,2048]{1,0:T(8,128)(2,1)} %param.12), channel_id=1, source_target_pairs={{0,24},{8,0},{16,8},{24,16},{1,25},{9,1},{17,9},{25,17},{2,26},{10... | collective-permute-start | bytes 393224 | tf_op jit(solution)/shard_map/ppermute | solution.py:429
  8.4 0.0 collective-permute-start.2
  8.4 1.0 %collective-permute-start.1 = (bf16[32,2048]{1,0:T(8,128)(2,1)}, bf16[32,2048]{1,0:T(8,128)(2,1)S(1)}, u32[]{:S(2)}, u32[]{:S(2)}) collective-permute-start(bf16[32,2048]{1,0:T(8,128)(2,1)} %param.12), channel_id=1, source_target_pairs={{0,8},{8,16},{16,24},{24,0},{1,9},{9,17},{17,25},{25,1},{2,10},{10... | collective-permute-start | bytes 393224 | tf_op jit(solution)/shard_map/ppermute | solution.py:429
  9.4 0.7 copy-done.9
  10.1 0.0 copy-done.10
  10.1 0.1 pad_add_fusion.scalars
  10.2 0.0 collective-permute-done.earlier
  10.2 1.0 %copy-done = bf16[1,128,1536]{2,1,0:T(8,128)(2,1)S(1)} copy-done((bf16[1,128,1536]{2,1,0:T(8,128)(2,1)S(1)}, bf16[1,128,1536]{2,1,0:T(8,128)(2,1)}, u32[]{:S(2)}) %copy-start) | copy-done | bytes 393240
  11.2 1.6 %shard_map.120 = (bf16[512,128]{1,0:T(8,128)(2,1)}, f32[512,128]{1,0:T(8,128)S(1)}) custom-call(s32[5]{0:T(128)S(1)} %pad_add_fusion.scalars, bf16[128,1536]{1,0:T(8,128)(2,1)S(1)} %bitcast.11, bf16[2,1536]{1,0:T(2,128)(2,1)S(1)} %collective-permute-done.earlier, f32[3,1536]{1,0:T(4,128)S(1)} %copy-done.6), custom_call_target="tpu_custom_call" | custom-call | flops 1048576 | bytes 1024 | tf_op jit(solution)/shard_map/pallas_call | solution.py:388
  12.8 5.3 %all-to-all-start = ((bf16[16,32,128]{2,1,0:T(8,128)(2,1)}), bf16[16,32,128]{2,1,0:T(8,128)(2,1)S(1)}, u32[]{:S(2)}, u32[]{:S(2)}) async-start(bf16[16,32,128]{2,1,0:T(8,128)(2,1)} %bitcast.3), calls=%async_computation | async-start | bytes 262144 | tf_op jit(solution)/shard_map/all_to_all | solution.py:475
  18.1 0.0 copy-start.8
  18.1 0.5 shard_map.121.filt_spec
  18.5 0.4 copy-done.8
  19.0 0.0 collective-permute-done.1
  19.0 2.2 %collective-permute-done.2 = bf16[32,2048]{1,0:T(8,128)(2,1)S(1)} collective-permute-done((bf16[32,2048]{1,0:T(8,128)(2,1)}, bf16[32,2048]{1,0:T(8,128)(2,1)S(1)}, u32[]{:S(2)}, u32[]{:S(2)}) %collective-permute-start.2) | collective-permute-done | bytes 131104 | tf_op jit(solution)/shard_map/ppermute | solution.py:429
  21.3 0.0 collective-permute-done.3
  21.3 1.2 %collective-permute-start.4 = (bf16[128,2048]{1,0:T(8,128)(2,1)S(1)}, bf16[128,2048]{1,0:T(8,128)(2,1)S(1)}, u32[]{:S(2)}, u32[]{:S(2)}) collective-permute-start(bf16[128,2048]{1,0:T(8,128)(2,1)S(1)} %constant_dynamic-update-slice_fusion.refs_0_), channel_id=1, source_target_pairs={{0,4},{4,0},{1,5},{5,1},{2,6},{6,2},{3,7},{7,3},{8,12},{12,8},{9,1... | collective-permute-start | bytes 1572872 | tf_op jit(solution)/shard_map/ppermute | solution.py:410
  22.4 3.5 %all-to-all-done.gated = bf16[16,32,128]{2,1,0:T(8,128)(2,1)S(1)} async-done(((bf16[16,32,128]{2,1,0:T(8,128)(2,1)}), bf16[16,32,128]{2,1,0:T(8,128)(2,1)S(1)}, u32[]{:S(2)}, u32[]{:S(2)}) %all-to-all-start) | async-done | bytes 131104 | tf_op jit(solution)/shard_map/all_to_all | solution.py:475
  26.0 1.8 %shard_map.122 = bf16[16,32,128]{2,1,0:T(8,128)(2,1)} custom-call(bf16[16,32,128]{2,1,0:T(8,128)(2,1)S(1)} %all-to-all-done.gated, f32[544,256]{1,0:T(8,128)S(1)} %shard_map.121.filt_spec, f32[2,17,128]{2,1,0:T(8,128)S(1)} %copy-done.7, bf16[2,256,256]{2,1,0:T(8,128)(2,1)S(1)} %copy-done.4), custom_call_target="tpu_custom_call" | custom-call | flops 32212254720 | bytes 1024 | tf_op jit(solution)/shard_map/pallas_call | solution.py:388
  27.8 3.9 %all-to-all-start.1 = ((bf16[16,32,128]{2,1,0:T(8,128)(2,1)}), bf16[16,32,128]{2,1,0:T(8,128)(2,1)S(1)}, u32[]{:S(2)}, u32[]{:S(2)}) async-start(bf16[16,32,128]{2,1,0:T(8,128)(2,1)} %shard_map.122), calls=%async_computation.1 | async-start | bytes 262144 | tf_op jit(solution)/shard_map/all_to_all | solution.py:475
  31.8 0.4 collective-permute-start.5
  32.2 7.5 %all-to-all-done.1 = bf16[16,32,128]{2,1,0:T(8,128)(2,1)S(1)} async-done(((bf16[16,32,128]{2,1,0:T(8,128)(2,1)}), bf16[16,32,128]{2,1,0:T(8,128)(2,1)S(1)}, u32[]{:S(2)}, u32[]{:S(2)}) %all-to-all-start.1) | async-done | bytes 131104 | tf_op jit(solution)/shard_map/all_to_all | solution.py:475
  39.7 0.0 collective-permute-done.4.refs_1_
  39.7 0.0 collective-permute-start.6
  39.7 0.7 shard_map.123.cot
  40.4 0.0 collective-permute-done.5.refs_2_
  40.4 1.2 %collective-permute-done.6.refs_3_ = bf16[128,2048]{1,0:T(8,128)(2,1)S(1)} collective-permute-done((bf16[128,2048]{1,0:T(8,128)(2,1)S(1)}, bf16[128,2048]{1,0:T(8,128)(2,1)S(1)}, u32[]{:S(2)}, u32[]{:S(2)}) %collective-permute-start.6) | collective-permute-done | bytes 524320 | tf_op jit(solution)/shard_map/ppermute | solution.py:410
  41.6 1.3 %shard_map.124 = (bf16[4,128,128]{2,1,0:T(8,128)(2,1)S(1)}, bf16[128,2048]{1,0:T(8,128)(2,1)S(1)}, bf16[128,2048]{1,0:T(8,128)(2,1)S(1)}, bf16[128,2048]{1,0:T(8,128)(2,1)S(1)}, bf16[128,2048]{1,0:T(8,128)(2,1)S(1)}) custom-call(s32[5]{0:T(128)S(1)} %pad_add_fusion.scalars, bf16[512,128]{1,0:T(8,128)(2,1)S(1)} %bitcast.14, ...), custom_call_target="tpu_custom_call" | custom-call | flops 1024 | bytes 1024 | tf_op jit(solution)/shard_map/pallas_call | solution.py:388
  42.9 0.2 collective-permute-start.8
  43.1 1.5 %shard_map.125 = bf16[128,2048]{1,0:T(8,128)(2,1)} custom-call(bf16[4,128,128]{2,1,0:T(8,128)(2,1)S(1)} %get-tuple-element.33.product, bf16[128,2048]{1,0:T(8,128)(2,1)S(1)} %constant_dynamic-update-slice_fusion.refs_0_, bf16[128,2048]{1,0:T(8,128)(2,1)S(1)} %collective-permute-done.4.refs_1_, bf16[128,2048]{1,0:T(8,128)(2,1)S(1)} %collective-permute-done.5.refs_2_, ...), custom_call_target="tpu_custom_call" | custom-call | flops 268435456 | bytes 1024 | tf_op jit(solution)/shard_map/pallas_call | solution.py:388
  44.6 0.3 collective-permute-done.8
  44.8 0.1 add_convert_fusion
  45.0 0.1 collective-permute-start.9
  45.1 0.2 collective-permute-start.7
  45.3 1.3 %shard_map.126 = (f32[512,128]{1,0:T(8,128)S(1)}, bf16[512,128]{1,0:T(8,128)(2,1)S(1)}) custom-call(s32[5]{0:T(128)S(1)} %pad_add_fusion.scalars, bf16[128,2048]{1,0:T(8,128)(2,1)S(1)} %shard_map.123.cot, f32[512,128]{1,0:T(8,128)S(1)} %get-tuple-element.27.query_t, bf16[128,2048]{1,0:T(8,128)(2,1)S(1)} %constant_dynamic-update-slice_fusion.refs_0_, ...), custom_call_target="tpu_custom_call" | custom-call | flops 268435456 | bytes 1024 | tf_op jit(solution)/shard_map/pallas_call | solution.py:388
  46.5 0.0 copy-start.5
  46.6 13.8 %all_to_all.20.d_long = bf16[16,32,128]{2,1,0:T(8,128)(2,1)S(1)} all-to-all(bf16[16,32,128]{2,1,0:T(8,128)(2,1)S(1)} %bitcast.20), channel_id=1, replica_groups=mesh['l'=4,'h'=2,'c'=2,'dp'=2] {'l','h','c'}, dimensions={0} | all-to-all | bytes 262144 | tf_op jit(solution)/shard_map/all_to_all | solution.py:475
  60.3 1.8 %shard_map.127 = bf16[16,32,128]{2,1,0:T(8,128)(2,1)} custom-call(bf16[16,32,128]{2,1,0:T(8,128)(2,1)S(1)} %all_to_all.20.d_long, f32[544,256]{1,0:T(8,128)S(1)} %shard_map.121.filt_spec, f32[2,17,128]{2,1,0:T(8,128)S(1)} %copy-done.7, bf16[2,256,256]{2,1,0:T(8,128)(2,1)S(1)} %copy-done.5), custom_call_target="tpu_custom_call" | custom-call | flops 427819008 | bytes 1024 | tf_op jit(solution)/shard_map/pallas_call | solution.py:388
  62.2 0.0 collective-permute-done.9
  62.2 0.0 collective-permute-done.7
  62.2 0.2 convert_add_fusion.2
  62.4 0.8 collective-permute-start.13
  63.2 0.7 collective-permute-start.12
  63.9 1.9 %collective-permute-start.11 = (bf16[32,2048]{1,0:T(8,128)(2,1)S(1)}, bf16[32,2048]{1,0:T(8,128)(2,1)S(1)}, u32[]{:S(2)}, u32[]{:S(2)}) collective-permute-start(bf16[32,2048]{1,0:T(8,128)(2,1)S(1)} %get-tuple-element.49), channel_id=1, source_target_pairs={{0,8},{8,16},{16,24},{24,0},{1,9},{9,17},{17,25},{25,1},{2,10},{10... | collective-permute-start | bytes 393224 | tf_op jit(solution)/shard_map/ppermute | solution.py:558
  65.8 3.5 %all-to-all-start.3 = ((bf16[16,32,128]{2,1,0:T(8,128)(2,1)}), bf16[16,32,128]{2,1,0:T(8,128)(2,1)S(1)}, u32[]{:S(2)}, u32[]{:S(2)}) async-start(bf16[16,32,128]{2,1,0:T(8,128)(2,1)} %shard_map.127), calls=%async_computation.3 | async-start | bytes 262144 | tf_op jit(solution)/shard_map/all_to_all | solution.py:475
  69.4 1.5 %shard_map.130 = bf16[32,2048]{1,0:T(8,128)(2,1)S(1)} custom-call(bf16[16,32,128]{2,1,0:T(8,128)(2,1)S(1)} %all_to_all.20.d_long, bf16[16,32,128]{2,1,0:T(8,128)(2,1)S(1)} %all-to-all-done.gated, f32[2,17,128]{2,1,0:T(8,128)S(1)} %copy-done.7, bf16[2,256,256]{2,1,0:T(8,128)(2,1)S(1)} %copy-done.5), custom_call_target="tpu_custom_call" | custom-call | flops 641728512 | bytes 1024 | tf_op jit(solution)/shard_map/pallas_call | solution.py:388
  70.9 0.0 copy-start.1
  70.9 1.6 %collective-permute-start.15 = (bf16[32,2048]{1,0:T(8,128)(2,1)S(1)}, bf16[32,2048]{1,0:T(8,128)(2,1)S(1)}, u32[]{:S(2)}, u32[]{:S(2)}) collective-permute-start(bf16[32,2048]{1,0:T(8,128)(2,1)S(1)} %shard_map.130), channel_id=1, source_target_pairs={{0,1},{1,0},{2,3},{3,2},{4,5},{5,4},{6,7},{7,6},{8,9},{9,8},{10,11... | collective-permute-start | bytes 393224 | tf_op jit(solution)/shard_map/ppermute | solution.py:410
  72.5 0.0 collective-permute-done.13
  72.5 5.5 %collective-permute-done.12 = bf16[32,2048]{1,0:T(8,128)(2,1)S(1)} collective-permute-done((bf16[32,2048]{1,0:T(8,128)(2,1)S(1)}, bf16[32,2048]{1,0:T(8,128)(2,1)S(1)}, u32[]{:S(2)}, u32[]{:S(2)}) %collective-permute-start.12) | collective-permute-done | bytes 131104 | tf_op jit(solution)/shard_map/ppermute | solution.py:558
  78.0 0.0 collective-permute-done.11
  78.0 0.1 add_convert_fusion.1
  78.0 1.6 %collective-permute-start.14 = (bf16[32,2048]{1,0:T(8,128)(2,1)S(1)}, bf16[32,2048]{1,0:T(8,128)(2,1)S(1)}, u32[]{:S(2)}, u32[]{:S(2)}) collective-permute-start(bf16[32,2048]{1,0:T(8,128)(2,1)S(1)} %add_convert_fusion.1), channel_id=1, source_target_pairs={{0,1},{1,0},{2,3},{3,2},{4,5},{5,4},{6,7},{7,6},{8,9},{9,8},{10,11... | collective-permute-start | bytes 393224 | tf_op jit(solution)/shard_map/ppermute | solution.py:410
  79.6 0.0 all-to-all-done.3
  79.7 0.7 shard_map.128
  80.3 1.3 %collective-permute-start.10 = (f32[2,1536]{1,0:T(2,128)S(1)}, f32[2,1536]{1,0:T(2,128)S(1)}, u32[]{:S(2)}, u32[]{:S(2)}) collective-permute-start(f32[2,1536]{1,0:T(2,128)S(1)} %slice.59), channel_id=1, source_target_pairs={{2,0},{4,2},{6,4},{8,6},{10,8},{12,10},{14,12},{16,14},{18,16},{20... | collective-permute-start | bytes 36872 | tf_op jit(solution)/shard_map/ppermute | solution.py:572
  81.6 0.0 collective-permute-done.15
  81.7 0.7 convert_add_fusion
  82.4 1.0 %collective-permute-done.10.later = f32[2,1536]{1,0:T(2,128)S(1)} collective-permute-done((f32[2,1536]{1,0:T(2,128)S(1)}, f32[2,1536]{1,0:T(2,128)S(1)}, u32[]{:S(2)}, u32[]{:S(2)}) %collective-permute-start.10) | collective-permute-done | bytes 12320 | tf_op jit(solution)/shard_map/ppermute | solution.py:572
  83.4 1.9 %shard_map.129 = bf16[128,1536]{1,0:T(8,128)(2,1)} custom-call(s32[5]{0:T(128)S(1)} %pad_add_fusion.scalars, bf16[128,1536]{1,0:T(8,128)(2,1)S(1)} %bitcast.13, bf16[2,1536]{1,0:T(2,128)(2,1)S(1)} %collective-permute-done.earlier, f32[3,1536]{1,0:T(4,128)S(1)} %copy-done.6, f32[512,128]{1,0:T(8,128)S(1)} %get-tuple-element.34.d_product_t, ...), custom_call_target="tpu_custom_call" | custom-call | flops 1048576 | bytes 1024 | tf_op jit(solution)/shard_map/pallas_call | solution.py:388
  85.4 0.0 collective-permute-done.14
  85.4 0.7 convert_add_fusion.1
  (20 shorter events, 0.1 us)
Async XLA Ops:
  0.6 9.6 %copy-start.6 = (f32[3,1536]{1,0:T(4,128)S(1)}, f32[3,1536]{1,0:T(4,128)}, u32[]{:S(2)}) copy-start(f32[3,1536]{1,0:T(4,128)} %taps.5) | copy-start | bytes 55300
  1.4 8.8 %collective-permute-start = (bf16[2,1536]{1,0:T(2,128)(2,1)S(1)}, bf16[2,1536]{1,0:T(2,128)(2,1)S(1)}, u32[]{:S(2)}, u32[]{:S(2)}) collective-permute-start(bf16[2,1536]{1,0:T(2,128)(2,1)S(1)} %slice_bitcast_fusion), channel_id=1, source_target_pairs={{0,2},{2,4},{4,6},{6,8},{8,10},{10,12},{12,14},{14,16},{16,18},{18... | collective-permute-start | bytes 18440 | tf_op jit(solution)/shard_map/ppermute | solution.py:448
  3.8 17.5 %collective-permute-start.3 = (bf16[32,2048]{1,0:T(8,128)(2,1)}, bf16[32,2048]{1,0:T(8,128)(2,1)S(1)}, u32[]{:S(2)}, u32[]{:S(2)}) collective-permute-start(bf16[32,2048]{1,0:T(8,128)(2,1)} %param.12), channel_id=1, source_target_pairs={{0,24},{8,0},{16,8},{24,16},{1,25},{9,1},{17,9},{25,17},{2,26},{10... | collective-permute-start | bytes 393224 | tf_op jit(solution)/shard_map/ppermute | solution.py:429
  8.4 12.8 %collective-permute-start.2 = (bf16[32,2048]{1,0:T(8,128)(2,1)}, bf16[32,2048]{1,0:T(8,128)(2,1)S(1)}, u32[]{:S(2)}, u32[]{:S(2)}) collective-permute-start(bf16[32,2048]{1,0:T(8,128)(2,1)} %param.12), channel_id=1, source_target_pairs={{0,16},{8,24},{16,0},{24,8},{1,17},{9,25},{17,1},{25,9},{2,18},{10... | collective-permute-start | bytes 393224 | tf_op jit(solution)/shard_map/ppermute | solution.py:429
  8.4 10.5 %collective-permute-start.1 = (bf16[32,2048]{1,0:T(8,128)(2,1)}, bf16[32,2048]{1,0:T(8,128)(2,1)S(1)}, u32[]{:S(2)}, u32[]{:S(2)}) collective-permute-start(bf16[32,2048]{1,0:T(8,128)(2,1)} %param.12), channel_id=1, source_target_pairs={{0,8},{8,16},{16,24},{24,0},{1,9},{9,17},{17,25},{25,1},{2,10},{10... | collective-permute-start | bytes 393224 | tf_op jit(solution)/shard_map/ppermute | solution.py:429
  9.4 0.7 copy-start.9
  9.4 0.7 copy-start.10
  10.2 1.0 %copy-start = (bf16[1,128,1536]{2,1,0:T(8,128)(2,1)S(1)}, bf16[1,128,1536]{2,1,0:T(8,128)(2,1)}, u32[]{:S(2)}) copy-start(bf16[1,128,1536]{2,1,0:T(8,128)(2,1)} %param.9) | copy-start | bytes 1179652
  11.2 6.8 %copy-start.3 = (f32[32,2048]{1,0:T(8,128)S(1)}, f32[32,2048]{1,0:T(8,128)}, u32[]{:S(2)}) copy-start(f32[32,2048]{1,0:T(8,128)} %filt) | copy-start | bytes 786436
  11.2 6.8 %copy-start.4 = (bf16[2,256,256]{2,1,0:T(8,128)(2,1)S(1)}, bf16[2,256,256]{2,1,0:T(8,128)(2,1)}, u32[]{:S(2)}) copy-start(bf16[2,256,256]{2,1,0:T(8,128)(2,1)} %constant.25.clone.matrix) | copy-start | bytes 786436
  12.8 5.3 %copy-start.7 = (f32[2,17,128]{2,1,0:T(8,128)S(1)}, f32[2,17,128]{2,1,0:T(8,128)}, u32[]{:S(2)}) copy-start(f32[2,17,128]{2,1,0:T(8,128)} %constant.24.clone.twist) | copy-start | bytes 52228
  12.8 13.2 %all-to-all-start = ((bf16[16,32,128]{2,1,0:T(8,128)(2,1)}), bf16[16,32,128]{2,1,0:T(8,128)(2,1)S(1)}, u32[]{:S(2)}, u32[]{:S(2)}) async-start(bf16[16,32,128]{2,1,0:T(8,128)(2,1)} %bitcast.3), calls=%async_computation | async-start | bytes 262144 | tf_op jit(solution)/shard_map/all_to_all | solution.py:475
  18.1 0.9 %copy-start.8 = (bf16[32,2048]{1,0:T(8,128)(2,1)S(1)}, bf16[32,2048]{1,0:T(8,128)(2,1)}, u32[]{:S(2)}) copy-start(bf16[32,2048]{1,0:T(8,128)(2,1)} %param.12) | copy-start | bytes 393220
  21.3 18.4 %collective-permute-start.4 = (bf16[128,2048]{1,0:T(8,128)(2,1)S(1)}, bf16[128,2048]{1,0:T(8,128)(2,1)S(1)}, u32[]{:S(2)}, u32[]{:S(2)}) collective-permute-start(bf16[128,2048]{1,0:T(8,128)(2,1)S(1)} %constant_dynamic-update-slice_fusion.refs_0_), channel_id=1, source_target_pairs={{0,4},{4,0},{1,5},{5,1},{2,6},{6,2},{3,7},{7,3},{8,12},{12,8},{9,1... | collective-permute-start | bytes 1572872 | tf_op jit(solution)/shard_map/ppermute | solution.py:410
  26.0 13.7 %copy-start.2 = (bf16[1,128,2048]{2,1,0:T(8,128)(2,1)S(1)}, bf16[1,128,2048]{2,1,0:T(8,128)(2,1)}, u32[]{:S(2)}) copy-start(bf16[1,128,2048]{2,1,0:T(8,128)(2,1)} %param.13) | copy-start | bytes 1572868
  27.8 11.9 %all-to-all-start.1 = ((bf16[16,32,128]{2,1,0:T(8,128)(2,1)}), bf16[16,32,128]{2,1,0:T(8,128)(2,1)S(1)}, u32[]{:S(2)}, u32[]{:S(2)}) async-start(bf16[16,32,128]{2,1,0:T(8,128)(2,1)} %shard_map.122), calls=%async_computation.1 | async-start | bytes 262144 | tf_op jit(solution)/shard_map/all_to_all | solution.py:475
  31.8 8.6 %collective-permute-start.5 = (bf16[128,2048]{1,0:T(8,128)(2,1)S(1)}, bf16[128,2048]{1,0:T(8,128)(2,1)S(1)}, u32[]{:S(2)}, u32[]{:S(2)}) collective-permute-start(bf16[128,2048]{1,0:T(8,128)(2,1)S(1)} %constant_dynamic-update-slice_fusion.refs_0_), channel_id=1, source_target_pairs={{0,2},{2,0},{1,3},{3,1},{4,6},{6,4},{5,7},{7,5},{8,10},{10,8},{9,1... | collective-permute-start | bytes 1572872 | tf_op jit(solution)/shard_map/ppermute | solution.py:410
  39.7 1.9 %collective-permute-start.6 = (bf16[128,2048]{1,0:T(8,128)(2,1)S(1)}, bf16[128,2048]{1,0:T(8,128)(2,1)S(1)}, u32[]{:S(2)}, u32[]{:S(2)}) collective-permute-start(bf16[128,2048]{1,0:T(8,128)(2,1)S(1)} %collective-permute-done.4.refs_1_), channel_id=1, source_target_pairs={{0,2},{2,0},{1,3},{3,1},{4,6},{6,4},{5,7},{7,5},{8,10},{10,8},{9,1... | collective-permute-start | bytes 1572872 | tf_op jit(solution)/shard_map/ppermute | solution.py:410
  42.9 2.0 %collective-permute-start.8 = (bf16[128,2048]{1,0:T(8,128)(2,1)S(1)}, bf16[128,2048]{1,0:T(8,128)(2,1)S(1)}, u32[]{:S(2)}, u32[]{:S(2)}) collective-permute-start(bf16[128,2048]{1,0:T(8,128)(2,1)S(1)} %get-tuple-element.39), channel_id=1, source_target_pairs={{0,2},{2,0},{1,3},{3,1},{4,6},{6,4},{5,7},{7,5},{8,10},{10,8},{9,1... | collective-permute-start | bytes 1572872 | tf_op jit(solution)/shard_map/ppermute | solution.py:410
  45.0 17.2 %collective-permute-start.9 = (bf16[128,2048]{1,0:T(8,128)(2,1)S(1)}, bf16[128,2048]{1,0:T(8,128)(2,1)S(1)}, u32[]{:S(2)}, u32[]{:S(2)}) collective-permute-start(bf16[128,2048]{1,0:T(8,128)(2,1)S(1)} %add_convert_fusion), channel_id=1, source_target_pairs={{0,4},{4,0},{1,5},{5,1},{2,6},{6,2},{3,7},{7,3},{8,12},{12,8},{9,1... | collective-permute-start | bytes 1572872 | tf_op jit(solution)/shard_map/ppermute | solution.py:410
  45.1 17.1 %collective-permute-start.7 = (bf16[128,2048]{1,0:T(8,128)(2,1)S(1)}, bf16[128,2048]{1,0:T(8,128)(2,1)S(1)}, u32[]{:S(2)}, u32[]{:S(2)}) collective-permute-start(bf16[128,2048]{1,0:T(8,128)(2,1)S(1)} %get-tuple-element.37), channel_id=1, source_target_pairs={{0,2},{2,0},{1,3},{3,1},{4,6},{6,4},{5,7},{7,5},{8,10},{10,8},{9,1... | collective-permute-start | bytes 1572872 | tf_op jit(solution)/shard_map/ppermute | solution.py:410
  46.5 13.8 %copy-start.5 = (bf16[2,256,256]{2,1,0:T(8,128)(2,1)S(1)}, bf16[2,256,256]{2,1,0:T(8,128)(2,1)}, u32[]{:S(2)}) copy-start(bf16[2,256,256]{2,1,0:T(8,128)(2,1)} %constant.25.clone.matrix) | copy-start | bytes 786436
  62.4 10.1 %collective-permute-start.13 = (bf16[32,2048]{1,0:T(8,128)(2,1)S(1)}, bf16[32,2048]{1,0:T(8,128)(2,1)S(1)}, u32[]{:S(2)}, u32[]{:S(2)}) collective-permute-start(bf16[32,2048]{1,0:T(8,128)(2,1)S(1)} %get-tuple-element.47), channel_id=1, source_target_pairs={{0,24},{8,0},{16,8},{24,16},{1,25},{9,1},{17,9},{25,17},{2,26},{10... | collective-permute-start | bytes 393224 | tf_op jit(solution)/shard_map/ppermute | solution.py:558
  63.2 14.8 %collective-permute-start.12 = (bf16[32,2048]{1,0:T(8,128)(2,1)S(1)}, bf16[32,2048]{1,0:T(8,128)(2,1)S(1)}, u32[]{:S(2)}, u32[]{:S(2)}) collective-permute-start(bf16[32,2048]{1,0:T(8,128)(2,1)S(1)} %get-tuple-element.48), channel_id=1, source_target_pairs={{0,16},{8,24},{16,0},{24,8},{1,17},{9,25},{17,1},{25,9},{2,18},{10... | collective-permute-start | bytes 393224 | tf_op jit(solution)/shard_map/ppermute | solution.py:558
  63.9 14.1 %collective-permute-start.11 = (bf16[32,2048]{1,0:T(8,128)(2,1)S(1)}, bf16[32,2048]{1,0:T(8,128)(2,1)S(1)}, u32[]{:S(2)}, u32[]{:S(2)}) collective-permute-start(bf16[32,2048]{1,0:T(8,128)(2,1)S(1)} %get-tuple-element.49), channel_id=1, source_target_pairs={{0,8},{8,16},{16,24},{24,0},{1,9},{9,17},{17,25},{25,1},{2,10},{10... | collective-permute-start | bytes 393224 | tf_op jit(solution)/shard_map/ppermute | solution.py:558
  65.8 13.8 %all-to-all-start.3 = ((bf16[16,32,128]{2,1,0:T(8,128)(2,1)}), bf16[16,32,128]{2,1,0:T(8,128)(2,1)S(1)}, u32[]{:S(2)}, u32[]{:S(2)}) async-start(bf16[16,32,128]{2,1,0:T(8,128)(2,1)} %shard_map.127), calls=%async_computation.3 | async-start | bytes 262144 | tf_op jit(solution)/shard_map/all_to_all | solution.py:475
  70.9 8.8 %copy-start.1 = (bf16[1,128,1536]{2,1,0:T(8,128)(2,1)S(1)}, bf16[1,128,1536]{2,1,0:T(8,128)(2,1)}, u32[]{:S(2)}) copy-start(bf16[1,128,1536]{2,1,0:T(8,128)(2,1)} %param.9) | copy-start | bytes 1179652
  70.9 10.8 %collective-permute-start.15 = (bf16[32,2048]{1,0:T(8,128)(2,1)S(1)}, bf16[32,2048]{1,0:T(8,128)(2,1)S(1)}, u32[]{:S(2)}, u32[]{:S(2)}) collective-permute-start(bf16[32,2048]{1,0:T(8,128)(2,1)S(1)} %shard_map.130), channel_id=1, source_target_pairs={{0,1},{1,0},{2,3},{3,2},{4,5},{5,4},{6,7},{7,6},{8,9},{9,8},{10,11... | collective-permute-start | bytes 393224 | tf_op jit(solution)/shard_map/ppermute | solution.py:410
  78.0 7.3 %collective-permute-start.14 = (bf16[32,2048]{1,0:T(8,128)(2,1)S(1)}, bf16[32,2048]{1,0:T(8,128)(2,1)S(1)}, u32[]{:S(2)}, u32[]{:S(2)}) collective-permute-start(bf16[32,2048]{1,0:T(8,128)(2,1)S(1)} %add_convert_fusion.1), channel_id=1, source_target_pairs={{0,1},{1,0},{2,3},{3,2},{4,5},{5,4},{6,7},{7,6},{8,9},{9,8},{10,11... | collective-permute-start | bytes 393224 | tf_op jit(solution)/shard_map/ppermute | solution.py:410
  80.3 3.1 %collective-permute-start.10 = (f32[2,1536]{1,0:T(2,128)S(1)}, f32[2,1536]{1,0:T(2,128)S(1)}, u32[]{:S(2)}, u32[]{:S(2)}) collective-permute-start(f32[2,1536]{1,0:T(2,128)S(1)} %slice.59), channel_id=1, source_target_pairs={{2,0},{4,2},{6,4},{8,6},{10,8},{12,10},{14,12},{16,14},{18,16},{20... | collective-permute-start | bytes 36872 | tf_op jit(solution)/shard_map/ppermute | solution.py:572
